TPU v7x, 32 devices: a whole 2x2x4 slice. The times are simulated.
32 devices in a mesh: fold: 2 (over y), vox: 16 (over z, x, core).
Axes of the slice: x: 2, y: 2, z: 4, core: 2. Of those that a mesh axis runs over, the one named last changes fastest.
Arguments:
- volumes: float32 [1024, 12288], P('fold', 'vox'), parts along dimension 0, may hold values from -6 to 6
- record_index: int32 [512], P('fold'), parts along dimension 0, may hold values from 0 to 511
- fold_of: int32 [1024], P('fold'), parts along dimension 0, may hold values from 0 to 4
- held_out: int32 [2], P('fold'), parts along dimension 0, may hold values from 0 to 4
- dictionary: float32 [12288, 512], P('vox'), may hold values from -1 to 1
Outputs:
- new_dictionary: float32 [24576, 512], P(('fold', 'vox')), parts along dimension 0
- code_matrix: float32 [512, 512], P('fold'), parts along dimension 0
- dict_gram: float32 [1024, 512], P('fold'), parts along dimension 0
There are 2 independent parts, one for each index of `fold`. A program takes and returns all parts, laid end to end along the dimension named above; an argument that names none is the same for every part. Nothing has to cross between parts.
All inputs are finite; a program needn't handle non-finite values.
Results may differ from a plain program's by a relative error of at most 0.0001.
Values sent between devices are 32-bit elements; how exact they have to be, the bound alone decides.
No kernel may reach another device: no remote copies, remote signals or barrier semaphores. Data moves between devices by JAX's collectives and lax.ppermute only.
A program may use at most 64 MiB of HBM per device.

v0:
```python
import jax
import jax.numpy as jnp
from jax import lax
from jax.sharding import PartitionSpec as P

ISTA_STEPS = 5


penalty = 0.5


def matmul(left, right):
    return jnp.dot(left, right, precision=lax.Precision.HIGHEST, preferred_element_type=jnp.float32)


def inner_cross(left, right):
    return lax.dot_general(
        left,
        right,
        (((0,), (0,)), ((), ())),
        precision=lax.Precision.HIGHEST,
        preferred_element_type=jnp.float32,
    )


def row_bound(matrix):
    return jnp.max(jnp.sum(jnp.abs(matrix), axis=1))


def shrink_codes(correlation, gram_total):
    bound = row_bound(gram_total)
    limit = penalty / bound
    code_rows = jnp.zeros_like(correlation)
    for sweep in range(ISTA_STEPS):
        moved = code_rows - (matmul(code_rows, gram_total) - correlation) / bound
        code_rows = moved - jnp.clip(moved, -limit, limit)
    return code_rows


def shards(volumes, record_index, fold_of, held_out, dictionary):
    batch_rows = volumes[record_index]
    weight = (fold_of[record_index] != held_out[0]).astype(jnp.float32)
    corr_part = matmul(batch_rows, dictionary)
    gram_part = inner_cross(dictionary, dictionary)
    correlation, gram_total = lax.psum((corr_part, gram_part), "vox")
    code_rows = shrink_codes(correlation, gram_total)
    weighted = code_rows * weight[:, None]
    moment = inner_cross(code_rows, weighted)
    target = inner_cross(batch_rows, weighted)
    step_size = 1.0 / (1.0 + row_bound(moment))
    current = dictionary
    stepped = current - step_size * (matmul(current, moment) - target)
    squares = lax.psum(jnp.sum(stepped * stepped, axis=0), "vox")
    current = stepped / jnp.maximum(jnp.sqrt(squares), 1.0)
    stepped = current - step_size * (matmul(current, moment) - target)
    raw_gram = lax.psum(inner_cross(stepped, stepped), "vox")
    divisor = jnp.maximum(jnp.sqrt(jnp.diagonal(raw_gram)), 1.0)
    current = stepped / divisor
    dict_gram = raw_gram / (divisor[:, None] * divisor[None, :])
    return (current, code_rows, dict_gram)


def solution(mesh):
    in_specs = (P("fold", "vox"), P("fold"), P("fold"), P("fold"), P("vox", None))
    out_specs = (P(("fold", "vox"), None), P("fold", None), P("fold", None))
    return jax.shard_map(shards, mesh=mesh, in_specs=in_specs, out_specs=out_specs, check_vma=False)
```

profile of v0, /device:TPU:0, one launch (start us, length us, event | category | flops | bytes accessed | tf_op | source)
XLA Modules:
  0.0 296.7 jit_solution(10499714131739453914)
XLA Ops:
  7.2 0.0 copy-start
  7.2 0.0 all-reduce.6.cloned.1.call-start
  7.2 0.8 compare_select_fusion
  8.0 5.5 %fusion.42 = f32[512,512]{1,0:T(8,128)} fusion(f32[768,512]{1,0:T(8,128)} %param.9), kind=kOutput, calls=%fused_computation.64 | convolution fusion | flops 2415919104 | bytes 2621440 | tf_op jit(solution)/shard_map/dot_general | solution.py:17
  13.5 0.0 copy-done
  13.5 0.0 copy-start.2
  13.5 2.0 gather_fusion
  15.5 0.0 copy-done.2
  15.5 3.4 %fusion.43 = f32[256,512]{1,0:T(8,128)} fusion(f32[256,768]{1,0:T(8,128)} %gather_fusion, f32[768,512]{1,0:T(8,128)S(1)} %copy-done.2), kind=kOutput, calls=%fused_computation.65 | convolution fusion | flops 1207959552 | bytes 2883584 | tf_op jit(solution)/shard_map/dot_general | solution.py:13
  18.9 0.0 all-reduce.6.cloned.1.call-update
  19.0 0.0 copy-start.1
  19.0 0.0 all-reduce.4.cloned.1.call-start
  19.0 1.6 copy.14
  20.6 0.0 copy-done.1
  20.6 2.1 gather_fusion.1
  23.4 94.1 %all-reduce.6.cloned.1.call-done = (f32[256,512]{1,0:T(8,128)}, f32[512,512]{1,0:T(8,128)}) async-done(((f32[256,512]{1,0:T(8,128)}, f32[512,512]{1,0:T(8,128)}), (f32[256,512]{1,0:T(8,128)}, f32[512,512]{1,0:T(8,128)})) %all-reduce.6.cloned.1.call-update) | async-done | bytes 1572880 | tf_op jit(solution)/shard_map/psum | solution.py:45
  117.5 1.4 abs_reduce_fusion.1
  118.9 0.6 reduce_max.18
  119.5 3.8 %fusion.4 = f32[256,512]{1,0:T(8,128)} fusion(f32[256,512]{1,0:T(8,128)} %get-tuple-element.9, f32[512,512]{1,0:T(8,128)} %get-tuple-element.10, f32[]{:T(128)} %reduce_max.18), kind=kOutput, calls=%fused_computation.15 | convolution fusion | flops 805699584 | bytes 2097156 | tf_op jit(solution)/shard_map/dot_general | solution.py:13
  124.0 0.0 copy-start.6
  124.0 0.0 copy-start.7
  124.0 3.6 %fusion.6 = f32[256,512]{1,0:T(8,128)S(1)} fusion(f32[256,512]{1,0:T(8,128)} %get-tuple-element.9, f32[512,512]{1,0:T(8,128)} %get-tuple-element.10, f32[256,512]{1,0:T(8,128)} %fusion.4, f32[]{:T(128)S(6)} %neg.2, f32[]{:T(128)S(6)} %div.49, f32[]{:T(128)} %reduce_max.18), kind=kOutput, calls=%fused_computation.17 | convolution fusion | flops 806486016 | bytes 2621452 | tf_op jit(solution)/shard_map/dot_general | solution.py:13
  127.6 0.0 copy-done.6
  127.6 0.0 copy-done.7
  127.6 1.8 fusion.8
  129.4 1.8 fusion.10
  131.2 0.0 copy-start.4
  131.2 1.9 minimum_subtract_fusion
  133.1 0.0 copy-done.4
  133.1 0.0 copy-start.5
  133.2 2.7 fusion.14
  135.8 2.1 abs_reduce_fusion
  137.9 0.0 copy-done.5
  137.9 0.6 reduce_max.19
  139.2 6.2 %multiply_reduce_fusion = (f32[512]{0:T(512)S(1)}, f32[768,512]{0,1:T(8,128)}) fusion(f32[768,512]{0,1:T(8,128)} %copy.14, f32[768,512]{0,1:T(8,128)} %fusion.14, f32[512,512]{0,1:T(8,128)} %get-tuple-element.12, f32[768,512]{1,0:T(8,128)S(1)} %copy-done.2, f32[]{:T(128)S(6)} %div.54), kind=kOutput, calls=%fused_computation.7 | convolution fusion | flops 2417884672 | bytes 7342084 | tf_op jit(solution)/shard_map/dot_general | solution.py:13
  145.4 30.2 %psum.30 = f32[512]{0:T(512)S(1)} all-reduce(f32[512]{0:T(512)S(1)} %get-tuple-element.13), channel_id=1, replica_groups=mesh['fold'=2,'vox'=16] {'vox'}, use_global_device_ids=true, to_apply=%region_7.8 | all-reduce | flops 512 | bytes 4096 | tf_op jit(solution)/shard_map/psum | solution.py:53
  175.6 5.7 %multiply_subtract_fusion = f32[768,512]{0,1:T(8,128)S(1)} fusion(f32[768,512]{0,1:T(8,128)} %fusion.14, f32[512,512]{0,1:T(8,128)} %get-tuple-element.12, f32[768,512]{0,1:T(8,128)} %get-tuple-element.14, f32[512]{0:T(512)S(1)} %sqrt_maximum_fusion.1, f32[]{:T(128)S(6)} %div.54), kind=kOutput, calls=%fused_computation.6 | convolution fusion | flops 2417885184 | bytes 5769220 | tf_op jit(solution)/shard_map/dot_general | solution.py:13
  181.3 3.7 %fusion.44 = f32[512,512]{1,0:T(8,128)} fusion(f32[768,512]{0,1:T(8,128)S(1)} %multiply_subtract_fusion), kind=kOutput, calls=%fused_computation.66 | convolution fusion | flops 2415919104 | bytes 2621440 | tf_op jit(solution)/shard_map/dot_general | solution.py:17
  185.0 0.0 all-reduce.4.cloned.1.call-update
  185.0 90.5 %all-reduce.4.cloned.1.call-done = f32[512,512]{1,0:T(8,128)} async-done(((f32[512,512]{1,0:T(8,128)}), f32[512,512]{1,0:T(8,128)}) %all-reduce.4.cloned.1.call-update) | async-done | bytes 1048592 | tf_op jit(solution)/shard_map/psum | solution.py:56
  275.5 8.7 %gather_fusion.2 = f32[512]{0:T(512)S(1)} fusion(f32[512,512]{1,0:T(8,128)} %all-reduce.4.cloned.1.call-done, s32[512]{0:T(512)S(1)} %bitcast.25), kind=kCustom, calls=%fused_computation.2 | custom fusion | bytes 8192 | tf_op jit(solution)/shard_map/jit(diagonal)/cond/branch_0_fun/gather | solution.py:57
  284.2 1.3 broadcast_divide_fusion
  285.6 0.0 copy-start.3
  285.6 3.1 %copy.17 = f32[768,512]{1,0:T(8,128)} copy(f32[768,512]{0,1:T(8,128)} %broadcast_divide_fusion) | data formatting | bytes 3145728
  288.7 0.0 copy-done.3
  288.7 1.2 multiply_divide_fusion
  (5 shorter events, 0.0 us)
Async XLA Ops:
  7.2 6.4 %copy-start = (f32[512,768]{1,0:T(8,128)S(1)}, f32[512,768]{1,0:T(8,128)}, u32[]{:S(2)}) copy-start(f32[512,768]{1,0:T(8,128)} %param.5) | copy-start | bytes 4718596
  7.2 110.4 %all-reduce.6.cloned.1.call-start = ((), (), s32[]{:S(2)}) async-start(), calls=%async_computation.1 | async-start | bytes 3145728 | tf_op jit(solution)/shard_map/psum | solution.py:45
  13.5 2.0 copy-start.2
  19.0 1.7 copy-start.1
  19.0 256.5 %all-reduce.4.cloned.1.call-start = ((), (), s32[]{:S(2)}) async-start(), calls=%async_computation | async-start | bytes 2097152 | tf_op jit(solution)/shard_map/psum | solution.py:56
  124.0 3.6 %copy-start.6 = (f32[512,512]{1,0:T(8,128)S(1)}, f32[512,512]{1,0:T(8,128)}, u32[]{:S(2)}) copy-start(f32[512,512]{1,0:T(8,128)} %get-tuple-element.10) | copy-start | bytes 3145732
  124.0 3.6 %copy-start.7 = (f32[256,512]{1,0:T(8,128)S(1)}, f32[256,512]{1,0:T(8,128)}, u32[]{:S(2)}) copy-start(f32[256,512]{1,0:T(8,128)} %get-tuple-element.9) | copy-start | bytes 1572868
  131.2 1.9 copy-start.4
  133.1 4.8 %copy-start.5 = (f32[256,512]{1,0:T(8,128)}, f32[256,512]{1,0:T(8,128)S(1)}, u32[]{:S(2)}) copy-start(f32[256,512]{1,0:T(8,128)S(1)} %minimum_subtract_fusion) | copy-start | bytes 1572868
  285.6 3.1 %copy-start.3 = (f32[512,512]{1,0:T(8,128)S(1)}, f32[512,512]{1,0:T(8,128)}, u32[]{:S(2)}) copy-start(f32[512,512]{1,0:T(8,128)} %all-reduce.4.cloned.1.call-done) | copy-start | bytes 3145732
Sparse Core Ops, SparseCore 0:
  19.1 98.4 all-reduce.5
  185.1 90.3 all-reduce.3
where the time goes:
time: 297 us
  waiting for transfers between devices  185 us (62%)
  matrix products  42.1 us (14%)
  blocking collectives  30.2 us (10%)
  local copies, waits for them, and re-layouts  17.6 us (6%)
  between operations  16.2 us (5%)
  other arithmetic  5.95 us (2%)
    psum x1, waiting for transfers between devices, shards(): correlation, gram_total = lax.psum((corr_part, gram_part), 'vox')  94.1 us
    psum x1, waiting for transfers between devices, shards(): raw_gram = lax.psum(inner_cross(stepped, stepped), 'vox')  90.5 us
    psum x1, blocking collectives, shards(): squares = lax.psum(jnp.sum(stepped * stepped, axis=0), 'vox')  30.2 us
    dot_general x8, matrix products, matmul(): jnp.dot(left, right, precision=lax.Precision.HIGHEST, preferred_element_t...  28.1 us
    dot_general x4, matrix products, inner_cross(): lax.dot_general(left, right, (((0,), (0,)), ((), ())), precision=lax.Prec...  13.9 us
    gather x1, local copies, waits for them, and re-layouts, shards(): divisor = jnp.maximum(jnp.sqrt(jnp.diagonal(raw_gram)), 1.0)  8.74 us
  transfers between devices with their start and end apart: 2, of which 2 were waited for; matrix products, arithmetic and copies ran while one was open for 1% of the time, Pallas kernels for 0%

commit v1 on v0

v1 whole, which is shorter than its diff:
```python
import functools

import jax
import jax.numpy as jnp
from jax import lax
from jax.experimental import pallas as pl
from jax.experimental.pallas import tpu as pltpu
from jax.sharding import PartitionSpec as P

ISTA_STEPS = 5
PENALTY = 0.5
TILE = 128
F32 = jnp.float32
BF16 = jnp.bfloat16

NN = (((1,), (0,)), ((), ()))
TN = (((0,), (0,)), ((), ()))
NT = (((1,), (1,)), ((), ()))


def halves(x):
    hi = x.astype(BF16)
    return hi, (x - hi.astype(F32)).astype(BF16)


def dot1(a, b, dims=NN):
    return lax.dot_general(a, b, dims, preferred_element_type=F32)


def dot3(a, b, dims=NN):
    return dot1(a[0], b[0], dims) + (dot1(a[0], b[1], dims) + dot1(a[1], b[0], dims))


def top_row_sum(x):
    return jnp.max(jnp.sum(jnp.abs(x), axis=1, keepdims=True), axis=0, keepdims=True)


def upper_tiles(batch, atoms):
    edge = (batch + atoms) // TILE
    return [(r, c) for r in range(edge) for c in range(r, edge)]


def slot_of(vox, bits):
    place = 0
    for k in range(bits):
        place = place + ((vox >> k) & 1) * (1 << (bits - 1 - k))
    return place


def gram_kernel(tiles, bits, index_ref, fold_ref, held_ref, volumes_ref, dict_ref,
                keep_ref, send_ref, bhi_ref, blo_ref, weight_ref, full):
    batch = index_ref.shape[1]
    records = volumes_ref.shape[0]
    atoms = dict_ref.shape[1]
    d = halves(dict_ref[...])
    for r in range(0, atoms, 256):
        left = (d[0][:, r:r + 256], d[1][:, r:r + 256])
        right = (d[0][:, r:], d[1][:, r:])
        full[batch + r:batch + r + 256, batch + r:] = dot3(left, right, TN)
    pick = lax.broadcasted_iota(jnp.int32, (records, batch), 0) == index_ref[...]
    pick = pick.astype(F32).astype(BF16)
    v = halves(volumes_ref[...])
    b = (dot1(pick, v[0], TN).astype(BF16), dot1(pick, v[1], TN).astype(BF16))
    bhi_ref[...] = b[0]
    blo_ref[...] = b[1]
    full[:batch, batch:] = dot3(b, d)
    full[:batch, :batch] = dot3(b, b, NT)
    fold = jnp.broadcast_to(fold_ref[...], (TILE, records)).astype(F32).astype(BF16)
    folds = dot1(pick, fold, (((0,), (1,)), ((), ())))
    weight_ref[...] = jnp.where(folds != held_ref[0].astype(F32), 1.0, 0.0)
    slots = 1 << bits
    rows = TILE // slots
    mine = slot_of(lax.axis_index("vox"), bits)
    half = slots // 2
    for o in range(slots):
        out = keep_ref if o < half else send_ref
        start = (mine ^ o) * rows
        for k, (r, c) in enumerate(tiles):
            at = pl.multiple_of(r * TILE + start, rows)
            out[o % half, k * rows:(k + 1) * rows, :] = full[pl.ds(at, rows), c * TILE:(c + 1) * TILE]


def step_kernel(tiles, bits, mine_ref, other_ref, bhi_ref, blo_ref, weight_ref, dict_ref,
                new_ref, code_ref, gram_ref, full):
    batch = bhi_ref.shape[0]
    atoms = dict_ref.shape[1]
    slots = 1 << bits
    rows = TILE // slots
    half = slots // 2
    place = slot_of(lax.axis_index("vox"), bits)
    for o in range(slots):
        source = mine_ref if o < half else other_ref
        start = (place ^ o) * rows
        for k, (r, c) in enumerate(tiles):
            at = pl.multiple_of(r * TILE + start, rows)
            full[pl.ds(at, rows), c * TILE:(c + 1) * TILE] = source[o % half, k * rows:(k + 1) * rows, :]
    for r, c in tiles:
        if r != c and (r * TILE >= batch or c * TILE < batch):
            full[c * TILE:(c + 1) * TILE, r * TILE:(r + 1) * TILE] = full[r * TILE:(r + 1) * TILE, c * TILE:(c + 1) * TILE].T
    gram = full[batch:, batch:]
    bound = top_row_sum(gram)
    inverse = 1.0 / bound
    limit = PENALTY * inverse
    g = halves(gram)
    corr = full[:batch, batch:]
    moved = corr * inverse
    code = moved - jnp.clip(moved, -limit, limit)
    for _ in range(ISTA_STEPS - 1):
        moved = code - (dot3(halves(code), g) - corr) * inverse
        code = moved - jnp.clip(moved, -limit, limit)
    code_ref[...] = code
    weight = jnp.concatenate([weight_ref[...]] * (atoms // TILE), axis=1)
    weighted = code * weight
    w = halves(weighted)
    moment = dot3(w, w, TN)
    step = 1.0 / (1.0 + top_row_sum(moment))
    diagonal = lax.broadcasted_iota(jnp.int32, (atoms, atoms), 0) == lax.broadcasted_iota(jnp.int32, (atoms, atoms), 1)
    eye = jnp.where(diagonal, 1.0, 0.0)
    pull = eye - step * moment
    p = halves(pull)
    c = halves(corr)
    k = halves(full[:batch, :batch])
    kw = step * dot3(k, w)
    cw = step * dot3(c, w, TN)
    upper = dot3(c, p) + kw
    lower = dot3(g, p) + cw
    squares = jnp.sum(pull * lower, axis=0, keepdims=True) + step * jnp.sum(weighted * upper, axis=0, keepdims=True)
    scale = 1.0 / jnp.sqrt(jnp.maximum(squares, 1.0))
    top = halves(step * (dot3(halves(weighted * scale), p) + weighted))
    bottom = halves(dot3(halves(pull * scale), p))
    upper = dot3(halves(upper * scale), p) + kw
    lower = dot3(halves(lower * scale), p) + cw
    raw = dot3(top, halves(upper), TN) + dot3(bottom, halves(lower), TN)
    lengths = jnp.sum(raw * eye, axis=0, keepdims=True)
    lengths_down = jnp.sum(raw * eye, axis=1, keepdims=True)
    scale = 1.0 / jnp.sqrt(jnp.maximum(lengths, 1.0))
    scale_down = 1.0 / jnp.sqrt(jnp.maximum(lengths_down, 1.0))
    gram_ref[...] = raw * scale * scale_down
    b = (bhi_ref[...], blo_ref[...])
    d = halves(dict_ref[...])
    new_ref[...] = (dot3(b, top, TN) + dot3(d, bottom)) * scale


def all_reduce(keep, send, devices, bits):
    def swap(x, bit):
        return lax.ppermute(x, "vox", [(i, i ^ bit) for i in range(devices)])

    total = keep + swap(send, 1)
    mid = bits - 1
    flips = []
    for o in range(1 << mid):
        flips.append(sum(1 << (bits - 1 - j) for j in range(mid) if (o >> j) & 1))
    parts = [total[o] for o in range(1 << mid)]
    got = [swap(parts[o], flips[o]) for o in range(1, 1 << mid)]
    own = parts[0]
    for part in got:
        own = own + part
    for bit in range(bits, devices.bit_length() - 1):
        own = own + swap(own, 1 << bit)
    mine = jnp.stack([own] + [swap(own, flips[o]) for o in range(1, 1 << mid)])
    return mine, swap(mine, 1)


def shards(devices, volumes, record_index, fold_of, held_out, dictionary):
    records, voxels = volumes.shape
    batch = record_index.shape[0]
    atoms = dictionary.shape[1]
    tiles = upper_tiles(batch, atoms)
    bits = 3
    slots = 1 << bits
    part = jax.ShapeDtypeStruct((slots // 2, len(tiles) * TILE // slots, TILE), F32)
    vmem = pl.BlockSpec(memory_space=pltpu.VMEM)
    smem = pl.BlockSpec(memory_space=pltpu.SMEM)
    full = pltpu.VMEM((batch + atoms, batch + atoms), F32)
    params = pltpu.CompilerParams(vmem_limit_bytes=48 << 20)
    keep, send, bhi, blo, weight = pl.pallas_call(
        functools.partial(gram_kernel, tiles, bits),
        out_shape=(part, part, jax.ShapeDtypeStruct((batch, voxels), BF16),
                   jax.ShapeDtypeStruct((batch, voxels), BF16), jax.ShapeDtypeStruct((batch, TILE), F32)),
        in_specs=[vmem, vmem, smem, vmem, vmem],
        out_specs=(vmem,) * 5,
        scratch_shapes=[full],
        compiler_params=params,
        name="grams",
    )(record_index[None], fold_of[None], held_out, volumes, dictionary)
    mine, other = all_reduce(keep, send, devices, bits)
    return pl.pallas_call(
        functools.partial(step_kernel, tiles, bits),
        out_shape=(jax.ShapeDtypeStruct(dictionary.shape, F32), jax.ShapeDtypeStruct((batch, atoms), F32),
                   jax.ShapeDtypeStruct((atoms, atoms), F32)),
        in_specs=[vmem] * 6,
        out_specs=(vmem,) * 3,
        scratch_shapes=[full],
        compiler_params=params,
        name="step",
    )(mine, other, bhi, blo, weight, dictionary)


def solution(mesh):
    devices = mesh.shape["vox"]
    in_specs = (P("fold", "vox"), P("fold"), P("fold"), P("fold"), P("vox", None))
    out_specs = (P(("fold", "vox"), None), P("fold", None), P("fold", None))
    return jax.shard_map(functools.partial(shards, devices), mesh=mesh, in_specs=in_specs, out_specs=out_specs, check_vma=False)
```

time: 297 us -> 59.6 us (0.20)
  waiting for transfers between devices: 185 us -> 26.9 us
  matrix products: 42.1 us -> 0 us
  blocking collectives: 30.2 us -> 0 us
  Pallas kernels: 0 us -> 15.3 us
  between operations: 16.2 us -> 1.34 us
  local copies, waits for them, and re-layouts: 17.6 us -> 4.21 us
  starting transfers between devices: 0.08 us -> 11.3 us
  other arithmetic: 5.95 us -> 0.24 us
    psum x2 -> x0, waiting for transfers between devices: 185 us -> none  [the longest x1 94.1 us: shards(): correlation, gram_total = lax.psum((corr_part, gram_part), 'vox')]
    dot_general x12 -> x0, matrix products: 42.1 us -> none  [the longest x8 28.1 us: matmul(): jnp.dot(left, right, precision=lax.Precision.HIGHEST, preferred_element_t...]
    psum x1 -> x0, blocking collectives: 30.2 us -> none  [shards(): squares = lax.psum(jnp.sum(stepped * stepped, axis=0), 'vox')]
    ppermute x0 -> x9, waiting for transfers between devices: none -> 26.9 us  [swap(): return lax.ppermute(x, 'vox', [(i, i ^ bit) for i in range(devices)])]
    pallas_call x0 -> x2, Pallas kernels: none -> 15.3 us  [the longest x1 12.3 us: shards(): pl.pallas_call(functools.partial(step_kernel, tiles, bits), out_shape=(ja...]
    gather x3 -> x0, local copies, waits for them, and re-layouts: 12.8 us -> none  [the longest x1 8.74 us: shards(): divisor = jnp.maximum(jnp.sqrt(jnp.diagonal(raw_gram)), 1.0)]
    ppermute x0 -> x9, starting transfers between devices: none -> 11.3 us  [swap(): return lax.ppermute(x, 'vox', [(i, i ^ bit) for i in range(devices)])]
  transfers between devices with their start and end apart: 2 -> 9, of which waited for: 2 -> 9; matrix products, arithmetic and copies ran while one was open for 1% -> 0% of each run, Pallas kernels for 0% -> 0%
where the time goes in v1:
time: 59.6 us; the launch traced here: 59.4 us
  waiting for transfers between devices  26.9 us (45%)
  Pallas kernels  15.3 us (26%)
  starting transfers between devices  11.3 us (19%)
  local copies, waits for them, and re-layouts  4.21 us (7%)
  between operations  1.34 us (2%)
    ppermute x9, waiting for transfers between devices, swap(): return lax.ppermute(x, 'vox', [(i, i ^ bit) for i in range(devices)])  26.9 us
    pallas_call x1, Pallas kernels, shards(): pl.pallas_call(functools.partial(step_kernel, tiles, bits), out_shape=(ja...  12.3 us
    ppermute x9, starting transfers between devices, swap(): return lax.ppermute(x, 'vox', [(i, i ^ bit) for i in range(devices)])  11.3 us
    unnamed x10, local copies, waits for them, and re-layouts  4.18 us
    pallas_call x1, Pallas kernels, shards(): pl.pallas_call(functools.partial(gram_kernel, tiles, bits), out_shape=(pa...  3.03 us
  transfers between devices with their start and end apart: 9, of which 9 were waited for; matrix products, arithmetic and copies ran while one was open for 0% of the time, Pallas kernels for 0%

profile of v1, /device:TPU:0, one launch (start us, length us, event | category | flops | bytes accessed | tf_op | source)
XLA Modules:
  0.0 59.4 jit_solution(1543499285068580328)
XLA Ops:
  1.3 0.0 copy-start
  1.3 1.4 %copy-done = f32[768,512]{1,0:T(8,128)S(1)} copy-done((f32[768,512]{1,0:T(8,128)S(1)}, f32[768,512]{1,0:T(8,128)}, u32[]{:S(2)}) %copy-start) | copy-done | bytes 1572888
  2.7 0.0 copy-start.2
  2.7 1.4 %copy-done.2 = f32[512,768]{1,0:T(8,128)S(1)} copy-done((f32[512,768]{1,0:T(8,128)S(1)}, f32[512,768]{1,0:T(8,128)}, u32[]{:S(2)}) %copy-start.2) | copy-done | bytes 1572888
  4.1 0.0 copy-start.3
  4.1 0.7 %copy-done.3 = s32[512]{0:T(512)S(1)} copy-done((s32[512]{0:T(512)S(1)}, s32[512]{0:T(512)}, u32[]{:S(2)}) %copy-start.3) | copy-done | bytes 2072
  4.8 0.0 copy-start.4
  4.8 0.7 %copy-done.4 = s32[256]{0:T(256)S(1)} copy-done((s32[256]{0:T(256)S(1)}, s32[256]{0:T(256)}, u32[]{:S(2)}) %copy-start.4) | copy-done | bytes 1048
  5.5 3.0 %grams.1 = (f32[4,336,128]{2,1,0:T(8,128)S(1)}, f32[4,336,128]{2,1,0:T(8,128)S(1)}, bf16[256,768]{1,0:T(8,128)(2,1)S(1)}, bf16[256,768]{1,0:T(8,128)(2,1)S(1)}, f32[256,128]{1,0:T(8,128)S(1)}) custom-call(s32[1,256]{1,0:T(1,128)S(1)} %bitcast.21, s32[1,512]{1,0:T(1,128)S(1)} %bitcast.20, s32[1]{0:T(128)S(6)} %copy.8.held_ref, f32[512,768]{1,0:T(8,128)S(1)} %copy-done.2, ...), custom_call_target="tpu_custom_call" | custom-call | tf_op jit(solution)/shard_map/grams/pallas_call | solution.py:176
  8.5 0.5 collective-permute-start
  9.0 1.8 %collective-permute-done = f32[4,336,128]{2,1,0:T(8,128)S(1)} collective-permute-done((f32[4,336,128]{2,1,0:T(8,128)S(1)}, f32[4,336,128]{2,1,0:T(8,128)S(1)}, u32[]{:S(2)}, u32[]{:S(2)}) %collective-permute-start) | collective-permute-done | bytes 688160 | tf_op jit(solution)/shard_map/ppermute | solution.py:146
  10.8 0.1 add.15
  10.9 0.0 copy-start.1
  11.0 3.0 %collective-permute-start.1 = (f32[336,128]{1,0:T(8,128)S(1)}, f32[336,128]{1,0:T(8,128)S(1)}, u32[]{:S(2)}, u32[]{:S(2)}) collective-permute-start(f32[336,128]{1,0:T(8,128)S(1)} %get-tuple-element.13), channel_id=1, source_target_pairs={{0,4},{1,5},{2,6},{3,7},{4,0},{5,1},{6,2},{7,3},{8,12},{9,13},{10,... | collective-permute-start | bytes 516104 | tf_op jit(solution)/shard_map/ppermute | solution.py:146
  14.0 1.4 %collective-permute-start.3 = (f32[336,128]{1,0:T(8,128)S(1)}, f32[336,128]{1,0:T(8,128)S(1)}, u32[]{:S(2)}, u32[]{:S(2)}) collective-permute-start(f32[336,128]{1,0:T(8,128)S(1)} %get-tuple-element.14), channel_id=1, source_target_pairs={{0,6},{1,7},{2,4},{3,5},{4,2},{5,3},{6,0},{7,1},{8,14},{9,15},{10,... | collective-permute-start | bytes 516104 | tf_op jit(solution)/shard_map/ppermute | solution.py:146
  15.3 0.2 collective-permute-start.2
  15.5 3.6 %collective-permute-done.1 = f32[336,128]{1,0:T(8,128)S(1)} collective-permute-done((f32[336,128]{1,0:T(8,128)S(1)}, f32[336,128]{1,0:T(8,128)S(1)}, u32[]{:S(2)}, u32[]{:S(2)}) %collective-permute-start.1) | collective-permute-done | bytes 172064 | tf_op jit(solution)/shard_map/ppermute | solution.py:146
  19.1 4.4 %collective-permute-done.3 = f32[336,128]{1,0:T(8,128)S(1)} collective-permute-done((f32[336,128]{1,0:T(8,128)S(1)}, f32[336,128]{1,0:T(8,128)S(1)}, u32[]{:S(2)}, u32[]{:S(2)}) %collective-permute-start.3) | collective-permute-done | bytes 172064 | tf_op jit(solution)/shard_map/ppermute | solution.py:146
  23.5 1.4 %collective-permute-done.2 = f32[336,128]{1,0:T(8,128)S(1)} collective-permute-done((f32[336,128]{1,0:T(8,128)S(1)}, f32[336,128]{1,0:T(8,128)S(1)}, u32[]{:S(2)}, u32[]{:S(2)}) %collective-permute-start.2) | collective-permute-done | bytes 172064 | tf_op jit(solution)/shard_map/ppermute | solution.py:146
  24.9 0.1 fusion.2
  24.9 2.7 %collective-permute-start.4 = (f32[336,128]{1,0:T(8,128)S(1)}, f32[336,128]{1,0:T(8,128)S(1)}, u32[]{:S(2)}, u32[]{:S(2)}) collective-permute-start(f32[336,128]{1,0:T(8,128)S(1)} %fusion.2), channel_id=1, source_target_pairs={{0,8},{1,9},{2,10},{3,11},{4,12},{5,13},{6,14},{7,15},{8,0},{9,1},... | collective-permute-start | bytes 516104 | tf_op jit(solution)/shard_map/ppermute | solution.py:146
  27.6 6.2 %collective-permute-done.4 = f32[336,128]{1,0:T(8,128)S(1)} collective-permute-done((f32[336,128]{1,0:T(8,128)S(1)}, f32[336,128]{1,0:T(8,128)S(1)}, u32[]{:S(2)}, u32[]{:S(2)}) %collective-permute-start.4) | collective-permute-done | bytes 172064 | tf_op jit(solution)/shard_map/ppermute | solution.py:146
  33.8 0.7 %collective-permute-start.7 = (f32[336,128]{1,0:T(8,128)S(1)}, f32[336,128]{1,0:T(8,128)S(1)}, u32[]{:S(2)}, u32[]{:S(2)}) collective-permute-start(f32[336,128]{1,0:T(8,128)S(1)} %add.19), channel_id=1, source_target_pairs={{0,6},{1,7},{2,4},{3,5},{4,2},{5,3},{6,0},{7,1},{8,14},{9,15},{10,... | collective-permute-start | bytes 516104 | tf_op jit(solution)/shard_map/ppermute | solution.py:146
  34.5 1.5 %collective-permute-start.6 = (f32[336,128]{1,0:T(8,128)S(1)}, f32[336,128]{1,0:T(8,128)S(1)}, u32[]{:S(2)}, u32[]{:S(2)}) collective-permute-start(f32[336,128]{1,0:T(8,128)S(1)} %add.19), channel_id=1, source_target_pairs={{0,2},{1,3},{2,0},{3,1},{4,6},{5,7},{6,4},{7,5},{8,10},{9,11},{10,... | collective-permute-start | bytes 516104 | tf_op jit(solution)/shard_map/ppermute | solution.py:146
  36.0 1.4 %collective-permute-start.5 = (f32[336,128]{1,0:T(8,128)S(1)}, f32[336,128]{1,0:T(8,128)S(1)}, u32[]{:S(2)}, u32[]{:S(2)}) collective-permute-start(f32[336,128]{1,0:T(8,128)S(1)} %add.19), channel_id=1, source_target_pairs={{0,4},{1,5},{2,6},{3,7},{4,0},{5,1},{6,2},{7,3},{8,12},{9,13},{10,... | collective-permute-start | bytes 516104 | tf_op jit(solution)/shard_map/ppermute | solution.py:146
  37.3 4.4 %collective-permute-done.7 = f32[336,128]{1,0:T(8,128)S(1)} collective-permute-done((f32[336,128]{1,0:T(8,128)S(1)}, f32[336,128]{1,0:T(8,128)S(1)}, u32[]{:S(2)}, u32[]{:S(2)}) %collective-permute-start.7) | collective-permute-done | bytes 172064 | tf_op jit(solution)/shard_map/ppermute | solution.py:146
  41.7 1.8 %collective-permute-done.6 = f32[336,128]{1,0:T(8,128)S(1)} collective-permute-done((f32[336,128]{1,0:T(8,128)S(1)}, f32[336,128]{1,0:T(8,128)S(1)}, u32[]{:S(2)}, u32[]{:S(2)}) %collective-permute-start.6) | collective-permute-done | bytes 172064 | tf_op jit(solution)/shard_map/ppermute | solution.py:146
  43.5 1.3 %collective-permute-done.5 = f32[336,128]{1,0:T(8,128)S(1)} collective-permute-done((f32[336,128]{1,0:T(8,128)S(1)}, f32[336,128]{1,0:T(8,128)S(1)}, u32[]{:S(2)}, u32[]{:S(2)}) %collective-permute-start.5) | collective-permute-done | bytes 172064 | tf_op jit(solution)/shard_map/ppermute | solution.py:146
  44.9 0.1 collective-permute-start.8
  44.9 2.1 %collective-permute-done.8.other_ref = f32[4,336,128]{2,1,0:T(8,128)S(1)} collective-permute-done((f32[4,336,128]{2,1,0:T(8,128)S(1)}, f32[4,336,128]{2,1,0:T(8,128)S(1)}, u32[]{:S(2)}, u32[]{:S(2)}) %collective-permute-start.8) | collective-permute-done | bytes 688160 | tf_op jit(solution)/shard_map/ppermute | solution.py:146
  47.1 0.0 copy-done.1
  47.1 12.3 %step.1 = (f32[768,512]{1,0:T(8,128)}, f32[256,512]{1,0:T(8,128)}, f32[512,512]{1,0:T(8,128)}) custom-call(f32[4,336,128]{2,1,0:T(8,128)S(1)} %pad_maximum_fusion.mine_ref, f32[4,336,128]{2,1,0:T(8,128)S(1)} %collective-permute-done.8.other_ref, bf16[256,768]{1,0:T(8,128)(2,1)S(1)} %get-tuple-element.10.bhi_ref, ...), custom_call_target="tpu_custom_call" | custom-call | tf_op jit(solution)/shard_map/step/pallas_call | solution.py:187
  (3 shorter events, 0.1 us)
Async XLA Ops:
  1.3 1.4 %copy-start = (f32[768,512]{1,0:T(8,128)S(1)}, f32[768,512]{1,0:T(8,128)}, u32[]{:S(2)}) copy-start(f32[768,512]{1,0:T(8,128)} %dict_ref.3) | copy-start | bytes 4718596
  2.7 1.4 %copy-start.2 = (f32[512,768]{1,0:T(8,128)S(1)}, f32[512,768]{1,0:T(8,128)}, u32[]{:S(2)}) copy-start(f32[512,768]{1,0:T(8,128)} %volumes_ref.1) | copy-start | bytes 4718596
  4.1 0.7 %copy-start.3 = (s32[512]{0:T(512)S(1)}, s32[512]{0:T(512)}, u32[]{:S(2)}) copy-start(s32[512]{0:T(512)} %param.7) | copy-start | bytes 6148
  4.8 0.7 %copy-start.4 = (s32[256]{0:T(256)S(1)}, s32[256]{0:T(256)}, u32[]{:S(2)}) copy-start(s32[256]{0:T(256)} %param.6) | copy-start | bytes 3076
  8.5 2.3 %collective-permute-start = (f32[4,336,128]{2,1,0:T(8,128)S(1)}, f32[4,336,128]{2,1,0:T(8,128)S(1)}, u32[]{:S(2)}, u32[]{:S(2)}) collective-permute-start(f32[4,336,128]{2,1,0:T(8,128)S(1)} %get-tuple-element.9), channel_id=1, source_target_pairs={{0,1},{1,0},{2,3},{3,2},{4,5},{5,4},{6,7},{7,6},{8,9},{9,8},{10,11... | collective-permute-start | bytes 2064392 | tf_op jit(solution)/shard_map/ppermute | solution.py:146
  10.9 36.1 %copy-start.1 = (f32[768,512]{1,0:T(8,128)S(1)}, f32[768,512]{1,0:T(8,128)}, u32[]{:S(2)}) copy-start(f32[768,512]{1,0:T(8,128)} %dict_ref.3) | copy-start | bytes 4718596
  11.0 8.2 %collective-permute-start.1 = (f32[336,128]{1,0:T(8,128)S(1)}, f32[336,128]{1,0:T(8,128)S(1)}, u32[]{:S(2)}, u32[]{:S(2)}) collective-permute-start(f32[336,128]{1,0:T(8,128)S(1)} %get-tuple-element.13), channel_id=1, source_target_pairs={{0,4},{1,5},{2,6},{3,7},{4,0},{5,1},{6,2},{7,3},{8,12},{9,13},{10,... | collective-permute-start | bytes 516104 | tf_op jit(solution)/shard_map/ppermute | solution.py:146
  14.0 9.6 %collective-permute-start.3 = (f32[336,128]{1,0:T(8,128)S(1)}, f32[336,128]{1,0:T(8,128)S(1)}, u32[]{:S(2)}, u32[]{:S(2)}) collective-permute-start(f32[336,128]{1,0:T(8,128)S(1)} %get-tuple-element.14), channel_id=1, source_target_pairs={{0,6},{1,7},{2,4},{3,5},{4,2},{5,3},{6,0},{7,1},{8,14},{9,15},{10,... | collective-permute-start | bytes 516104 | tf_op jit(solution)/shard_map/ppermute | solution.py:146
  15.3 9.5 %collective-permute-start.2 = (f32[336,128]{1,0:T(8,128)S(1)}, f32[336,128]{1,0:T(8,128)S(1)}, u32[]{:S(2)}, u32[]{:S(2)}) collective-permute-start(f32[336,128]{1,0:T(8,128)S(1)} %get-tuple-element.15), channel_id=1, source_target_pairs={{0,2},{1,3},{2,0},{3,1},{4,6},{5,7},{6,4},{7,5},{8,10},{9,11},{10,... | collective-permute-start | bytes 516104 | tf_op jit(solution)/shard_map/ppermute | solution.py:146
  24.9 8.8 %collective-permute-start.4 = (f32[336,128]{1,0:T(8,128)S(1)}, f32[336,128]{1,0:T(8,128)S(1)}, u32[]{:S(2)}, u32[]{:S(2)}) collective-permute-start(f32[336,128]{1,0:T(8,128)S(1)} %fusion.2), channel_id=1, source_target_pairs={{0,8},{1,9},{2,10},{3,11},{4,12},{5,13},{6,14},{7,15},{8,0},{9,1},... | collective-permute-start | bytes 516104 | tf_op jit(solution)/shard_map/ppermute | solution.py:146
  33.8 7.9 %collective-permute-start.7 = (f32[336,128]{1,0:T(8,128)S(1)}, f32[336,128]{1,0:T(8,128)S(1)}, u32[]{:S(2)}, u32[]{:S(2)}) collective-permute-start(f32[336,128]{1,0:T(8,128)S(1)} %add.19), channel_id=1, source_target_pairs={{0,6},{1,7},{2,4},{3,5},{4,2},{5,3},{6,0},{7,1},{8,14},{9,15},{10,... | collective-permute-start | bytes 516104 | tf_op jit(solution)/shard_map/ppermute | solution.py:146
  34.5 9.0 %collective-permute-start.6 = (f32[336,128]{1,0:T(8,128)S(1)}, f32[336,128]{1,0:T(8,128)S(1)}, u32[]{:S(2)}, u32[]{:S(2)}) collective-permute-start(f32[336,128]{1,0:T(8,128)S(1)} %add.19), channel_id=1, source_target_pairs={{0,2},{1,3},{2,0},{3,1},{4,6},{5,7},{6,4},{7,5},{8,10},{9,11},{10,... | collective-permute-start | bytes 516104 | tf_op jit(solution)/shard_map/ppermute | solution.py:146
  36.0 8.8 %collective-permute-start.5 = (f32[336,128]{1,0:T(8,128)S(1)}, f32[336,128]{1,0:T(8,128)S(1)}, u32[]{:S(2)}, u32[]{:S(2)}) collective-permute-start(f32[336,128]{1,0:T(8,128)S(1)} %add.19), channel_id=1, source_target_pairs={{0,4},{1,5},{2,6},{3,7},{4,0},{5,1},{6,2},{7,3},{8,12},{9,13},{10,... | collective-permute-start | bytes 516104 | tf_op jit(solution)/shard_map/ppermute | solution.py:146
  44.9 2.2 %collective-permute-start.8 = (f32[4,336,128]{2,1,0:T(8,128)S(1)}, f32[4,336,128]{2,1,0:T(8,128)S(1)}, u32[]{:S(2)}, u32[]{:S(2)}) collective-permute-start(f32[4,336,128]{2,1,0:T(8,128)S(1)} %pad_maximum_fusion.mine_ref), channel_id=1, source_target_pairs={{0,1},{1,0},{2,3},{3,2},{4,5},{5,4},{6,7},{7,6},{8,9},{9,8},{10,11... | collective-permute-start | bytes 2064392 | tf_op jit(solution)/shard_map/ppermute | solution.py:146

commit v2 on v1

v2 whole, which is shorter than its diff:
```python
import functools

import jax
import jax.numpy as jnp
from jax import lax
from jax.experimental import pallas as pl
from jax.experimental.pallas import tpu as pltpu
from jax.sharding import PartitionSpec as P

ISTA_STEPS = 5
PENALTY = 0.5
TILE = 128
F32 = jnp.float32
BF16 = jnp.bfloat16

NN = (((1,), (0,)), ((), ()))
TN = (((0,), (0,)), ((), ()))
NT = (((1,), (1,)), ((), ()))


def halves(x):
    hi = x.astype(BF16)
    return hi, (x - hi.astype(F32)).astype(BF16)


def dot1(a, b, dims=NN):
    return lax.dot_general(a, b, dims, preferred_element_type=F32)


def dot3(a, b, dims=NN):
    return dot1(a[0], b[0], dims) + (dot1(a[0], b[1], dims) + dot1(a[1], b[0], dims))


def top_row_sum(x):
    return jnp.max(jnp.sum(jnp.abs(x), axis=1, keepdims=True), axis=0, keepdims=True)


def upper_tiles(batch, atoms):
    edge = (batch + atoms) // TILE
    return [(r, c) for r in range(edge) for c in range(r, edge)]


def slot_of(vox, bits):
    place = 0
    for k in range(bits):
        bit = (vox >> k) & 1
        if k == bits - 1:
            bit = bit ^ ((vox >> bits) & 1)
        place = place + bit * (1 << (bits - 1 - k))
    return place


def column(row):
    return jnp.broadcast_to(row, (TILE, row.shape[1])).T[:, :1]


def gram_kernel(tiles, bits, index_hbm, fold_hbm, held_ref, volumes_hbm, dict_hbm,
                keep_ref, send_ref, flipped_ref, weight_ref, index_ref, fold_ref, volumes_ref, dict_ref, full, sems):
    pairs = ((dict_hbm, dict_ref), (index_hbm, index_ref), (fold_hbm, fold_ref), (volumes_hbm, volumes_ref))
    copies = [pltpu.make_async_copy(source, target, sems.at[j]) for j, (source, target) in enumerate(pairs)]
    for copy in copies:
        copy.start()
    batch = index_ref.shape[1]
    records = volumes_ref.shape[0]
    atoms = dict_ref.shape[1]
    copies[0].wait()
    d = halves(dict_ref[...])
    for r in range(0, atoms, 256):
        left = (d[0][:, r:r + 256], d[1][:, r:r + 256])
        right = (d[0][:, r:], d[1][:, r:])
        full[batch + r:batch + r + 256, batch + r:] = dot3(left, right, TN)
    for copy in copies[1:]:
        copy.wait()
    pick = lax.broadcasted_iota(jnp.int32, (records, batch), 0) == index_ref[...]
    pick = pick.astype(F32).astype(BF16)
    v = halves(volumes_ref[...])
    b = (dot1(pick, v[0], TN), dot1(pick, v[1], TN))
    flipped_ref[...] = (b[0] + b[1]).T
    b = (b[0].astype(BF16), b[1].astype(BF16))
    full[:batch, batch:] = dot3(b, d)
    full[:batch, :batch] = dot3(b, b, NT)
    fold = jnp.broadcast_to(fold_ref[...], (TILE, records)).astype(F32).astype(BF16)
    folds = dot1(pick, fold, (((0,), (1,)), ((), ())))
    weight_ref[...] = jnp.where(folds != held_ref[0].astype(F32), 1.0, 0.0)
    slots = 1 << bits
    rows = TILE // slots
    mine = slot_of(lax.axis_index("vox"), bits)
    half = slots // 2
    for o in range(slots):
        out = keep_ref if o < half else send_ref
        start = (mine ^ o) * rows
        for k, (r, c) in enumerate(tiles):
            at = pl.multiple_of(r * TILE + start, rows)
            out[o % half, k * rows:(k + 1) * rows, :] = full[pl.ds(at, rows), c * TILE:(c + 1) * TILE]


def step_kernel(tiles, bits, mine_ref, other_ref, flipped_ref, weight_ref, dict_ref,
                new_hbm, code_hbm, gram_hbm, full, new_ref, code_ref, gram_ref, sems):
    batch = flipped_ref.shape[1]
    voxels, atoms = dict_ref.shape
    slots = 1 << bits
    rows = TILE // slots
    half = slots // 2
    place = slot_of(lax.axis_index("vox"), bits)
    for o in range(slots):
        source = mine_ref if o < half else other_ref
        start = (place ^ o) * rows
        for k, (r, c) in enumerate(tiles):
            at = pl.multiple_of(r * TILE + start, rows)
            full[pl.ds(at, rows), c * TILE:(c + 1) * TILE] = source[o % half, k * rows:(k + 1) * rows, :]
    for r, c in tiles:
        if r != c and (r * TILE >= batch or c * TILE < batch):
            full[c * TILE:(c + 1) * TILE, r * TILE:(r + 1) * TILE] = full[r * TILE:(r + 1) * TILE, c * TILE:(c + 1) * TILE].T

    gram = full[batch:, batch:]
    bound = top_row_sum(gram)
    inverse = 1.0 / bound
    limit = PENALTY * inverse
    g = halves(gram)
    corr = full[:batch, batch:]
    moved = corr * inverse
    code = moved - jnp.clip(moved, -limit, limit)
    groups = [slice(0, batch // 2), slice(batch // 2, batch)]
    codes = [code[group] for group in groups]
    for _ in range(ISTA_STEPS - 1):
        for j, group in enumerate(groups):
            moved = codes[j] - (dot3(halves(codes[j]), g) - corr[group]) * inverse
            codes[j] = moved - jnp.clip(moved, -limit, limit)
    code = jnp.concatenate(codes, axis=0)
    code_ref[...] = code
    code_copy = pltpu.make_async_copy(code_ref, code_hbm, sems.at[0])
    code_copy.start()

    x = halves(code)
    weighted = code * jnp.concatenate([weight_ref[...]] * (atoms // TILE), axis=1)
    w = halves(weighted)
    step = 1.0 / (1.0 + top_row_sum(dot3(w, w, TN)))

    block = voxels // 3 if voxels % 3 == 0 and (voxels // 3) % 16 == 0 else voxels
    rows_of = [slice(at, at + block) for at in range(0, voxels, block)]

    def pulled(now, here):
        return dot3(halves(flipped_ref[here, :] - dot3(halves(now), x, NT)), w)

    for here in rows_of:
        new_ref[here, :] = pulled(dict_ref[here, :], here)

    def half_change(gram_now, corr_now):
        fit = corr_now - dot3(x, halves(gram_now))
        cross = full[:batch, :batch] - dot3(halves(corr_now), x, NT)
        square = cross - dot3(x, halves(fit), NT)
        return cross, fit + (0.5 * step) * dot3(halves(square), w)

    tile_eye = lax.broadcasted_iota(jnp.int32, (TILE, TILE), 0) == lax.broadcasted_iota(jnp.int32, (TILE, TILE), 1)
    squares = jnp.concatenate(
        [jnp.sum(jnp.where(tile_eye, gram[r:r + TILE, r:r + TILE], 0.0), axis=0, keepdims=True)
         for r in range(0, atoms, TILE)], axis=1)
    cross, change = half_change(gram, corr)
    squares = squares + 2.0 * step * jnp.sum(weighted * change, axis=0, keepdims=True)
    scale = 1.0 / jnp.sqrt(jnp.maximum(squares, 1.0))
    outer = dot3(w, halves(change), TN)
    gram = (gram + step * (outer + outer.T)) * scale * column(scale)
    corr = (corr + step * dot3(halves(cross), w)) * scale
    squares = squares * scale * scale
    _, change = half_change(gram, corr)
    squares = squares + 2.0 * step * jnp.sum(weighted * change, axis=0, keepdims=True)
    last_scale = 1.0 / jnp.sqrt(jnp.maximum(squares, 1.0))
    outer = dot3(w, halves(change), TN)
    gram_ref[...] = (gram + step * (outer + outer.T)) * last_scale * column(last_scale)
    gram_copy = pltpu.make_async_copy(gram_ref, gram_hbm, sems.at[1])
    gram_copy.start()

    copies = [code_copy, gram_copy]
    for j, here in enumerate(rows_of):
        now = (dict_ref[here, :] + step * new_ref[here, :]) * scale
        new_ref[here, :] = (now + step * pulled(now, here)) * last_scale
        copy = pltpu.make_async_copy(new_ref.at[here, :], new_hbm.at[here, :], sems.at[2 + j])
        copy.start()
        copies.append(copy)
    for copy in copies:
        copy.wait()


def all_reduce(keep, send, devices, bits):
    def swap(x, bit):
        return lax.ppermute(x, "vox", [(i, i ^ bit) for i in range(devices)])

    total = keep + swap(send, 1)
    mid = bits - 1
    flips = []
    for o in range(1 << mid):
        flips.append(sum(1 << (bits - 1 - j) for j in range(mid) if (o >> j) & 1))
    parts = [total[o] for o in range(1 << mid)]
    got = [swap(parts[o], flips[o]) for o in range(1, 1 << mid)]
    own = parts[0]
    for part in got:
        own = own + part
    for k in range(bits, devices.bit_length() - 1):
        own = own + swap(own, 3 << (k - 1) if k == bits else 1 << k)
    mine = jnp.stack([own] + [swap(own, flips[o]) for o in range(1, 1 << mid)])
    return mine, swap(mine, 1)


def pin(x):
    return pltpu.with_memory_space_constraint(x, pltpu.HBM)


def shards(devices, volumes, record_index, fold_of, held_out, dictionary):
    records, voxels = volumes.shape
    batch = record_index.shape[0]
    atoms = dictionary.shape[1]
    tiles = upper_tiles(batch, atoms)
    bits = 3
    slots = 1 << bits
    part = jax.ShapeDtypeStruct((slots // 2, len(tiles) * TILE // slots, TILE), F32)
    vmem = pl.BlockSpec(memory_space=pltpu.VMEM)
    smem = pl.BlockSpec(memory_space=pltpu.SMEM)
    hbm = pl.BlockSpec(memory_space=pltpu.HBM)
    full = pltpu.VMEM((batch + atoms, batch + atoms), F32)
    params = pltpu.CompilerParams(vmem_limit_bytes=48 << 20)
    keep, send, flipped, weight = pl.pallas_call(
        functools.partial(gram_kernel, tiles, bits),
        out_shape=(part, part, jax.ShapeDtypeStruct((voxels, batch), F32), jax.ShapeDtypeStruct((batch, TILE), F32)),
        in_specs=[hbm, hbm, smem, hbm, hbm],
        out_specs=(vmem,) * 4,
        scratch_shapes=[pltpu.VMEM((1, batch), jnp.int32), pltpu.VMEM((1, records), jnp.int32),
                        pltpu.VMEM(volumes.shape, F32), pltpu.VMEM(dictionary.shape, F32), full,
                        pltpu.SemaphoreType.DMA((4,))],
        compiler_params=params,
        name="grams",
    )(pin(record_index[None]), pin(fold_of[None]), held_out, pin(volumes), pin(dictionary))
    mine, other = all_reduce(keep, send, devices, bits)
    outs = [dictionary.shape, (batch, atoms), (atoms, atoms)]
    return pl.pallas_call(
        functools.partial(step_kernel, tiles, bits),
        out_shape=tuple(jax.ShapeDtypeStruct(shape, F32) for shape in outs),
        in_specs=[vmem] * 5,
        out_specs=(hbm,) * 3,
        scratch_shapes=[full] + [pltpu.VMEM(shape, F32) for shape in outs] + [pltpu.SemaphoreType.DMA((5,))],
        compiler_params=params,
        name="step",
    )(mine, other, flipped, weight, dictionary)


def solution(mesh):
    devices = mesh.shape["vox"]
    in_specs = (P("fold", "vox"), P("fold"), P("fold"), P("fold"), P("vox", None))
    out_specs = (P(("fold", "vox"), None), P("fold", None), P("fold", None))
    return jax.shard_map(functools.partial(shards, devices), mesh=mesh, in_specs=in_specs, out_specs=out_specs, check_vma=False)
```

time: 59.6 us -> 53.2 us (0.89)
  local copies, waits for them, and re-layouts: 4.21 us -> 0.04 us
  waiting for transfers between devices: 26.9 us -> 22.8 us
  starting transfers between devices: 11.3 us -> 12.4 us
  Pallas kernels: 15.3 us -> 16.3 us
    unnamed x10 -> x2, local copies, waits for them, and re-layouts: 4.18 us -> 0.01 us
    ppermute x9, waiting for transfers between devices: 26.9 us -> 22.8 us  [swap(): return lax.ppermute(x, 'vox', [(i, i ^ bit) for i in range(devices)])]
    pallas_call x1, Pallas kernels: 3.03 us -> 5.3 us  [shards(): pl.pallas_call(functools.partial(gram_kernel, tiles, bits), out_shape=(pa...]
    pallas_call x1, Pallas kernels: 12.3 us -> 11 us  [shards(): pl.pallas_call(functools.partial(step_kernel, tiles, bits), out_shape=tup...]
    ppermute x9, starting transfers between devices: 11.3 us -> 12.4 us  [swap(): return lax.ppermute(x, 'vox', [(i, i ^ bit) for i in range(devices)])]
  transfers between devices with their start and end apart: 9 -> 9, of which waited for: 9 -> 8; matrix products, arithmetic and copies ran while one was open for 0% -> 0% of each run, Pallas kernels for 0% -> 0%
where the time goes in v2:
time: 53.2 us; the launch traced here: 53 us
  waiting for transfers between devices  22.8 us (43%)
  Pallas kernels  16.3 us (31%)
  starting transfers between devices  12.4 us (23%)
  between operations  1.33 us (2%)
    ppermute x9, waiting for transfers between devices, swap(): return lax.ppermute(x, 'vox', [(i, i ^ bit) for i in range(devices)])  22.8 us
    ppermute x9, starting transfers between devices, swap(): return lax.ppermute(x, 'vox', [(i, i ^ bit) for i in range(devices)])  12.4 us
    pallas_call x1, Pallas kernels, shards(): pl.pallas_call(functools.partial(step_kernel, tiles, bits), out_shape=tup...  11 us
    pallas_call x1, Pallas kernels, shards(): pl.pallas_call(functools.partial(gram_kernel, tiles, bits), out_shape=(pa...  5.3 us
  transfers between devices with their start and end apart: 9, of which 8 were waited for; matrix products, arithmetic and copies ran while one was open for 0% of the time, Pallas kernels for 0%

profile of v2, /device:TPU:0, one launch (start us, length us, event | category | flops | bytes accessed | tf_op | source)
XLA Modules:
  0.0 53.0 jit_solution(1613588958934516087)
XLA Ops:
  1.3 5.3 %grams.1 = (f32[4,336,128]{2,1,0:T(8,128)S(1)}, f32[4,336,128]{2,1,0:T(8,128)S(1)}, f32[768,256]{1,0:T(8,128)S(1)}, f32[256,128]{1,0:T(8,128)S(1)}) custom-call(s32[1,256]{1,0:T(1,128)} %bitcast.25, s32[1,512]{1,0:T(1,128)} %bitcast.24, s32[1]{0:T(128)S(6)} %copy.8.held_ref, f32[512,768]{1,0:T(8,128)} %volumes_hbm.1, f32[768,512]{1,0:T(8,128)} %dict_ref.1), custom_call_target="tpu_custom_call" | custom-call | tf_op jit(solution)/shard_map/grams/pallas_call | solution.py:221
  6.6 0.5 collective-permute-start
  7.1 1.8 %collective-permute-done = f32[4,336,128]{2,1,0:T(8,128)S(1)} collective-permute-done((f32[4,336,128]{2,1,0:T(8,128)S(1)}, f32[4,336,128]{2,1,0:T(8,128)S(1)}, u32[]{:S(2)}, u32[]{:S(2)}) %collective-permute-start) | collective-permute-done | bytes 688160 | tf_op jit(solution)/shard_map/ppermute | solution.py:186
  8.9 0.1 add.15
  9.0 0.0 copy-start
  9.0 3.0 %collective-permute-start.1 = (f32[336,128]{1,0:T(8,128)S(1)}, f32[336,128]{1,0:T(8,128)S(1)}, u32[]{:S(2)}, u32[]{:S(2)}) collective-permute-start(f32[336,128]{1,0:T(8,128)S(1)} %get-tuple-element.11), channel_id=1, source_target_pairs={{0,4},{1,5},{2,6},{3,7},{4,0},{5,1},{6,2},{7,3},{8,12},{9,13},{10,... | collective-permute-start | bytes 516104 | tf_op jit(solution)/shard_map/ppermute | solution.py:186
  12.0 1.4 %collective-permute-start.3 = (f32[336,128]{1,0:T(8,128)S(1)}, f32[336,128]{1,0:T(8,128)S(1)}, u32[]{:S(2)}, u32[]{:S(2)}) collective-permute-start(f32[336,128]{1,0:T(8,128)S(1)} %get-tuple-element.12), channel_id=1, source_target_pairs={{0,6},{1,7},{2,4},{3,5},{4,2},{5,3},{6,0},{7,1},{8,14},{9,15},{10,... | collective-permute-start | bytes 516104 | tf_op jit(solution)/shard_map/ppermute | solution.py:186
  13.4 0.2 collective-permute-start.2
  13.5 3.6 %collective-permute-done.1 = f32[336,128]{1,0:T(8,128)S(1)} collective-permute-done((f32[336,128]{1,0:T(8,128)S(1)}, f32[336,128]{1,0:T(8,128)S(1)}, u32[]{:S(2)}, u32[]{:S(2)}) %collective-permute-start.1) | collective-permute-done | bytes 172064 | tf_op jit(solution)/shard_map/ppermute | solution.py:186
  17.2 4.4 %collective-permute-done.3 = f32[336,128]{1,0:T(8,128)S(1)} collective-permute-done((f32[336,128]{1,0:T(8,128)S(1)}, f32[336,128]{1,0:T(8,128)S(1)}, u32[]{:S(2)}, u32[]{:S(2)}) %collective-permute-start.3) | collective-permute-done | bytes 172064 | tf_op jit(solution)/shard_map/ppermute | solution.py:186
  21.6 1.4 %collective-permute-done.2 = f32[336,128]{1,0:T(8,128)S(1)} collective-permute-done((f32[336,128]{1,0:T(8,128)S(1)}, f32[336,128]{1,0:T(8,128)S(1)}, u32[]{:S(2)}, u32[]{:S(2)}) %collective-permute-start.2) | collective-permute-done | bytes 172064 | tf_op jit(solution)/shard_map/ppermute | solution.py:186
  23.0 3.7 %collective-permute-start.4 = (f32[336,128]{1,0:T(8,128)S(1)}, f32[336,128]{1,0:T(8,128)S(1)}, u32[]{:S(2)}, u32[]{:S(2)}) collective-permute-start(f32[336,128]{1,0:T(8,128)S(1)} %fusion.2), channel_id=1, source_target_pairs={{0,12},{1,13},{2,14},{3,15},{4,8},{5,9},{6,10},{7,11},{8,4},{9,5},... | collective-permute-start | bytes 516104 | tf_op jit(solution)/shard_map/ppermute | solution.py:186
  26.6 4.7 %collective-permute-done.4 = f32[336,128]{1,0:T(8,128)S(1)} collective-permute-done((f32[336,128]{1,0:T(8,128)S(1)}, f32[336,128]{1,0:T(8,128)S(1)}, u32[]{:S(2)}, u32[]{:S(2)}) %collective-permute-start.4) | collective-permute-done | bytes 172064 | tf_op jit(solution)/shard_map/ppermute | solution.py:186
  31.4 1.2 %collective-permute-start.7 = (f32[336,128]{1,0:T(8,128)S(1)}, f32[336,128]{1,0:T(8,128)S(1)}, u32[]{:S(2)}, u32[]{:S(2)}) collective-permute-start(f32[336,128]{1,0:T(8,128)S(1)} %add.19), channel_id=1, source_target_pairs={{0,6},{1,7},{2,4},{3,5},{4,2},{5,3},{6,0},{7,1},{8,14},{9,15},{10,... | collective-permute-start | bytes 516104 | tf_op jit(solution)/shard_map/ppermute | solution.py:186
  32.5 1.5 %collective-permute-start.6 = (f32[336,128]{1,0:T(8,128)S(1)}, f32[336,128]{1,0:T(8,128)S(1)}, u32[]{:S(2)}, u32[]{:S(2)}) collective-permute-start(f32[336,128]{1,0:T(8,128)S(1)} %add.19), channel_id=1, source_target_pairs={{0,2},{1,3},{2,0},{3,1},{4,6},{5,7},{6,4},{7,5},{8,10},{9,11},{10,... | collective-permute-start | bytes 516104 | tf_op jit(solution)/shard_map/ppermute | solution.py:186
  34.0 0.9 %collective-permute-start.5 = (f32[336,128]{1,0:T(8,128)S(1)}, f32[336,128]{1,0:T(8,128)S(1)}, u32[]{:S(2)}, u32[]{:S(2)}) collective-permute-start(f32[336,128]{1,0:T(8,128)S(1)} %add.19), channel_id=1, source_target_pairs={{0,4},{1,5},{2,6},{3,7},{4,0},{5,1},{6,2},{7,3},{8,12},{9,13},{10,... | collective-permute-start | bytes 516104 | tf_op jit(solution)/shard_map/ppermute | solution.py:186
  34.9 3.5 %collective-permute-done.7 = f32[336,128]{1,0:T(8,128)S(1)} collective-permute-done((f32[336,128]{1,0:T(8,128)S(1)}, f32[336,128]{1,0:T(8,128)S(1)}, u32[]{:S(2)}, u32[]{:S(2)}) %collective-permute-start.7) | collective-permute-done | bytes 172064 | tf_op jit(solution)/shard_map/ppermute | solution.py:186
  38.4 1.3 %collective-permute-done.6 = f32[336,128]{1,0:T(8,128)S(1)} collective-permute-done((f32[336,128]{1,0:T(8,128)S(1)}, f32[336,128]{1,0:T(8,128)S(1)}, u32[]{:S(2)}, u32[]{:S(2)}) %collective-permute-start.6) | collective-permute-done | bytes 172064 | tf_op jit(solution)/shard_map/ppermute | solution.py:186
  39.7 0.0 collective-permute-done.5
  39.7 0.1 collective-permute-start.8
  39.8 2.1 %collective-permute-done.8.other_ref = f32[4,336,128]{2,1,0:T(8,128)S(1)} collective-permute-done((f32[4,336,128]{2,1,0:T(8,128)S(1)}, f32[4,336,128]{2,1,0:T(8,128)S(1)}, u32[]{:S(2)}, u32[]{:S(2)}) %collective-permute-start.8) | collective-permute-done | bytes 688160 | tf_op jit(solution)/shard_map/ppermute | solution.py:186
  42.0 0.0 copy-done
  42.0 11.0 %step.1 = (f32[768,512]{1,0:T(8,128)}, f32[256,512]{1,0:T(8,128)}, f32[512,512]{1,0:T(8,128)}) custom-call(f32[4,336,128]{2,1,0:T(8,128)S(1)} %pad_maximum_fusion.mine_ref, f32[4,336,128]{2,1,0:T(8,128)S(1)} %collective-permute-done.8.other_ref, f32[768,256]{1,0:T(8,128)S(1)} %get-tuple-element.9.flipped_ref, f32[256,128]{1,0:T(8,128)S(1)} %get-tuple-element.10.weight_ref, ...), custom_call_target="tpu_custom_call" | custom-call | tf_op jit(solution)/shard_map/step/pallas_call | solution.py:234
  (4 shorter events, 0.1 us)
Async XLA Ops:
  6.6 2.3 %collective-permute-start = (f32[4,336,128]{2,1,0:T(8,128)S(1)}, f32[4,336,128]{2,1,0:T(8,128)S(1)}, u32[]{:S(2)}, u32[]{:S(2)}) collective-permute-start(f32[4,336,128]{2,1,0:T(8,128)S(1)} %get-tuple-element.8), channel_id=1, source_target_pairs={{0,1},{1,0},{2,3},{3,2},{4,5},{5,4},{6,7},{7,6},{8,9},{9,8},{10,11... | collective-permute-start | bytes 2064392 | tf_op jit(solution)/shard_map/ppermute | solution.py:186
  9.0 33.0 %copy-start = (f32[768,512]{1,0:T(8,128)S(1)}, f32[768,512]{1,0:T(8,128)}, u32[]{:S(2)}) copy-start(f32[768,512]{1,0:T(8,128)} %dict_ref.1) | copy-start | bytes 4718596
  9.0 8.2 %collective-permute-start.1 = (f32[336,128]{1,0:T(8,128)S(1)}, f32[336,128]{1,0:T(8,128)S(1)}, u32[]{:S(2)}, u32[]{:S(2)}) collective-permute-start(f32[336,128]{1,0:T(8,128)S(1)} %get-tuple-element.11), channel_id=1, source_target_pairs={{0,4},{1,5},{2,6},{3,7},{4,0},{5,1},{6,2},{7,3},{8,12},{9,13},{10,... | collective-permute-start | bytes 516104 | tf_op jit(solution)/shard_map/ppermute | solution.py:186
  12.0 9.6 %collective-permute-start.3 = (f32[336,128]{1,0:T(8,128)S(1)}, f32[336,128]{1,0:T(8,128)S(1)}, u32[]{:S(2)}, u32[]{:S(2)}) collective-permute-start(f32[336,128]{1,0:T(8,128)S(1)} %get-tuple-element.12), channel_id=1, source_target_pairs={{0,6},{1,7},{2,4},{3,5},{4,2},{5,3},{6,0},{7,1},{8,14},{9,15},{10,... | collective-permute-start | bytes 516104 | tf_op jit(solution)/shard_map/ppermute | solution.py:186
  13.4 9.5 %collective-permute-start.2 = (f32[336,128]{1,0:T(8,128)S(1)}, f32[336,128]{1,0:T(8,128)S(1)}, u32[]{:S(2)}, u32[]{:S(2)}) collective-permute-start(f32[336,128]{1,0:T(8,128)S(1)} %get-tuple-element.13), channel_id=1, source_target_pairs={{0,2},{1,3},{2,0},{3,1},{4,6},{5,7},{6,4},{7,5},{8,10},{9,11},{10,... | collective-permute-start | bytes 516104 | tf_op jit(solution)/shard_map/ppermute | solution.py:186
  23.0 8.4 %collective-permute-start.4 = (f32[336,128]{1,0:T(8,128)S(1)}, f32[336,128]{1,0:T(8,128)S(1)}, u32[]{:S(2)}, u32[]{:S(2)}) collective-permute-start(f32[336,128]{1,0:T(8,128)S(1)} %fusion.2), channel_id=1, source_target_pairs={{0,12},{1,13},{2,14},{3,15},{4,8},{5,9},{6,10},{7,11},{8,4},{9,5},... | collective-permute-start | bytes 516104 | tf_op jit(solution)/shard_map/ppermute | solution.py:186
  31.4 7.0 %collective-permute-start.7 = (f32[336,128]{1,0:T(8,128)S(1)}, f32[336,128]{1,0:T(8,128)S(1)}, u32[]{:S(2)}, u32[]{:S(2)}) collective-permute-start(f32[336,128]{1,0:T(8,128)S(1)} %add.19), channel_id=1, source_target_pairs={{0,6},{1,7},{2,4},{3,5},{4,2},{5,3},{6,0},{7,1},{8,14},{9,15},{10,... | collective-permute-start | bytes 516104 | tf_op jit(solution)/shard_map/ppermute | solution.py:186
  32.5 7.2 %collective-permute-start.6 = (f32[336,128]{1,0:T(8,128)S(1)}, f32[336,128]{1,0:T(8,128)S(1)}, u32[]{:S(2)}, u32[]{:S(2)}) collective-permute-start(f32[336,128]{1,0:T(8,128)S(1)} %add.19), channel_id=1, source_target_pairs={{0,2},{1,3},{2,0},{3,1},{4,6},{5,7},{6,4},{7,5},{8,10},{9,11},{10,... | collective-permute-start | bytes 516104 | tf_op jit(solution)/shard_map/ppermute | solution.py:186
  34.0 5.7 %collective-permute-start.5 = (f32[336,128]{1,0:T(8,128)S(1)}, f32[336,128]{1,0:T(8,128)S(1)}, u32[]{:S(2)}, u32[]{:S(2)}) collective-permute-start(f32[336,128]{1,0:T(8,128)S(1)} %add.19), channel_id=1, source_target_pairs={{0,4},{1,5},{2,6},{3,7},{4,0},{5,1},{6,2},{7,3},{8,12},{9,13},{10,... | collective-permute-start | bytes 516104 | tf_op jit(solution)/shard_map/ppermute | solution.py:186
  39.7 2.2 %collective-permute-start.8 = (f32[4,336,128]{2,1,0:T(8,128)S(1)}, f32[4,336,128]{2,1,0:T(8,128)S(1)}, u32[]{:S(2)}, u32[]{:S(2)}) collective-permute-start(f32[4,336,128]{2,1,0:T(8,128)S(1)} %pad_maximum_fusion.mine_ref), channel_id=1, source_target_pairs={{0,1},{1,0},{2,3},{3,2},{4,5},{5,4},{6,7},{7,6},{8,9},{9,8},{10,11... | collective-permute-start | bytes 2064392 | tf_op jit(solution)/shard_map/ppermute | solution.py:186

commit v3 on v2

--- a/solution.py
+++ b/solution.py
@@ -10,6 +10,9 @@
 ISTA_STEPS = 5
 PENALTY = 0.5
 TILE = 128
+SPARE = 8
+BITS = 3
+SQUARE = (4, 6, 2)
 F32 = jnp.float32
 BF16 = jnp.bfloat16
 
@@ -35,27 +38,61 @@
     return jnp.max(jnp.sum(jnp.abs(x), axis=1, keepdims=True), axis=0, keepdims=True)
 
 
-def upper_tiles(batch, atoms):
-    edge = (batch + atoms) // TILE
-    return [(r, c) for r in range(edge) for c in range(r, edge)]
-
-
-def slot_of(vox, bits):
-    place = 0
-    for k in range(bits):
-        bit = (vox >> k) & 1
-        if k == bits - 1:
-            bit = bit ^ ((vox >> bits) & 1)
-        place = place + bit * (1 << (bits - 1 - k))
-    return place
+def upper_tiles(first, count):
+    ends = range(first, first + count)
+    return [(r, c) for r in ends for c in ends if c > r], [(r, r + 1) for r in ends[::2]]
+
+
+def layout(batch, atoms):
+    edge, wide = batch // TILE, atoms // TILE
+    grams = []
+    for fold in range(2):
+        plain, pairs = upper_tiles(edge + fold * wide // 2, wide // 2)
+        strip = range(edge + fold * wide // 4, edge + (fold + 1) * wide // 4)
+        plain = plain + [(r, c) for r in strip for c in range(edge + wide // 2, edge + wide)]
+        grams.append((pairs, plain))
+    plain, pairs = upper_tiles(0, edge)
+    rest = (pairs, plain + [(r, c) for r in range(edge) for c in range(edge, edge + wide)])
+    return grams, rest
+
+
+def slot_of(vox):
+    x = (vox >> 1) & 1
+    z = ((vox >> 2) ^ (vox >> 3)) & 1
+    return (vox & 1) * 4 + x * 2 + (x ^ z)
 
 
 def column(row):
     return jnp.broadcast_to(row, (TILE, row.shape[1])).T[:, :1]
 
 
-def gram_kernel(tiles, bits, index_hbm, fold_hbm, held_ref, volumes_hbm, dict_hbm,
-                keep_ref, send_ref, flipped_ref, weight_ref, index_ref, fold_ref, volumes_ref, dict_ref, full, sems):
+def eye_tile():
+    rows = lax.broadcasted_iota(jnp.int32, (TILE, TILE), 0)
+    columns = lax.broadcasted_iota(jnp.int32, (TILE, TILE), 1)
+    return rows, columns
+
+
+def pack(pairs, plain, block, first, stage, at):
+    rows, columns = eye_tile()
+
+    def tile(r, c):
+        r, c = (r - first[0]) * TILE, (c - first[1]) * TILE
+        return block[r:r + TILE, c:c + TILE]
+
+    apart = []
+    for one, other in pairs:
+        low = tile(other, other)
+        stage[at * TILE:(at + 1) * TILE, :] = jnp.where(rows <= columns, tile(one, one), low)
+        apart.append(jnp.sum(jnp.where(rows == columns, low, 0.0), axis=0, keepdims=True))
+        at += 1
+    for r, c in plain:
+        stage[at * TILE:(at + 1) * TILE, :] = tile(r, c)
+        at += 1
+    return apart, at
+
+
+def gram_kernel(index_hbm, fold_hbm, held_ref, volumes_hbm, dict_hbm,
+                keep_ref, send_ref, flipped_ref, weight_ref, index_ref, fold_ref, volumes_ref, dict_ref, stage, sems):
     pairs = ((dict_hbm, dict_ref), (index_hbm, index_ref), (fold_hbm, fold_ref), (volumes_hbm, volumes_ref))
     copies = [pltpu.make_async_copy(source, target, sems.at[j]) for j, (source, target) in enumerate(pairs)]
     for copy in copies:
@@ -63,12 +100,20 @@
     batch = index_ref.shape[1]
     records = volumes_ref.shape[0]
     atoms = dict_ref.shape[1]
+    edge = batch // TILE
+    wide = atoms // TILE
+    grams, (rest_pairs, rest_plain) = layout(batch, atoms)
+    fold = lax.axis_index("fold") & 1
     copies[0].wait()
     d = halves(dict_ref[...])
-    for r in range(0, atoms, 256):
-        left = (d[0][:, r:r + 256], d[1][:, r:r + 256])
-        right = (d[0][:, r:], d[1][:, r:])
-        full[batch + r:batch + r + 256, batch + r:] = dot3(left, right, TN)
+    far = slice(atoms // 2, atoms)
+    mine = halves(dict_ref[:, pl.ds(pl.multiple_of(fold * (atoms // 2), TILE), atoms // 2)])
+    strip = halves(dict_ref[:, pl.ds(pl.multiple_of(fold * (atoms // 4), TILE), atoms // 4)])
+    near, plain = grams[0]
+    apart, at = pack(near, [t for t in plain if t[1] < edge + wide // 2], dot3(mine, mine, TN), (edge, edge), stage, 0)
+    _, at = pack([], [t for t in plain if t[1] >= edge + wide // 2],
+                 dot3(strip, (d[0][:, far], d[1][:, far]), TN), (edge, edge + wide // 2), stage, at)
+    first = at
     for copy in copies[1:]:
         copy.wait()
     pick = lax.broadcasted_iota(jnp.int32, (records, batch), 0) == index_ref[...]
@@ -77,39 +122,77 @@
     b = (dot1(pick, v[0], TN), dot1(pick, v[1], TN))
     flipped_ref[...] = (b[0] + b[1]).T
     b = (b[0].astype(BF16), b[1].astype(BF16))
-    full[:batch, batch:] = dot3(b, d)
-    full[:batch, :batch] = dot3(b, b, NT)
-    fold = jnp.broadcast_to(fold_ref[...], (TILE, records)).astype(F32).astype(BF16)
-    folds = dot1(pick, fold, (((0,), (1,)), ((), ())))
+    own, at = pack(rest_pairs, [t for t in rest_plain if t[1] < edge], dot3(b, b, NT), (0, 0), stage, at)
+    _, at = pack([], [t for t in rest_plain if t[1] >= edge], dot3(b, d), (0, edge), stage, at)
+    folds = jnp.broadcast_to(fold_ref[...], (TILE, records)).astype(F32).astype(BF16)
+    folds = dot1(pick, folds, (((0,), (1,)), ((), ())))
     weight_ref[...] = jnp.where(folds != held_ref[0].astype(F32), 1.0, 0.0)
-    slots = 1 << bits
+
+    place = lax.broadcasted_iota(jnp.int32, (SPARE, TILE), 0) - fold * (SPARE // 2)
+    spare = jnp.zeros((SPARE, TILE), F32)
+    for j, row in enumerate(apart + own):
+        spare = spare + jnp.where(place == j, row, 0.0)
+    slots = 1 << BITS
     rows = TILE // slots
-    mine = slot_of(lax.axis_index("vox"), bits)
+    me = slot_of(lax.axis_index("vox"))
     half = slots // 2
     for o in range(slots):
         out = keep_ref if o < half else send_ref
-        start = (mine ^ o) * rows
-        for k, (r, c) in enumerate(tiles):
-            at = pl.multiple_of(r * TILE + start, rows)
-            out[o % half, k * rows:(k + 1) * rows, :] = full[pl.ds(at, rows), c * TILE:(c + 1) * TILE]
-
-
-def step_kernel(tiles, bits, mine_ref, other_ref, flipped_ref, weight_ref, dict_ref,
-                new_hbm, code_hbm, gram_hbm, full, new_ref, code_ref, gram_ref, sems):
+        which = me ^ o
+        base = o % half * (at * rows + SPARE)
+        for k in range(at):
+            to = base + k * rows + (SPARE if k >= first else 0)
+            out[to:to + rows, :] = stage[pl.ds(pl.multiple_of(k * TILE + which * rows, rows), rows), :]
+        out[base + first * rows:base + first * rows + SPARE, :] = jnp.where(which == 0, spare, 0.0)
+
+
+def step_kernel(mine_ref, other_ref, flipped_ref, weight_ref, dict_ref,
+                new_hbm, code_hbm, gram_hbm, full, stage, new_ref, code_ref, gram_ref, sems):
     batch = flipped_ref.shape[1]
     voxels, atoms = dict_ref.shape
-    slots = 1 << bits
+    slots = 1 << BITS
     rows = TILE // slots
     half = slots // 2
-    place = slot_of(lax.axis_index("vox"), bits)
+    place = slot_of(lax.axis_index("vox"))
+    grams, rest = layout(batch, atoms)
+    kinds = []
+    for pairs, plain in grams + [rest]:
+        kinds += [(pair, True) for pair in pairs] + [(tile, False) for tile in plain]
+    split = len(kinds) - len(rest[0]) - len(rest[1])
+    spare = jnp.zeros((SPARE, TILE), F32)
     for o in range(slots):
         source = mine_ref if o < half else other_ref
         start = (place ^ o) * rows
-        for k, (r, c) in enumerate(tiles):
-            at = pl.multiple_of(r * TILE + start, rows)
-            full[pl.ds(at, rows), c * TILE:(c + 1) * TILE] = source[o % half, k * rows:(k + 1) * rows, :]
-    for r, c in tiles:
-        if r != c and (r * TILE >= batch or c * TILE < batch):
+        base = o % half * (len(kinds) * rows + SPARE)
+        packed = 0
+        for k, ((r, c), pair) in enumerate(kinds):
+            at = base + k * rows + (SPARE if k >= split else 0)
+            value = source[at:at + rows, :]
+            if pair:
+                stage[pl.ds(pl.multiple_of(packed * TILE + start, rows), rows), :] = value
+                packed += 1
+            else:
+                full[pl.ds(pl.multiple_of(r * TILE + start, rows), rows), c * TILE:(c + 1) * TILE] = value
+        spare = spare + source[base + split * rows:base + split * rows + SPARE, :]
+    across, down = eye_tile()
+    own = len(grams[0][0])
+    mate = lax.axis_index("fold") & 1
+    packed = 0
+    for k, ((r, c), pair) in enumerate(kinds):
+        if pair:
+            value = stage[packed * TILE:(packed + 1) * TILE, :]
+            turned = value.T
+            if packed < 2 * own:
+                at = packed // own * (SPARE // 2) + packed % own
+                diagonal = spare[at:at + 1, :]
+            else:
+                at = own + packed - 2 * own
+                diagonal = jnp.where(mate == 0, spare[at:at + 1, :], spare[at + SPARE // 2:at + SPARE // 2 + 1, :])
+            packed += 1
+            full[r * TILE:(r + 1) * TILE, r * TILE:(r + 1) * TILE] = jnp.where(across <= down, value, turned)
+            full[c * TILE:(c + 1) * TILE, c * TILE:(c + 1) * TILE] = jnp.where(
+                across == down, diagonal, jnp.where(across > down, value, turned))
+        elif r * TILE >= batch or c * TILE < batch:
             full[c * TILE:(c + 1) * TILE, r * TILE:(r + 1) * TILE] = full[r * TILE:(r + 1) * TILE, c * TILE:(c + 1) * TILE].T
 
     gram = full[batch:, batch:]
@@ -181,23 +264,29 @@
         copy.wait()
 
 
-def all_reduce(keep, send, devices, bits):
+def all_reduce(keep, send, gram_rows, devices, folds):
     def swap(x, bit):
         return lax.ppermute(x, "vox", [(i, i ^ bit) for i in range(devices)])
 
     total = keep + swap(send, 1)
-    mid = bits - 1
-    flips = []
-    for o in range(1 << mid):
-        flips.append(sum(1 << (bits - 1 - j) for j in range(mid) if (o >> j) & 1))
-    parts = [total[o] for o in range(1 << mid)]
-    got = [swap(parts[o], flips[o]) for o in range(1, 1 << mid)]
-    own = parts[0]
+    slot = total.shape[0] // (len(SQUARE) + 1)
+    own = total[:slot]
+    got = [swap(total[(k + 1) * slot:(k + 2) * slot], bit) for k, bit in enumerate(SQUARE)]
     for part in got:
         own = own + part
-    for k in range(bits, devices.bit_length() - 1):
-        own = own + swap(own, 3 << (k - 1) if k == bits else 1 << k)
-    mine = jnp.stack([own] + [swap(own, flips[o]) for o in range(1, 1 << mid)])
+    gram, rest = own[:gram_rows + SPARE], own[gram_rows + SPARE:]
+    gram, rest = lax.optimization_barrier((gram, rest))
+    for k in range(BITS, devices.bit_length() - 1):
+        bit = 3 << (k - 1) if k == BITS else 1 << k
+        other = swap(rest, bit), swap(gram, bit)
+        gram, rest = gram + other[1], rest + other[0]
+    next_gram = lax.ppermute(gram, "fold", [(i, i ^ 1) for i in range(folds)])
+    next_gram, rest = lax.optimization_barrier((next_gram, rest))
+    even = lax.axis_index("fold") & 1 == 0
+    first = jnp.where(even, gram[:gram_rows], next_gram[:gram_rows])
+    second = jnp.where(even, next_gram[:gram_rows], gram[:gram_rows])
+    own = jnp.concatenate([first, second, gram[gram_rows:] + next_gram[gram_rows:], rest])
+    mine = jnp.concatenate([own] + [swap(own, bit) for bit in SQUARE])
     return mine, swap(mine, 1)
 
 
@@ -205,45 +294,45 @@
     return pltpu.with_memory_space_constraint(x, pltpu.HBM)
 
 
-def shards(devices, volumes, record_index, fold_of, held_out, dictionary):
+def shards(devices, folds, volumes, record_index, fold_of, held_out, dictionary):
     records, voxels = volumes.shape
     batch = record_index.shape[0]
     atoms = dictionary.shape[1]
-    tiles = upper_tiles(batch, atoms)
-    bits = 3
-    slots = 1 << bits
-    part = jax.ShapeDtypeStruct((slots // 2, len(tiles) * TILE // slots, TILE), F32)
+    grams, rest = layout(batch, atoms)
+    gram_tiles, rest_tiles = (len(pairs) + len(plain) for pairs, plain in (grams[0], rest))
+    slots = 1 << BITS
+    part = jax.ShapeDtypeStruct((slots // 2 * ((gram_tiles + rest_tiles) * TILE // slots + SPARE), TILE), F32)
     vmem = pl.BlockSpec(memory_space=pltpu.VMEM)
     smem = pl.BlockSpec(memory_space=pltpu.SMEM)
     hbm = pl.BlockSpec(memory_space=pltpu.HBM)
-    full = pltpu.VMEM((batch + atoms, batch + atoms), F32)
     params = pltpu.CompilerParams(vmem_limit_bytes=48 << 20)
     keep, send, flipped, weight = pl.pallas_call(
-        functools.partial(gram_kernel, tiles, bits),
+        gram_kernel,
         out_shape=(part, part, jax.ShapeDtypeStruct((voxels, batch), F32), jax.ShapeDtypeStruct((batch, TILE), F32)),
         in_specs=[hbm, hbm, smem, hbm, hbm],
         out_specs=(vmem,) * 4,
         scratch_shapes=[pltpu.VMEM((1, batch), jnp.int32), pltpu.VMEM((1, records), jnp.int32),
-                        pltpu.VMEM(volumes.shape, F32), pltpu.VMEM(dictionary.shape, F32), full,
+                        pltpu.VMEM(volumes.shape, F32), pltpu.VMEM(dictionary.shape, F32),
+                        pltpu.VMEM(((gram_tiles + rest_tiles) * TILE, TILE), F32),
                         pltpu.SemaphoreType.DMA((4,))],
         compiler_params=params,
         name="grams",
     )(pin(record_index[None]), pin(fold_of[None]), held_out, pin(volumes), pin(dictionary))
-    mine, other = all_reduce(keep, send, devices, bits)
+    mine, other = all_reduce(keep, send, gram_tiles * TILE // slots, devices, folds)
     outs = [dictionary.shape, (batch, atoms), (atoms, atoms)]
     return pl.pallas_call(
-        functools.partial(step_kernel, tiles, bits),
+        step_kernel,
         out_shape=tuple(jax.ShapeDtypeStruct(shape, F32) for shape in outs),
         in_specs=[vmem] * 5,
         out_specs=(hbm,) * 3,
-        scratch_shapes=[full] + [pltpu.VMEM(shape, F32) for shape in outs] + [pltpu.SemaphoreType.DMA((5,))],
+        scratch_shapes=[pltpu.VMEM((batch + atoms, batch + atoms), F32), pltpu.VMEM(((batch + atoms) // 2, TILE), F32)]
+        + [pltpu.VMEM(shape, F32) for shape in outs] + [pltpu.SemaphoreType.DMA((5,))],
         compiler_params=params,
         name="step",
     )(mine, other, flipped, weight, dictionary)
 
 
 def solution(mesh):
-    devices = mesh.shape["vox"]
     in_specs = (P("fold", "vox"), P("fold"), P("fold"), P("fold"), P("vox", None))
     out_specs = (P(("fold", "vox"), None), P("fold", None), P("fold", None))
-    return jax.shard_map(functools.partial(shards, devices), mesh=mesh, in_specs=in_specs, out_specs=out_specs, check_vma=False)
+    return jax.shard_map(functools.partial(shards, mesh.shape["vox"], mesh.shape["fold"]), mesh=mesh, in_specs=in_specs, out_specs=out_specs, check_vma=False)

time: 53.2 us -> 51.7 us (0.972)
  waiting for transfers between devices: 22.8 us -> 20.5 us
  starting transfers between devices: 12.4 us -> 14.1 us
  Pallas kernels: 16.3 us -> 15.3 us
    ppermute x9 -> x10, waiting for transfers between devices: 22.8 us -> 18.1 us  [swap(): return lax.ppermute(x, 'vox', [(i, i ^ bit) for i in range(devices)])]
    ppermute x0 -> x1, waiting for transfers between devices: none -> 2.42 us  [all_reduce(): next_gram = lax.ppermute(gram, 'fold', [(i, i ^ 1) for i in range(folds)])]
    ppermute x0 -> x1, starting transfers between devices: none -> 1.52 us  [all_reduce(): next_gram = lax.ppermute(gram, 'fold', [(i, i ^ 1) for i in range(folds)])]
    pallas_call x2, Pallas kernels: 16.3 us -> 15.3 us  [the longest x1 11.1 us: shards(): pl.pallas_call(step_kernel, out_shape=tuple((jax.ShapeDtypeStruct(shape,...]
    ppermute x9 -> x10, starting transfers between devices: 12.4 us -> 12.6 us  [swap(): return lax.ppermute(x, 'vox', [(i, i ^ bit) for i in range(devices)])]
  transfers between devices with their start and end apart: 9 -> 11, of which waited for: 8 -> 8; matrix products, arithmetic and copies ran while one was open for 0% -> 0% of each run, Pallas kernels for 0% -> 0%
where the time goes in v3:
time: 51.7 us; the launch traced here: 51.6 us
  waiting for transfers between devices  20.5 us (40%)
  Pallas kernels  15.3 us (30%)
  starting transfers between devices  14.1 us (27%)
  between operations  1.4 us (3%)
    ppermute x10, waiting for transfers between devices, swap(): return lax.ppermute(x, 'vox', [(i, i ^ bit) for i in range(devices)])  18.1 us
    ppermute x10, starting transfers between devices, swap(): return lax.ppermute(x, 'vox', [(i, i ^ bit) for i in range(devices)])  12.6 us
    pallas_call x1, Pallas kernels, shards(): pl.pallas_call(step_kernel, out_shape=tuple((jax.ShapeDtypeStruct(shape,...  11.1 us
    pallas_call x1, Pallas kernels, shards(): pl.pallas_call(gram_kernel, out_shape=(part, part, jax.ShapeDtypeStruct((...  4.23 us
    ppermute x1, waiting for transfers between devices, all_reduce(): next_gram = lax.ppermute(gram, 'fold', [(i, i ^ 1) for i in range(folds)])  2.42 us
    ppermute x1, starting transfers between devices, all_reduce(): next_gram = lax.ppermute(gram, 'fold', [(i, i ^ 1) for i in range(folds)])  1.52 us
  transfers between devices with their start and end apart: 11, of which 8 were waited for; matrix products, arithmetic and copies ran while one was open for 0% of the time, Pallas kernels for 0%

profile of v3, /device:TPU:0, one launch (start us, length us, event | category | flops | bytes accessed | tf_op | source)
XLA Modules:
  0.0 51.6 jit_solution(9246627871739724502)
XLA Ops:
  1.3 4.2 %grams.1 = (f32[928,128]{1,0:T(8,128)S(1)}, f32[928,128]{1,0:T(8,128)S(1)}, f32[768,256]{1,0:T(8,128)S(1)}, f32[256,128]{1,0:T(8,128)S(1)}) custom-call(s32[1,256]{1,0:T(1,128)} %bitcast.3, s32[1,512]{1,0:T(1,128)} %bitcast.2, s32[1]{0:T(128)S(6)} %copy.14.held_ref, f32[512,768]{1,0:T(8,128)} %volumes_hbm.1, f32[768,512]{1,0:T(8,128)} %dict_ref.1), custom_call_target="tpu_custom_call" | custom-call | tf_op jit(solution)/shard_map/grams/pallas_call | solution.py:309
  5.5 0.5 %collective-permute-start = (f32[928,128]{1,0:T(8,128)S(1)}, f32[928,128]{1,0:T(8,128)S(1)}, u32[]{:S(2)}, u32[]{:S(2)}) collective-permute-start(f32[928,128]{1,0:T(8,128)S(1)} %get-tuple-element.12), channel_id=1, source_target_pairs={{0,1},{1,0},{2,3},{3,2},{4,5},{5,4},{6,7},{7,6},{8,9},{9,8},{10,11... | collective-permute-start | bytes 1425416 | tf_op jit(solution)/shard_map/ppermute | solution.py:269
  6.0 1.5 %collective-permute-done = f32[928,128]{1,0:T(8,128)S(1)} collective-permute-done((f32[928,128]{1,0:T(8,128)S(1)}, f32[928,128]{1,0:T(8,128)S(1)}, u32[]{:S(2)}, u32[]{:S(2)}) %collective-permute-start) | collective-permute-done | bytes 475168 | tf_op jit(solution)/shard_map/ppermute | solution.py:269
  7.6 0.0 copy-start
  7.6 3.0 %collective-permute-start.1 = (f32[232,128]{1,0:T(8,128)S(1)}, f32[232,128]{1,0:T(8,128)S(1)}, u32[]{:S(2)}, u32[]{:S(2)}) collective-permute-start(f32[232,128]{1,0:T(8,128)S(1)} %get-tuple-element.25), channel_id=1, source_target_pairs={{0,4},{1,5},{2,6},{3,7},{4,0},{5,1},{6,2},{7,3},{8,12},{9,13},{10,... | collective-permute-start | bytes 356360 | tf_op jit(solution)/shard_map/ppermute | solution.py:269
  10.6 1.5 %collective-permute-start.3 = (f32[232,128]{1,0:T(8,128)S(1)}, f32[232,128]{1,0:T(8,128)S(1)}, u32[]{:S(2)}, u32[]{:S(2)}) collective-permute-start(f32[232,128]{1,0:T(8,128)S(1)} %get-tuple-element.26), channel_id=1, source_target_pairs={{0,2},{1,3},{2,0},{3,1},{4,6},{5,7},{6,4},{7,5},{8,10},{9,11},{10,... | collective-permute-start | bytes 356360 | tf_op jit(solution)/shard_map/ppermute | solution.py:269
  12.1 0.1 collective-permute-start.2
  12.2 2.1 %collective-permute-done.1 = f32[232,128]{1,0:T(8,128)S(1)} collective-permute-done((f32[232,128]{1,0:T(8,128)S(1)}, f32[232,128]{1,0:T(8,128)S(1)}, u32[]{:S(2)}, u32[]{:S(2)}) %collective-permute-start.1) | collective-permute-done | bytes 118816 | tf_op jit(solution)/shard_map/ppermute | solution.py:269
  14.2 3.9 %collective-permute-done.3 = f32[232,128]{1,0:T(8,128)S(1)} collective-permute-done((f32[232,128]{1,0:T(8,128)S(1)}, f32[232,128]{1,0:T(8,128)S(1)}, u32[]{:S(2)}, u32[]{:S(2)}) %collective-permute-start.3) | collective-permute-done | bytes 118816 | tf_op jit(solution)/shard_map/ppermute | solution.py:269
  18.2 0.0 collective-permute-done.2
  18.2 3.3 %collective-permute-start.6 = (f32[160,128]{1,0:T(8,128)S(1)}, f32[160,128]{1,0:T(8,128)S(1)}, u32[]{:S(2)}, u32[]{:S(2)}) collective-permute-start(f32[160,128]{1,0:T(8,128)S(1)} %slice.47), channel_id=1, source_target_pairs={{0,12},{1,13},{2,14},{3,15},{4,8},{5,9},{6,10},{7,11},{8,4},{9,5},... | collective-permute-start | bytes 245768 | tf_op jit(solution)/shard_map/ppermute | solution.py:269
  21.5 0.6 %collective-permute-start.4 = (f32[72,128]{1,0:T(8,128)S(1)}, f32[72,128]{1,0:T(8,128)S(1)}, u32[]{:S(2)}, u32[]{:S(2)}) collective-permute-start(f32[72,128]{1,0:T(8,128)S(1)} %slice.46), channel_id=1, source_target_pairs={{0,12},{1,13},{2,14},{3,15},{4,8},{5,9},{6,10},{7,11},{8,4},{9,5},... | collective-permute-start | bytes 110600 | tf_op jit(solution)/shard_map/ppermute | solution.py:269
  22.1 5.2 %collective-permute-done.4 = f32[72,128]{1,0:T(8,128)S(1)} collective-permute-done((f32[72,128]{1,0:T(8,128)S(1)}, f32[72,128]{1,0:T(8,128)S(1)}, u32[]{:S(2)}, u32[]{:S(2)}) %collective-permute-start.4) | collective-permute-done | bytes 36896 | tf_op jit(solution)/shard_map/ppermute | solution.py:269
  27.3 1.5 %collective-permute-start.5 = (f32[72,128]{1,0:T(8,128)S(1)}, f32[72,128]{1,0:T(8,128)S(1)}, u32[]{:S(2)}, u32[]{:S(2)}) collective-permute-start(f32[72,128]{1,0:T(8,128)S(1)} %add.25), channel_id=1, source_target_pairs={{0,16},{16,0},{1,17},{17,1},{2,18},{18,2},{3,19},{19,3},{4,20},{20... | collective-permute-start | bytes 110600 | tf_op jit(solution)/shard_map/ppermute | solution.py:283
  28.8 0.0 collective-permute-done.6
  28.8 2.4 %collective-permute-done.5 = f32[72,128]{1,0:T(8,128)S(1)} collective-permute-done((f32[72,128]{1,0:T(8,128)S(1)}, f32[72,128]{1,0:T(8,128)S(1)}, u32[]{:S(2)}, u32[]{:S(2)}) %collective-permute-start.5) | collective-permute-done | bytes 36896 | tf_op jit(solution)/shard_map/ppermute | solution.py:283
  31.3 0.1 collective-permute-start.7
  31.4 0.8 %collective-permute-start.9 = (f32[296,128]{1,0:T(8,128)S(1)}, f32[296,128]{1,0:T(8,128)S(1)}, u32[]{:S(2)}, u32[]{:S(2)}) collective-permute-start(f32[296,128]{1,0:T(8,128)S(1)} %pad_maximum_fusion), channel_id=1, source_target_pairs={{0,2},{1,3},{2,0},{3,1},{4,6},{5,7},{6,4},{7,5},{8,10},{9,11},{10,... | collective-permute-start | bytes 454664 | tf_op jit(solution)/shard_map/ppermute | solution.py:269
  32.2 2.7 %collective-permute-start.8 = (f32[296,128]{1,0:T(8,128)S(1)}, f32[296,128]{1,0:T(8,128)S(1)}, u32[]{:S(2)}, u32[]{:S(2)}) collective-permute-start(f32[296,128]{1,0:T(8,128)S(1)} %pad_maximum_fusion), channel_id=1, source_target_pairs={{0,6},{1,7},{2,4},{3,5},{4,2},{5,3},{6,0},{7,1},{8,14},{9,15},{10,... | collective-permute-start | bytes 454664 | tf_op jit(solution)/shard_map/ppermute | solution.py:269
  34.9 1.7 %collective-permute-done.7 = f32[296,128]{1,0:T(8,128)S(1)} collective-permute-done((f32[296,128]{1,0:T(8,128)S(1)}, f32[296,128]{1,0:T(8,128)S(1)}, u32[]{:S(2)}, u32[]{:S(2)}) %collective-permute-start.7) | collective-permute-done | bytes 151584 | tf_op jit(solution)/shard_map/ppermute | solution.py:269
  36.6 1.8 %collective-permute-done.8 = f32[296,128]{1,0:T(8,128)S(1)} collective-permute-done((f32[296,128]{1,0:T(8,128)S(1)}, f32[296,128]{1,0:T(8,128)S(1)}, u32[]{:S(2)}, u32[]{:S(2)}) %collective-permute-start.8) | collective-permute-done | bytes 151584 | tf_op jit(solution)/shard_map/ppermute | solution.py:269
  38.4 0.0 collective-permute-done.9
  38.4 0.1 collective-permute-start.10
  38.5 2.0 %collective-permute-done.10.other_ref = f32[1184,128]{1,0:T(8,128)S(1)} collective-permute-done((f32[1184,128]{1,0:T(8,128)S(1)}, f32[1184,128]{1,0:T(8,128)S(1)}, u32[]{:S(2)}, u32[]{:S(2)}) %collective-permute-start.10) | collective-permute-done | bytes 606240 | tf_op jit(solution)/shard_map/ppermute | solution.py:269
  40.5 0.0 copy-done
  40.5 11.1 %step.1 = (f32[768,512]{1,0:T(8,128)}, f32[256,512]{1,0:T(8,128)}, f32[512,512]{1,0:T(8,128)}) custom-call(f32[1184,128]{1,0:T(8,128)S(1)} %constant_dynamic-update-slice_fusion.mine_ref, f32[1184,128]{1,0:T(8,128)S(1)} %collective-permute-done.10.other_ref, f32[768,256]{1,0:T(8,128)S(1)} %get-tuple-element.17.flipped_ref, ...), custom_call_target="tpu_custom_call" | custom-call | tf_op jit(solution)/shard_map/step/pallas_call | solution.py:323
  (15 shorter events, 0.2 us)
Async XLA Ops:
  5.5 2.0 %collective-permute-start = (f32[928,128]{1,0:T(8,128)S(1)}, f32[928,128]{1,0:T(8,128)S(1)}, u32[]{:S(2)}, u32[]{:S(2)}) collective-permute-start(f32[928,128]{1,0:T(8,128)S(1)} %get-tuple-element.12), channel_id=1, source_target_pairs={{0,1},{1,0},{2,3},{3,2},{4,5},{5,4},{6,7},{7,6},{8,9},{9,8},{10,11... | collective-permute-start | bytes 1425416 | tf_op jit(solution)/shard_map/ppermute | solution.py:269
  7.6 32.9 %copy-start = (f32[768,512]{1,0:T(8,128)S(1)}, f32[768,512]{1,0:T(8,128)}, u32[]{:S(2)}) copy-start(f32[768,512]{1,0:T(8,128)} %dict_ref.1) | copy-start | bytes 4718596
  7.6 6.6 %collective-permute-start.1 = (f32[232,128]{1,0:T(8,128)S(1)}, f32[232,128]{1,0:T(8,128)S(1)}, u32[]{:S(2)}, u32[]{:S(2)}) collective-permute-start(f32[232,128]{1,0:T(8,128)S(1)} %get-tuple-element.25), channel_id=1, source_target_pairs={{0,4},{1,5},{2,6},{3,7},{4,0},{5,1},{6,2},{7,3},{8,12},{9,13},{10,... | collective-permute-start | bytes 356360 | tf_op jit(solution)/shard_map/ppermute | solution.py:269
  10.6 7.5 %collective-permute-start.3 = (f32[232,128]{1,0:T(8,128)S(1)}, f32[232,128]{1,0:T(8,128)S(1)}, u32[]{:S(2)}, u32[]{:S(2)}) collective-permute-start(f32[232,128]{1,0:T(8,128)S(1)} %get-tuple-element.26), channel_id=1, source_target_pairs={{0,2},{1,3},{2,0},{3,1},{4,6},{5,7},{6,4},{7,5},{8,10},{9,11},{10,... | collective-permute-start | bytes 356360 | tf_op jit(solution)/shard_map/ppermute | solution.py:269
  12.1 6.1 %collective-permute-start.2 = (f32[232,128]{1,0:T(8,128)S(1)}, f32[232,128]{1,0:T(8,128)S(1)}, u32[]{:S(2)}, u32[]{:S(2)}) collective-permute-start(f32[232,128]{1,0:T(8,128)S(1)} %get-tuple-element.27), channel_id=1, source_target_pairs={{0,6},{1,7},{2,4},{3,5},{4,2},{5,3},{6,0},{7,1},{8,14},{9,15},{10,... | collective-permute-start | bytes 356360 | tf_op jit(solution)/shard_map/ppermute | solution.py:269
  18.2 10.6 %collective-permute-start.6 = (f32[160,128]{1,0:T(8,128)S(1)}, f32[160,128]{1,0:T(8,128)S(1)}, u32[]{:S(2)}, u32[]{:S(2)}) collective-permute-start(f32[160,128]{1,0:T(8,128)S(1)} %slice.47), channel_id=1, source_target_pairs={{0,12},{1,13},{2,14},{3,15},{4,8},{5,9},{6,10},{7,11},{8,4},{9,5},... | collective-permute-start | bytes 245768 | tf_op jit(solution)/shard_map/ppermute | solution.py:269
  21.5 5.8 %collective-permute-start.4 = (f32[72,128]{1,0:T(8,128)S(1)}, f32[72,128]{1,0:T(8,128)S(1)}, u32[]{:S(2)}, u32[]{:S(2)}) collective-permute-start(f32[72,128]{1,0:T(8,128)S(1)} %slice.46), channel_id=1, source_target_pairs={{0,12},{1,13},{2,14},{3,15},{4,8},{5,9},{6,10},{7,11},{8,4},{9,5},... | collective-permute-start | bytes 110600 | tf_op jit(solution)/shard_map/ppermute | solution.py:269
  27.3 4.0 %collective-permute-start.5 = (f32[72,128]{1,0:T(8,128)S(1)}, f32[72,128]{1,0:T(8,128)S(1)}, u32[]{:S(2)}, u32[]{:S(2)}) collective-permute-start(f32[72,128]{1,0:T(8,128)S(1)} %add.25), channel_id=1, source_target_pairs={{0,16},{16,0},{1,17},{17,1},{2,18},{18,2},{3,19},{19,3},{4,20},{20... | collective-permute-start | bytes 110600 | tf_op jit(solution)/shard_map/ppermute | solution.py:283
  31.3 5.3 %collective-permute-start.7 = (f32[296,128]{1,0:T(8,128)S(1)}, f32[296,128]{1,0:T(8,128)S(1)}, u32[]{:S(2)}, u32[]{:S(2)}) collective-permute-start(f32[296,128]{1,0:T(8,128)S(1)} %pad_maximum_fusion), channel_id=1, source_target_pairs={{0,4},{1,5},{2,6},{3,7},{4,0},{5,1},{6,2},{7,3},{8,12},{9,13},{10,... | collective-permute-start | bytes 454664 | tf_op jit(solution)/shard_map/ppermute | solution.py:269
  31.4 7.0 %collective-permute-start.9 = (f32[296,128]{1,0:T(8,128)S(1)}, f32[296,128]{1,0:T(8,128)S(1)}, u32[]{:S(2)}, u32[]{:S(2)}) collective-permute-start(f32[296,128]{1,0:T(8,128)S(1)} %pad_maximum_fusion), channel_id=1, source_target_pairs={{0,2},{1,3},{2,0},{3,1},{4,6},{5,7},{6,4},{7,5},{8,10},{9,11},{10,... | collective-permute-start | bytes 454664 | tf_op jit(solution)/shard_map/ppermute | solution.py:269
  32.2 6.2 %collective-permute-start.8 = (f32[296,128]{1,0:T(8,128)S(1)}, f32[296,128]{1,0:T(8,128)S(1)}, u32[]{:S(2)}, u32[]{:S(2)}) collective-permute-start(f32[296,128]{1,0:T(8,128)S(1)} %pad_maximum_fusion), channel_id=1, source_target_pairs={{0,6},{1,7},{2,4},{3,5},{4,2},{5,3},{6,0},{7,1},{8,14},{9,15},{10,... | collective-permute-start | bytes 454664 | tf_op jit(solution)/shard_map/ppermute | solution.py:269
  38.4 2.1 %collective-permute-start.10 = (f32[1184,128]{1,0:T(8,128)S(1)}, f32[1184,128]{1,0:T(8,128)S(1)}, u32[]{:S(2)}, u32[]{:S(2)}) collective-permute-start(f32[1184,128]{1,0:T(8,128)S(1)} %constant_dynamic-update-slice_fusion.mine_ref), channel_id=1, source_target_pairs={{0,1},{1,0},{2,3},{3,2},{4,5},{5,4},{6,7},{7,6},{8,9},{9,8},{10,11... | collective-permute-start | bytes 1818632 | tf_op jit(solution)/shard_map/ppermute | solution.py:269

commit v4 on v3

--- a/solution.py
+++ b/solution.py
@@ -31,7 +31,15 @@
 
 
 def dot3(a, b, dims=NN):
-    return dot1(a[0], b[0], dims) + (dot1(a[0], b[1], dims) + dot1(a[1], b[0], dims))
+    (left,), _ = dims[0]
+    rows = a[0].shape[1 - left]
+    both = dot1(jnp.concatenate(a, axis=1 - left), b[0], dims)
+    return both[:rows] + (both[rows:] + dot1(a[0], b[1], dims))
+
+
+def square3(a, b, dims=NN):
+    mixed = dot1(a[0], b[1], dims)
+    return dot1(a[0], b[0], dims) + (mixed + mixed.T)
 
 
 def top_row_sum(x):
@@ -93,7 +101,7 @@
 
 def gram_kernel(index_hbm, fold_hbm, held_ref, volumes_hbm, dict_hbm,
                 keep_ref, send_ref, flipped_ref, weight_ref, index_ref, fold_ref, volumes_ref, dict_ref, stage, sems):
-    pairs = ((dict_hbm, dict_ref), (index_hbm, index_ref), (fold_hbm, fold_ref), (volumes_hbm, volumes_ref))
+    pairs = ((index_hbm, index_ref), (fold_hbm, fold_ref), (volumes_hbm, volumes_ref), (dict_hbm, dict_ref))
     copies = [pltpu.make_async_copy(source, target, sems.at[j]) for j, (source, target) in enumerate(pairs)]
     for copy in copies:
         copy.start()
@@ -104,17 +112,7 @@
     wide = atoms // TILE
     grams, (rest_pairs, rest_plain) = layout(batch, atoms)
     fold = lax.axis_index("fold") & 1
-    copies[0].wait()
-    d = halves(dict_ref[...])
-    far = slice(atoms // 2, atoms)
-    mine = halves(dict_ref[:, pl.ds(pl.multiple_of(fold * (atoms // 2), TILE), atoms // 2)])
-    strip = halves(dict_ref[:, pl.ds(pl.multiple_of(fold * (atoms // 4), TILE), atoms // 4)])
-    near, plain = grams[0]
-    apart, at = pack(near, [t for t in plain if t[1] < edge + wide // 2], dot3(mine, mine, TN), (edge, edge), stage, 0)
-    _, at = pack([], [t for t in plain if t[1] >= edge + wide // 2],
-                 dot3(strip, (d[0][:, far], d[1][:, far]), TN), (edge, edge + wide // 2), stage, at)
-    first = at
-    for copy in copies[1:]:
+    for copy in copies[:-1]:
         copy.wait()
     pick = lax.broadcasted_iota(jnp.int32, (records, batch), 0) == index_ref[...]
     pick = pick.astype(F32).astype(BF16)
@@ -122,7 +120,17 @@
     b = (dot1(pick, v[0], TN), dot1(pick, v[1], TN))
     flipped_ref[...] = (b[0] + b[1]).T
     b = (b[0].astype(BF16), b[1].astype(BF16))
-    own, at = pack(rest_pairs, [t for t in rest_plain if t[1] < edge], dot3(b, b, NT), (0, 0), stage, at)
+    copies[-1].wait()
+    d = halves(dict_ref[...])
+    far = slice(atoms // 2, atoms)
+    mine = halves(dict_ref[:, pl.ds(pl.multiple_of(fold * (atoms // 2), TILE), atoms // 2)])
+    strip = halves(dict_ref[:, pl.ds(pl.multiple_of(fold * (atoms // 4), TILE), atoms // 4)])
+    near, plain = grams[0]
+    apart, at = pack(near, [t for t in plain if t[1] < edge + wide // 2], square3(mine, mine, TN), (edge, edge), stage, 0)
+    _, at = pack([], [t for t in plain if t[1] >= edge + wide // 2],
+                 dot3(strip, (d[0][:, far], d[1][:, far]), TN), (edge, edge + wide // 2), stage, at)
+    first = at
+    own, at = pack(rest_pairs, [t for t in rest_plain if t[1] < edge], square3(b, b, NT), (0, 0), stage, at)
     _, at = pack([], [t for t in rest_plain if t[1] >= edge], dot3(b, d), (0, edge), stage, at)
     folds = jnp.broadcast_to(fold_ref[...], (TILE, records)).astype(F32).astype(BF16)
     folds = dot1(pick, folds, (((0,), (1,)), ((), ())))
@@ -217,49 +225,48 @@
     x = halves(code)
     weighted = code * jnp.concatenate([weight_ref[...]] * (atoms // TILE), axis=1)
     w = halves(weighted)
-    step = 1.0 / (1.0 + top_row_sum(dot3(w, w, TN)))
-
-    block = voxels // 3 if voxels % 3 == 0 and (voxels // 3) % 16 == 0 else voxels
-    rows_of = [slice(at, at + block) for at in range(0, voxels, block)]
-
-    def pulled(now, here):
-        return dot3(halves(flipped_ref[here, :] - dot3(halves(now), x, NT)), w)
-
-    for here in rows_of:
-        new_ref[here, :] = pulled(dict_ref[here, :], here)
-
-    def half_change(gram_now, corr_now):
-        fit = corr_now - dot3(x, halves(gram_now))
-        cross = full[:batch, :batch] - dot3(halves(corr_now), x, NT)
-        square = cross - dot3(x, halves(fit), NT)
-        return cross, fit + (0.5 * step) * dot3(halves(square), w)
-
-    tile_eye = lax.broadcasted_iota(jnp.int32, (TILE, TILE), 0) == lax.broadcasted_iota(jnp.int32, (TILE, TILE), 1)
+    turned_w = halves(weighted.T)
+    fit = corr - dot3(x, g)
+
+    def residuals(corr_now, now):
+        both = dot3(halves(jnp.concatenate([corr_now, now], axis=0)), x, NT)
+        return full[:batch, :batch] - both[:batch], flipped_ref[...] - both[batch:]
+
+    cross, rest = residuals(corr, dict_ref[...])
+    step = 1.0 / (1.0 + top_row_sum(square3(turned_w, w)))
+    square = cross - dot3(x, halves(fit), NT)
+    tile_eye = across == down
     squares = jnp.concatenate(
         [jnp.sum(jnp.where(tile_eye, gram[r:r + TILE, r:r + TILE], 0.0), axis=0, keepdims=True)
          for r in range(0, atoms, TILE)], axis=1)
-    cross, change = half_change(gram, corr)
+    moves = dot3(halves(jnp.concatenate([square, cross, rest], axis=0)), w)
+    change = fit + (0.5 * step) * moves[:batch]
     squares = squares + 2.0 * step * jnp.sum(weighted * change, axis=0, keepdims=True)
     scale = 1.0 / jnp.sqrt(jnp.maximum(squares, 1.0))
-    outer = dot3(w, halves(change), TN)
+    outer = dot3(turned_w, halves(change))
+    corr = (corr + step * moves[batch:2 * batch]) * scale
+    now = (dict_ref[...] + step * moves[2 * batch:]) * scale
+    new_ref[...] = now
+    cross, rest = residuals(corr, now)
     gram = (gram + step * (outer + outer.T)) * scale * column(scale)
-    corr = (corr + step * dot3(halves(cross), w)) * scale
+    fit = corr - dot3(x, halves(gram))
+    square = cross - dot3(x, halves(fit), NT)
     squares = squares * scale * scale
-    _, change = half_change(gram, corr)
+    moves = dot3(halves(jnp.concatenate([square, rest], axis=0)), w)
+    change = fit + (0.5 * step) * moves[:batch]
     squares = squares + 2.0 * step * jnp.sum(weighted * change, axis=0, keepdims=True)
-    last_scale = 1.0 / jnp.sqrt(jnp.maximum(squares, 1.0))
-    outer = dot3(w, halves(change), TN)
-    gram_ref[...] = (gram + step * (outer + outer.T)) * last_scale * column(last_scale)
-    gram_copy = pltpu.make_async_copy(gram_ref, gram_hbm, sems.at[1])
-    gram_copy.start()
-
-    copies = [code_copy, gram_copy]
-    for j, here in enumerate(rows_of):
-        now = (dict_ref[here, :] + step * new_ref[here, :]) * scale
-        new_ref[here, :] = (now + step * pulled(now, here)) * last_scale
-        copy = pltpu.make_async_copy(new_ref.at[here, :], new_hbm.at[here, :], sems.at[2 + j])
-        copy.start()
-        copies.append(copy)
+    scale = 1.0 / jnp.sqrt(jnp.maximum(squares, 1.0))
+    copies = [code_copy]
+    block = voxels // 3 if voxels % 3 == 0 and (voxels // 3) % 16 == 0 else voxels
+    for j in range(voxels // block):
+        here = slice(j * block, (j + 1) * block)
+        new_ref[here, :] = (new_ref[here, :] + step * moves[batch + j * block:batch + (j + 1) * block]) * scale
+        copies.append(pltpu.make_async_copy(new_ref.at[here, :], new_hbm.at[here, :], sems.at[2 + j]))
+        copies[-1].start()
+    outer = dot3(turned_w, halves(change))
+    gram_ref[...] = (gram + step * (outer + outer.T)) * scale * column(scale)
+    copies.append(pltpu.make_async_copy(gram_ref, gram_hbm, sems.at[1]))
+    copies[-1].start()
     for copy in copies:
         copy.wait()
 

time: 51.7 us -> 50 us (0.967)
  Pallas kernels: 15.3 us -> 13.6 us
    pallas_call x1, Pallas kernels: 11.1 us -> 9.84 us  [shards(): pl.pallas_call(step_kernel, out_shape=tuple((jax.ShapeDtypeStruct(shape,...]
where the time goes in v4:
time: 50 us; the launch traced here: 49.8 us
  waiting for transfers between devices  20.5 us (41%)
  starting transfers between devices  14.1 us (28%)
  Pallas kernels  13.6 us (27%)
  between operations  1.4 us (3%)
    ppermute x10, waiting for transfers between devices, swap(): return lax.ppermute(x, 'vox', [(i, i ^ bit) for i in range(devices)])  18.1 us
    ppermute x10, starting transfers between devices, swap(): return lax.ppermute(x, 'vox', [(i, i ^ bit) for i in range(devices)])  12.6 us
    pallas_call x1, Pallas kernels, shards(): pl.pallas_call(step_kernel, out_shape=tuple((jax.ShapeDtypeStruct(shape,...  9.84 us
    pallas_call x1, Pallas kernels, shards(): pl.pallas_call(gram_kernel, out_shape=(part, part, jax.ShapeDtypeStruct((...  3.73 us
    ppermute x1, waiting for transfers between devices, all_reduce(): next_gram = lax.ppermute(gram, 'fold', [(i, i ^ 1) for i in range(folds)])  2.4 us
    ppermute x1, starting transfers between devices, all_reduce(): next_gram = lax.ppermute(gram, 'fold', [(i, i ^ 1) for i in range(folds)])  1.54 us
  transfers between devices with their start and end apart: 11, of which 8 were waited for; matrix products, arithmetic and copies ran while one was open for 0% of the time, Pallas kernels for 0%

profile of v4, /device:TPU:0, one launch (start us, length us, event | category | flops | bytes accessed | tf_op | source)
XLA Modules:
  0.0 49.8 jit_solution(10355465711719641611)
XLA Ops:
  1.3 3.7 %grams.1 = (f32[928,128]{1,0:T(8,128)S(1)}, f32[928,128]{1,0:T(8,128)S(1)}, f32[768,256]{1,0:T(8,128)S(1)}, f32[256,128]{1,0:T(8,128)S(1)}) custom-call(s32[1,256]{1,0:T(1,128)} %bitcast.3, s32[1,512]{1,0:T(1,128)} %bitcast.2, s32[1]{0:T(128)S(6)} %copy.14.held_ref, f32[512,768]{1,0:T(8,128)} %volumes_hbm.1, f32[768,512]{1,0:T(8,128)} %dict_ref.1), custom_call_target="tpu_custom_call" | custom-call | tf_op jit(solution)/shard_map/grams/pallas_call | solution.py:316
  5.0 0.5 %collective-permute-start = (f32[928,128]{1,0:T(8,128)S(1)}, f32[928,128]{1,0:T(8,128)S(1)}, u32[]{:S(2)}, u32[]{:S(2)}) collective-permute-start(f32[928,128]{1,0:T(8,128)S(1)} %get-tuple-element.12), channel_id=1, source_target_pairs={{0,1},{1,0},{2,3},{3,2},{4,5},{5,4},{6,7},{7,6},{8,9},{9,8},{10,11... | collective-permute-start | bytes 1425416 | tf_op jit(solution)/shard_map/ppermute | solution.py:276
  5.5 1.5 %collective-permute-done = f32[928,128]{1,0:T(8,128)S(1)} collective-permute-done((f32[928,128]{1,0:T(8,128)S(1)}, f32[928,128]{1,0:T(8,128)S(1)}, u32[]{:S(2)}, u32[]{:S(2)}) %collective-permute-start) | collective-permute-done | bytes 475168 | tf_op jit(solution)/shard_map/ppermute | solution.py:276
  7.1 0.0 copy-start
  7.1 3.0 %collective-permute-start.1 = (f32[232,128]{1,0:T(8,128)S(1)}, f32[232,128]{1,0:T(8,128)S(1)}, u32[]{:S(2)}, u32[]{:S(2)}) collective-permute-start(f32[232,128]{1,0:T(8,128)S(1)} %get-tuple-element.25), channel_id=1, source_target_pairs={{0,4},{1,5},{2,6},{3,7},{4,0},{5,1},{6,2},{7,3},{8,12},{9,13},{10,... | collective-permute-start | bytes 356360 | tf_op jit(solution)/shard_map/ppermute | solution.py:276
  10.1 1.5 %collective-permute-start.3 = (f32[232,128]{1,0:T(8,128)S(1)}, f32[232,128]{1,0:T(8,128)S(1)}, u32[]{:S(2)}, u32[]{:S(2)}) collective-permute-start(f32[232,128]{1,0:T(8,128)S(1)} %get-tuple-element.26), channel_id=1, source_target_pairs={{0,2},{1,3},{2,0},{3,1},{4,6},{5,7},{6,4},{7,5},{8,10},{9,11},{10,... | collective-permute-start | bytes 356360 | tf_op jit(solution)/shard_map/ppermute | solution.py:276
  11.6 0.1 collective-permute-start.2
  11.7 2.1 %collective-permute-done.1 = f32[232,128]{1,0:T(8,128)S(1)} collective-permute-done((f32[232,128]{1,0:T(8,128)S(1)}, f32[232,128]{1,0:T(8,128)S(1)}, u32[]{:S(2)}, u32[]{:S(2)}) %collective-permute-start.1) | collective-permute-done | bytes 118816 | tf_op jit(solution)/shard_map/ppermute | solution.py:276
  13.7 3.9 %collective-permute-done.3 = f32[232,128]{1,0:T(8,128)S(1)} collective-permute-done((f32[232,128]{1,0:T(8,128)S(1)}, f32[232,128]{1,0:T(8,128)S(1)}, u32[]{:S(2)}, u32[]{:S(2)}) %collective-permute-start.3) | collective-permute-done | bytes 118816 | tf_op jit(solution)/shard_map/ppermute | solution.py:276
  17.7 0.0 collective-permute-done.2
  17.7 3.3 %collective-permute-start.6 = (f32[160,128]{1,0:T(8,128)S(1)}, f32[160,128]{1,0:T(8,128)S(1)}, u32[]{:S(2)}, u32[]{:S(2)}) collective-permute-start(f32[160,128]{1,0:T(8,128)S(1)} %slice.47), channel_id=1, source_target_pairs={{0,12},{1,13},{2,14},{3,15},{4,8},{5,9},{6,10},{7,11},{8,4},{9,5},... | collective-permute-start | bytes 245768 | tf_op jit(solution)/shard_map/ppermute | solution.py:276
  21.0 0.6 %collective-permute-start.4 = (f32[72,128]{1,0:T(8,128)S(1)}, f32[72,128]{1,0:T(8,128)S(1)}, u32[]{:S(2)}, u32[]{:S(2)}) collective-permute-start(f32[72,128]{1,0:T(8,128)S(1)} %slice.46), channel_id=1, source_target_pairs={{0,12},{1,13},{2,14},{3,15},{4,8},{5,9},{6,10},{7,11},{8,4},{9,5},... | collective-permute-start | bytes 110600 | tf_op jit(solution)/shard_map/ppermute | solution.py:276
  21.6 5.2 %collective-permute-done.4 = f32[72,128]{1,0:T(8,128)S(1)} collective-permute-done((f32[72,128]{1,0:T(8,128)S(1)}, f32[72,128]{1,0:T(8,128)S(1)}, u32[]{:S(2)}, u32[]{:S(2)}) %collective-permute-start.4) | collective-permute-done | bytes 36896 | tf_op jit(solution)/shard_map/ppermute | solution.py:276
  26.8 1.5 %collective-permute-start.5 = (f32[72,128]{1,0:T(8,128)S(1)}, f32[72,128]{1,0:T(8,128)S(1)}, u32[]{:S(2)}, u32[]{:S(2)}) collective-permute-start(f32[72,128]{1,0:T(8,128)S(1)} %add.25), channel_id=1, source_target_pairs={{0,16},{16,0},{1,17},{17,1},{2,18},{18,2},{3,19},{19,3},{4,20},{20... | collective-permute-start | bytes 110600 | tf_op jit(solution)/shard_map/ppermute | solution.py:290
  28.3 0.0 collective-permute-done.6
  28.3 2.4 %collective-permute-done.5 = f32[72,128]{1,0:T(8,128)S(1)} collective-permute-done((f32[72,128]{1,0:T(8,128)S(1)}, f32[72,128]{1,0:T(8,128)S(1)}, u32[]{:S(2)}, u32[]{:S(2)}) %collective-permute-start.5) | collective-permute-done | bytes 36896 | tf_op jit(solution)/shard_map/ppermute | solution.py:290
  30.8 0.1 collective-permute-start.7
  30.9 0.8 %collective-permute-start.9 = (f32[296,128]{1,0:T(8,128)S(1)}, f32[296,128]{1,0:T(8,128)S(1)}, u32[]{:S(2)}, u32[]{:S(2)}) collective-permute-start(f32[296,128]{1,0:T(8,128)S(1)} %pad_maximum_fusion), channel_id=1, source_target_pairs={{0,2},{1,3},{2,0},{3,1},{4,6},{5,7},{6,4},{7,5},{8,10},{9,11},{10,... | collective-permute-start | bytes 454664 | tf_op jit(solution)/shard_map/ppermute | solution.py:276
  31.7 2.7 %collective-permute-start.8 = (f32[296,128]{1,0:T(8,128)S(1)}, f32[296,128]{1,0:T(8,128)S(1)}, u32[]{:S(2)}, u32[]{:S(2)}) collective-permute-start(f32[296,128]{1,0:T(8,128)S(1)} %pad_maximum_fusion), channel_id=1, source_target_pairs={{0,6},{1,7},{2,4},{3,5},{4,2},{5,3},{6,0},{7,1},{8,14},{9,15},{10,... | collective-permute-start | bytes 454664 | tf_op jit(solution)/shard_map/ppermute | solution.py:276
  34.4 1.7 %collective-permute-done.7 = f32[296,128]{1,0:T(8,128)S(1)} collective-permute-done((f32[296,128]{1,0:T(8,128)S(1)}, f32[296,128]{1,0:T(8,128)S(1)}, u32[]{:S(2)}, u32[]{:S(2)}) %collective-permute-start.7) | collective-permute-done | bytes 151584 | tf_op jit(solution)/shard_map/ppermute | solution.py:276
  36.1 1.8 %collective-permute-done.8 = f32[296,128]{1,0:T(8,128)S(1)} collective-permute-done((f32[296,128]{1,0:T(8,128)S(1)}, f32[296,128]{1,0:T(8,128)S(1)}, u32[]{:S(2)}, u32[]{:S(2)}) %collective-permute-start.8) | collective-permute-done | bytes 151584 | tf_op jit(solution)/shard_map/ppermute | solution.py:276
  37.9 0.0 collective-permute-done.9
  37.9 0.1 collective-permute-start.10
  38.0 2.0 %collective-permute-done.10.other_ref = f32[1184,128]{1,0:T(8,128)S(1)} collective-permute-done((f32[1184,128]{1,0:T(8,128)S(1)}, f32[1184,128]{1,0:T(8,128)S(1)}, u32[]{:S(2)}, u32[]{:S(2)}) %collective-permute-start.10) | collective-permute-done | bytes 606240 | tf_op jit(solution)/shard_map/ppermute | solution.py:276
  40.0 0.0 copy-done
  40.0 9.8 %step.1 = (f32[768,512]{1,0:T(8,128)}, f32[256,512]{1,0:T(8,128)}, f32[512,512]{1,0:T(8,128)}) custom-call(f32[1184,128]{1,0:T(8,128)S(1)} %constant_dynamic-update-slice_fusion.mine_ref, f32[1184,128]{1,0:T(8,128)S(1)} %collective-permute-done.10.other_ref, f32[768,256]{1,0:T(8,128)S(1)} %get-tuple-element.17.flipped_ref, ...), custom_call_target="tpu_custom_call" | custom-call | tf_op jit(solution)/shard_map/step/pallas_call | solution.py:330
  (15 shorter events, 0.2 us)
Async XLA Ops:
  5.0 2.0 %collective-permute-start = (f32[928,128]{1,0:T(8,128)S(1)}, f32[928,128]{1,0:T(8,128)S(1)}, u32[]{:S(2)}, u32[]{:S(2)}) collective-permute-start(f32[928,128]{1,0:T(8,128)S(1)} %get-tuple-element.12), channel_id=1, source_target_pairs={{0,1},{1,0},{2,3},{3,2},{4,5},{5,4},{6,7},{7,6},{8,9},{9,8},{10,11... | collective-permute-start | bytes 1425416 | tf_op jit(solution)/shard_map/ppermute | solution.py:276
  7.1 32.9 %copy-start = (f32[768,512]{1,0:T(8,128)S(1)}, f32[768,512]{1,0:T(8,128)}, u32[]{:S(2)}) copy-start(f32[768,512]{1,0:T(8,128)} %dict_ref.1) | copy-start | bytes 4718596
  7.1 6.6 %collective-permute-start.1 = (f32[232,128]{1,0:T(8,128)S(1)}, f32[232,128]{1,0:T(8,128)S(1)}, u32[]{:S(2)}, u32[]{:S(2)}) collective-permute-start(f32[232,128]{1,0:T(8,128)S(1)} %get-tuple-element.25), channel_id=1, source_target_pairs={{0,4},{1,5},{2,6},{3,7},{4,0},{5,1},{6,2},{7,3},{8,12},{9,13},{10,... | collective-permute-start | bytes 356360 | tf_op jit(solution)/shard_map/ppermute | solution.py:276
  10.1 7.5 %collective-permute-start.3 = (f32[232,128]{1,0:T(8,128)S(1)}, f32[232,128]{1,0:T(8,128)S(1)}, u32[]{:S(2)}, u32[]{:S(2)}) collective-permute-start(f32[232,128]{1,0:T(8,128)S(1)} %get-tuple-element.26), channel_id=1, source_target_pairs={{0,2},{1,3},{2,0},{3,1},{4,6},{5,7},{6,4},{7,5},{8,10},{9,11},{10,... | collective-permute-start | bytes 356360 | tf_op jit(solution)/shard_map/ppermute | solution.py:276
  11.6 6.1 %collective-permute-start.2 = (f32[232,128]{1,0:T(8,128)S(1)}, f32[232,128]{1,0:T(8,128)S(1)}, u32[]{:S(2)}, u32[]{:S(2)}) collective-permute-start(f32[232,128]{1,0:T(8,128)S(1)} %get-tuple-element.27), channel_id=1, source_target_pairs={{0,6},{1,7},{2,4},{3,5},{4,2},{5,3},{6,0},{7,1},{8,14},{9,15},{10,... | collective-permute-start | bytes 356360 | tf_op jit(solution)/shard_map/ppermute | solution.py:276
  17.7 10.6 %collective-permute-start.6 = (f32[160,128]{1,0:T(8,128)S(1)}, f32[160,128]{1,0:T(8,128)S(1)}, u32[]{:S(2)}, u32[]{:S(2)}) collective-permute-start(f32[160,128]{1,0:T(8,128)S(1)} %slice.47), channel_id=1, source_target_pairs={{0,12},{1,13},{2,14},{3,15},{4,8},{5,9},{6,10},{7,11},{8,4},{9,5},... | collective-permute-start | bytes 245768 | tf_op jit(solution)/shard_map/ppermute | solution.py:276
  21.0 5.8 %collective-permute-start.4 = (f32[72,128]{1,0:T(8,128)S(1)}, f32[72,128]{1,0:T(8,128)S(1)}, u32[]{:S(2)}, u32[]{:S(2)}) collective-permute-start(f32[72,128]{1,0:T(8,128)S(1)} %slice.46), channel_id=1, source_target_pairs={{0,12},{1,13},{2,14},{3,15},{4,8},{5,9},{6,10},{7,11},{8,4},{9,5},... | collective-permute-start | bytes 110600 | tf_op jit(solution)/shard_map/ppermute | solution.py:276
  26.8 4.0 %collective-permute-start.5 = (f32[72,128]{1,0:T(8,128)S(1)}, f32[72,128]{1,0:T(8,128)S(1)}, u32[]{:S(2)}, u32[]{:S(2)}) collective-permute-start(f32[72,128]{1,0:T(8,128)S(1)} %add.25), channel_id=1, source_target_pairs={{0,16},{16,0},{1,17},{17,1},{2,18},{18,2},{3,19},{19,3},{4,20},{20... | collective-permute-start | bytes 110600 | tf_op jit(solution)/shard_map/ppermute | solution.py:290
  30.8 5.3 %collective-permute-start.7 = (f32[296,128]{1,0:T(8,128)S(1)}, f32[296,128]{1,0:T(8,128)S(1)}, u32[]{:S(2)}, u32[]{:S(2)}) collective-permute-start(f32[296,128]{1,0:T(8,128)S(1)} %pad_maximum_fusion), channel_id=1, source_target_pairs={{0,4},{1,5},{2,6},{3,7},{4,0},{5,1},{6,2},{7,3},{8,12},{9,13},{10,... | collective-permute-start | bytes 454664 | tf_op jit(solution)/shard_map/ppermute | solution.py:276
  30.9 7.0 %collective-permute-start.9 = (f32[296,128]{1,0:T(8,128)S(1)}, f32[296,128]{1,0:T(8,128)S(1)}, u32[]{:S(2)}, u32[]{:S(2)}) collective-permute-start(f32[296,128]{1,0:T(8,128)S(1)} %pad_maximum_fusion), channel_id=1, source_target_pairs={{0,2},{1,3},{2,0},{3,1},{4,6},{5,7},{6,4},{7,5},{8,10},{9,11},{10,... | collective-permute-start | bytes 454664 | tf_op jit(solution)/shard_map/ppermute | solution.py:276
  31.7 6.2 %collective-permute-start.8 = (f32[296,128]{1,0:T(8,128)S(1)}, f32[296,128]{1,0:T(8,128)S(1)}, u32[]{:S(2)}, u32[]{:S(2)}) collective-permute-start(f32[296,128]{1,0:T(8,128)S(1)} %pad_maximum_fusion), channel_id=1, source_target_pairs={{0,6},{1,7},{2,4},{3,5},{4,2},{5,3},{6,0},{7,1},{8,14},{9,15},{10,... | collective-permute-start | bytes 454664 | tf_op jit(solution)/shard_map/ppermute | solution.py:276
  37.9 2.1 %collective-permute-start.10 = (f32[1184,128]{1,0:T(8,128)S(1)}, f32[1184,128]{1,0:T(8,128)S(1)}, u32[]{:S(2)}, u32[]{:S(2)}) collective-permute-start(f32[1184,128]{1,0:T(8,128)S(1)} %constant_dynamic-update-slice_fusion.mine_ref), channel_id=1, source_target_pairs={{0,1},{1,0},{2,3},{3,2},{4,5},{5,4},{6,7},{7,6},{8,9},{9,8},{10,11... | collective-permute-start | bytes 1818632 | tf_op jit(solution)/shard_map/ppermute | solution.py:276

commit v5 on v4

--- a/solution.py
+++ b/solution.py
@@ -281,19 +281,22 @@
     got = [swap(total[(k + 1) * slot:(k + 2) * slot], bit) for k, bit in enumerate(SQUARE)]
     for part in got:
         own = own + part
-    gram, rest = own[:gram_rows + SPARE], own[gram_rows + SPARE:]
-    gram, rest = lax.optimization_barrier((gram, rest))
+    head = gram_rows + SPARE
+    cut = max(head, -(-own.shape[0] // 16) * 8)
+    gram, rest = lax.optimization_barrier((own[:cut], own[cut:]))
     for k in range(BITS, devices.bit_length() - 1):
         bit = 3 << (k - 1) if k == BITS else 1 << k
-        other = swap(rest, bit), swap(gram, bit)
-        gram, rest = gram + other[1], rest + other[0]
-    next_gram = lax.ppermute(gram, "fold", [(i, i ^ 1) for i in range(folds)])
+        other = swap(gram, bit), swap(rest, bit)
+        gram, rest = gram + other[0], rest + other[1]
+    next_gram = lax.ppermute(gram[:head], "fold", [(i, i ^ 1) for i in range(folds)])
     next_gram, rest = lax.optimization_barrier((next_gram, rest))
     even = lax.axis_index("fold") & 1 == 0
     first = jnp.where(even, gram[:gram_rows], next_gram[:gram_rows])
     second = jnp.where(even, next_gram[:gram_rows], gram[:gram_rows])
-    own = jnp.concatenate([first, second, gram[gram_rows:] + next_gram[gram_rows:], rest])
-    mine = jnp.concatenate([own] + [swap(own, bit) for bit in SQUARE])
+    own = jnp.concatenate([first, second, gram[gram_rows:head] + next_gram[gram_rows:], gram[head:], rest])
+    ahead, across, along = (swap(own, bit) for bit in SQUARE)
+    across, along, ahead = lax.optimization_barrier((across, along, ahead))
+    mine = jnp.concatenate([own, ahead, across, along])
     return mine, swap(mine, 1)
 
 

time: 50 us -> 48.3 us (0.966)
  waiting for transfers between devices: 20.5 us -> 18.7 us
    ppermute x1, waiting for transfers between devices: 2.4 us -> 0.85 us  [all_reduce(): lax.ppermute(gram[:head], 'fold', [(i, i ^ 1) for i in range(folds)])]
  transfers between devices with their start and end apart: 11 -> 11, of which waited for: 8 -> 10; matrix products, arithmetic and copies ran while one was open for 0% -> 0% of each run, Pallas kernels for 0% -> 0%
where the time goes in v5:
time: 48.3 us; the launch traced here: 48.1 us
  waiting for transfers between devices  18.7 us (39%)
  starting transfers between devices  14.2 us (29%)
  Pallas kernels  13.6 us (28%)
  between operations  1.41 us (3%)
    ppermute x10, waiting for transfers between devices, swap(): return lax.ppermute(x, 'vox', [(i, i ^ bit) for i in range(devices)])  17.9 us
    ppermute x10, starting transfers between devices, swap(): return lax.ppermute(x, 'vox', [(i, i ^ bit) for i in range(devices)])  12.6 us
    pallas_call x1, Pallas kernels, shards(): pl.pallas_call(step_kernel, out_shape=tuple((jax.ShapeDtypeStruct(shape,...  9.85 us
    pallas_call x1, Pallas kernels, shards(): pl.pallas_call(gram_kernel, out_shape=(part, part, jax.ShapeDtypeStruct((...  3.73 us
    ppermute x1, starting transfers between devices, all_reduce(): lax.ppermute(gram[:head], 'fold', [(i, i ^ 1) for i in range(folds)])  1.6 us
  transfers between devices with their start and end apart: 11, of which 10 were waited for; matrix products, arithmetic and copies ran while one was open for 0% of the time, Pallas kernels for 0%

profile of v5, /device:TPU:0, one launch (start us, length us, event | category | flops | bytes accessed | tf_op | source)
XLA Modules:
  0.0 48.1 jit_solution(7440596237974987427)
XLA Ops:
  1.3 3.7 %grams.1 = (f32[928,128]{1,0:T(8,128)S(1)}, f32[928,128]{1,0:T(8,128)S(1)}, f32[768,256]{1,0:T(8,128)S(1)}, f32[256,128]{1,0:T(8,128)S(1)}) custom-call(s32[1,256]{1,0:T(1,128)} %bitcast.3, s32[1,512]{1,0:T(1,128)} %bitcast.2, s32[1]{0:T(128)S(6)} %copy.19.held_ref, f32[512,768]{1,0:T(8,128)} %volumes_hbm.1, f32[768,512]{1,0:T(8,128)} %dict_ref.1), custom_call_target="tpu_custom_call" | custom-call | tf_op jit(solution)/shard_map/grams/pallas_call | solution.py:319
  5.0 0.5 %collective-permute-start = (f32[928,128]{1,0:T(8,128)S(1)}, f32[928,128]{1,0:T(8,128)S(1)}, u32[]{:S(2)}, u32[]{:S(2)}) collective-permute-start(f32[928,128]{1,0:T(8,128)S(1)} %get-tuple-element.15), channel_id=1, source_target_pairs={{0,1},{1,0},{2,3},{3,2},{4,5},{5,4},{6,7},{7,6},{8,9},{9,8},{10,11... | collective-permute-start | bytes 1425416 | tf_op jit(solution)/shard_map/ppermute | solution.py:276
  5.5 1.5 %collective-permute-done = f32[928,128]{1,0:T(8,128)S(1)} collective-permute-done((f32[928,128]{1,0:T(8,128)S(1)}, f32[928,128]{1,0:T(8,128)S(1)}, u32[]{:S(2)}, u32[]{:S(2)}) %collective-permute-start) | collective-permute-done | bytes 475168 | tf_op jit(solution)/shard_map/ppermute | solution.py:276
  7.0 0.0 copy-start
  7.1 3.0 %collective-permute-start.1 = (f32[232,128]{1,0:T(8,128)S(1)}, f32[232,128]{1,0:T(8,128)S(1)}, u32[]{:S(2)}, u32[]{:S(2)}) collective-permute-start(f32[232,128]{1,0:T(8,128)S(1)} %get-tuple-element.25), channel_id=1, source_target_pairs={{0,4},{1,5},{2,6},{3,7},{4,0},{5,1},{6,2},{7,3},{8,12},{9,13},{10,... | collective-permute-start | bytes 356360 | tf_op jit(solution)/shard_map/ppermute | solution.py:276
  10.1 1.5 %collective-permute-start.3 = (f32[232,128]{1,0:T(8,128)S(1)}, f32[232,128]{1,0:T(8,128)S(1)}, u32[]{:S(2)}, u32[]{:S(2)}) collective-permute-start(f32[232,128]{1,0:T(8,128)S(1)} %get-tuple-element.26), channel_id=1, source_target_pairs={{0,2},{1,3},{2,0},{3,1},{4,6},{5,7},{6,4},{7,5},{8,10},{9,11},{10,... | collective-permute-start | bytes 356360 | tf_op jit(solution)/shard_map/ppermute | solution.py:276
  11.6 0.1 collective-permute-start.2
  11.7 2.1 %collective-permute-done.1 = f32[232,128]{1,0:T(8,128)S(1)} collective-permute-done((f32[232,128]{1,0:T(8,128)S(1)}, f32[232,128]{1,0:T(8,128)S(1)}, u32[]{:S(2)}, u32[]{:S(2)}) %collective-permute-start.1) | collective-permute-done | bytes 118816 | tf_op jit(solution)/shard_map/ppermute | solution.py:276
  13.7 3.9 %collective-permute-done.3 = f32[232,128]{1,0:T(8,128)S(1)} collective-permute-done((f32[232,128]{1,0:T(8,128)S(1)}, f32[232,128]{1,0:T(8,128)S(1)}, u32[]{:S(2)}, u32[]{:S(2)}) %collective-permute-start.3) | collective-permute-done | bytes 118816 | tf_op jit(solution)/shard_map/ppermute | solution.py:276
  17.7 0.0 collective-permute-done.2
  17.7 3.3 %collective-permute-start.4 = (f32[120,128]{1,0:T(8,128)S(1)}, f32[120,128]{1,0:T(8,128)S(1)}, u32[]{:S(2)}, u32[]{:S(2)}) collective-permute-start(f32[120,128]{1,0:T(8,128)S(1)} %slice.54), channel_id=1, source_target_pairs={{0,12},{1,13},{2,14},{3,15},{4,8},{5,9},{6,10},{7,11},{8,4},{9,5},... | collective-permute-start | bytes 184328 | tf_op jit(solution)/shard_map/ppermute | solution.py:276
  21.0 0.6 %collective-permute-start.6 = (f32[112,128]{1,0:T(8,128)S(1)}, f32[112,128]{1,0:T(8,128)S(1)}, u32[]{:S(2)}, u32[]{:S(2)}) collective-permute-start(f32[112,128]{1,0:T(8,128)S(1)} %slice.55), channel_id=1, source_target_pairs={{0,12},{1,13},{2,14},{3,15},{4,8},{5,9},{6,10},{7,11},{8,4},{9,5},... | collective-permute-start | bytes 172040 | tf_op jit(solution)/shard_map/ppermute | solution.py:276
  21.6 2.2 %collective-permute-done.4 = f32[120,128]{1,0:T(8,128)S(1)} collective-permute-done((f32[120,128]{1,0:T(8,128)S(1)}, f32[120,128]{1,0:T(8,128)S(1)}, u32[]{:S(2)}, u32[]{:S(2)}) %collective-permute-start.4) | collective-permute-done | bytes 61472 | tf_op jit(solution)/shard_map/ppermute | solution.py:276
  23.8 1.6 %collective-permute-start.5 = (f32[72,128]{1,0:T(8,128)S(1)}, f32[72,128]{1,0:T(8,128)S(1)}, u32[]{:S(2)}, u32[]{:S(2)}) collective-permute-start(f32[72,128]{1,0:T(8,128)S(1)} %slice.57), channel_id=1, source_target_pairs={{0,16},{16,0},{1,17},{17,1},{2,18},{18,2},{3,19},{19,3},{4,20},{20... | collective-permute-start | bytes 110600 | tf_op jit(solution)/shard_map/ppermute | solution.py:291
  25.4 1.6 %collective-permute-done.6 = f32[112,128]{1,0:T(8,128)S(1)} collective-permute-done((f32[112,128]{1,0:T(8,128)S(1)}, f32[112,128]{1,0:T(8,128)S(1)}, u32[]{:S(2)}, u32[]{:S(2)}) %collective-permute-start.6) | collective-permute-done | bytes 57376 | tf_op jit(solution)/shard_map/ppermute | solution.py:276
  27.0 0.9 %collective-permute-done.5 = f32[72,128]{1,0:T(8,128)S(1)} collective-permute-done((f32[72,128]{1,0:T(8,128)S(1)}, f32[72,128]{1,0:T(8,128)S(1)}, u32[]{:S(2)}, u32[]{:S(2)}) %collective-permute-start.5) | collective-permute-done | bytes 36896 | tf_op jit(solution)/shard_map/ppermute | solution.py:291
  27.9 1.4 %collective-permute-start.9 = (f32[296,128]{1,0:T(8,128)S(1)}, f32[296,128]{1,0:T(8,128)S(1)}, u32[]{:S(2)}, u32[]{:S(2)}) collective-permute-start(f32[296,128]{1,0:T(8,128)S(1)} %get-tuple-element.36), channel_id=1, source_target_pairs={{0,4},{1,5},{2,6},{3,7},{4,0},{5,1},{6,2},{7,3},{8,12},{9,13},{10,... | collective-permute-start | bytes 454664 | tf_op jit(solution)/shard_map/ppermute | solution.py:276
  29.3 0.6 %collective-permute-start.8 = (f32[296,128]{1,0:T(8,128)S(1)}, f32[296,128]{1,0:T(8,128)S(1)}, u32[]{:S(2)}, u32[]{:S(2)}) collective-permute-start(f32[296,128]{1,0:T(8,128)S(1)} %get-tuple-element.36), channel_id=1, source_target_pairs={{0,2},{1,3},{2,0},{3,1},{4,6},{5,7},{6,4},{7,5},{8,10},{9,11},{10,... | collective-permute-start | bytes 454664 | tf_op jit(solution)/shard_map/ppermute | solution.py:276
  29.9 1.6 %collective-permute-start.7 = (f32[296,128]{1,0:T(8,128)S(1)}, f32[296,128]{1,0:T(8,128)S(1)}, u32[]{:S(2)}, u32[]{:S(2)}) collective-permute-start(f32[296,128]{1,0:T(8,128)S(1)} %get-tuple-element.36), channel_id=1, source_target_pairs={{0,6},{1,7},{2,4},{3,5},{4,2},{5,3},{6,0},{7,1},{8,14},{9,15},{10,... | collective-permute-start | bytes 454664 | tf_op jit(solution)/shard_map/ppermute | solution.py:276
  31.5 1.7 %collective-permute-done.9 = f32[296,128]{1,0:T(8,128)S(1)} collective-permute-done((f32[296,128]{1,0:T(8,128)S(1)}, f32[296,128]{1,0:T(8,128)S(1)}, u32[]{:S(2)}, u32[]{:S(2)}) %collective-permute-start.9) | collective-permute-done | bytes 151584 | tf_op jit(solution)/shard_map/ppermute | solution.py:276
  33.2 1.3 %collective-permute-done.8 = f32[296,128]{1,0:T(8,128)S(1)} collective-permute-done((f32[296,128]{1,0:T(8,128)S(1)}, f32[296,128]{1,0:T(8,128)S(1)}, u32[]{:S(2)}, u32[]{:S(2)}) %collective-permute-start.8) | collective-permute-done | bytes 151584 | tf_op jit(solution)/shard_map/ppermute | solution.py:276
  34.5 1.6 %collective-permute-done.7 = f32[296,128]{1,0:T(8,128)S(1)} collective-permute-done((f32[296,128]{1,0:T(8,128)S(1)}, f32[296,128]{1,0:T(8,128)S(1)}, u32[]{:S(2)}, u32[]{:S(2)}) %collective-permute-start.7) | collective-permute-done | bytes 151584 | tf_op jit(solution)/shard_map/ppermute | solution.py:276
  36.2 0.1 collective-permute-start.10
  36.3 2.0 %collective-permute-done.10.other_ref = f32[1184,128]{1,0:T(8,128)S(1)} collective-permute-done((f32[1184,128]{1,0:T(8,128)S(1)}, f32[1184,128]{1,0:T(8,128)S(1)}, u32[]{:S(2)}, u32[]{:S(2)}) %collective-permute-start.10) | collective-permute-done | bytes 606240 | tf_op jit(solution)/shard_map/ppermute | solution.py:276
  38.3 0.0 copy-done
  38.3 9.8 %step.1 = (f32[768,512]{1,0:T(8,128)}, f32[256,512]{1,0:T(8,128)}, f32[512,512]{1,0:T(8,128)}) custom-call(f32[1184,128]{1,0:T(8,128)S(1)} %constant_dynamic-update-slice_fusion.5.mine_ref, f32[1184,128]{1,0:T(8,128)S(1)} %collective-permute-done.10.other_ref, f32[768,256]{1,0:T(8,128)S(1)} %get-tuple-element.23.flipped_ref, ...), custom_call_target="tpu_custom_call" | custom-call | tf_op jit(solution)/shard_map/step/pallas_call | solution.py:333
  (16 shorter events, 0.2 us)
Async XLA Ops:
  5.0 2.0 %collective-permute-start = (f32[928,128]{1,0:T(8,128)S(1)}, f32[928,128]{1,0:T(8,128)S(1)}, u32[]{:S(2)}, u32[]{:S(2)}) collective-permute-start(f32[928,128]{1,0:T(8,128)S(1)} %get-tuple-element.15), channel_id=1, source_target_pairs={{0,1},{1,0},{2,3},{3,2},{4,5},{5,4},{6,7},{7,6},{8,9},{9,8},{10,11... | collective-permute-start | bytes 1425416 | tf_op jit(solution)/shard_map/ppermute | solution.py:276
  7.0 31.2 %copy-start = (f32[768,512]{1,0:T(8,128)S(1)}, f32[768,512]{1,0:T(8,128)}, u32[]{:S(2)}) copy-start(f32[768,512]{1,0:T(8,128)} %dict_ref.1) | copy-start | bytes 4718596
  7.1 6.6 %collective-permute-start.1 = (f32[232,128]{1,0:T(8,128)S(1)}, f32[232,128]{1,0:T(8,128)S(1)}, u32[]{:S(2)}, u32[]{:S(2)}) collective-permute-start(f32[232,128]{1,0:T(8,128)S(1)} %get-tuple-element.25), channel_id=1, source_target_pairs={{0,4},{1,5},{2,6},{3,7},{4,0},{5,1},{6,2},{7,3},{8,12},{9,13},{10,... | collective-permute-start | bytes 356360 | tf_op jit(solution)/shard_map/ppermute | solution.py:276
  10.1 7.5 %collective-permute-start.3 = (f32[232,128]{1,0:T(8,128)S(1)}, f32[232,128]{1,0:T(8,128)S(1)}, u32[]{:S(2)}, u32[]{:S(2)}) collective-permute-start(f32[232,128]{1,0:T(8,128)S(1)} %get-tuple-element.26), channel_id=1, source_target_pairs={{0,2},{1,3},{2,0},{3,1},{4,6},{5,7},{6,4},{7,5},{8,10},{9,11},{10,... | collective-permute-start | bytes 356360 | tf_op jit(solution)/shard_map/ppermute | solution.py:276
  11.6 6.1 %collective-permute-start.2 = (f32[232,128]{1,0:T(8,128)S(1)}, f32[232,128]{1,0:T(8,128)S(1)}, u32[]{:S(2)}, u32[]{:S(2)}) collective-permute-start(f32[232,128]{1,0:T(8,128)S(1)} %get-tuple-element.27), channel_id=1, source_target_pairs={{0,6},{1,7},{2,4},{3,5},{4,2},{5,3},{6,0},{7,1},{8,14},{9,15},{10,... | collective-permute-start | bytes 356360 | tf_op jit(solution)/shard_map/ppermute | solution.py:276
  17.7 6.1 %collective-permute-start.4 = (f32[120,128]{1,0:T(8,128)S(1)}, f32[120,128]{1,0:T(8,128)S(1)}, u32[]{:S(2)}, u32[]{:S(2)}) collective-permute-start(f32[120,128]{1,0:T(8,128)S(1)} %slice.54), channel_id=1, source_target_pairs={{0,12},{1,13},{2,14},{3,15},{4,8},{5,9},{6,10},{7,11},{8,4},{9,5},... | collective-permute-start | bytes 184328 | tf_op jit(solution)/shard_map/ppermute | solution.py:276
  21.0 6.0 %collective-permute-start.6 = (f32[112,128]{1,0:T(8,128)S(1)}, f32[112,128]{1,0:T(8,128)S(1)}, u32[]{:S(2)}, u32[]{:S(2)}) collective-permute-start(f32[112,128]{1,0:T(8,128)S(1)} %slice.55), channel_id=1, source_target_pairs={{0,12},{1,13},{2,14},{3,15},{4,8},{5,9},{6,10},{7,11},{8,4},{9,5},... | collective-permute-start | bytes 172040 | tf_op jit(solution)/shard_map/ppermute | solution.py:276
  23.8 4.0 %collective-permute-start.5 = (f32[72,128]{1,0:T(8,128)S(1)}, f32[72,128]{1,0:T(8,128)S(1)}, u32[]{:S(2)}, u32[]{:S(2)}) collective-permute-start(f32[72,128]{1,0:T(8,128)S(1)} %slice.57), channel_id=1, source_target_pairs={{0,16},{16,0},{1,17},{17,1},{2,18},{18,2},{3,19},{19,3},{4,20},{20... | collective-permute-start | bytes 110600 | tf_op jit(solution)/shard_map/ppermute | solution.py:291
  27.9 5.3 %collective-permute-start.9 = (f32[296,128]{1,0:T(8,128)S(1)}, f32[296,128]{1,0:T(8,128)S(1)}, u32[]{:S(2)}, u32[]{:S(2)}) collective-permute-start(f32[296,128]{1,0:T(8,128)S(1)} %get-tuple-element.36), channel_id=1, source_target_pairs={{0,4},{1,5},{2,6},{3,7},{4,0},{5,1},{6,2},{7,3},{8,12},{9,13},{10,... | collective-permute-start | bytes 454664 | tf_op jit(solution)/shard_map/ppermute | solution.py:276
  29.3 5.2 %collective-permute-start.8 = (f32[296,128]{1,0:T(8,128)S(1)}, f32[296,128]{1,0:T(8,128)S(1)}, u32[]{:S(2)}, u32[]{:S(2)}) collective-permute-start(f32[296,128]{1,0:T(8,128)S(1)} %get-tuple-element.36), channel_id=1, source_target_pairs={{0,2},{1,3},{2,0},{3,1},{4,6},{5,7},{6,4},{7,5},{8,10},{9,11},{10,... | collective-permute-start | bytes 454664 | tf_op jit(solution)/shard_map/ppermute | solution.py:276
  29.9 6.2 %collective-permute-start.7 = (f32[296,128]{1,0:T(8,128)S(1)}, f32[296,128]{1,0:T(8,128)S(1)}, u32[]{:S(2)}, u32[]{:S(2)}) collective-permute-start(f32[296,128]{1,0:T(8,128)S(1)} %get-tuple-element.36), channel_id=1, source_target_pairs={{0,6},{1,7},{2,4},{3,5},{4,2},{5,3},{6,0},{7,1},{8,14},{9,15},{10,... | collective-permute-start | bytes 454664 | tf_op jit(solution)/shard_map/ppermute | solution.py:276
  36.2 2.1 %collective-permute-start.10 = (f32[1184,128]{1,0:T(8,128)S(1)}, f32[1184,128]{1,0:T(8,128)S(1)}, u32[]{:S(2)}, u32[]{:S(2)}) collective-permute-start(f32[1184,128]{1,0:T(8,128)S(1)} %constant_dynamic-update-slice_fusion.5.mine_ref), channel_id=1, source_target_pairs={{0,1},{1,0},{2,3},{3,2},{4,5},{5,4},{6,7},{7,6},{8,9},{9,8},{10,11... | collective-permute-start | bytes 1818632 | tf_op jit(solution)/shard_map/ppermute | solution.py:276

commit v6 on v5

--- a/solution.py
+++ b/solution.py
@@ -282,7 +282,7 @@
     for part in got:
         own = own + part
     head = gram_rows + SPARE
-    cut = max(head, -(-own.shape[0] // 16) * 8)
+    cut = head + 2 * SPARE
     gram, rest = lax.optimization_barrier((own[:cut], own[cut:]))
     for k in range(BITS, devices.bit_length() - 1):
         bit = 3 << (k - 1) if k == BITS else 1 << k

time: 48.3 us -> 47.9 us (level)
  no operation moved by 1% of the time
where the time goes in v6:
time: 47.9 us; the launch traced here: 47.7 us
  waiting for transfers between devices  18.3 us (38%)
  starting transfers between devices  14.2 us (30%)
  Pallas kernels  13.6 us (28%)
  between operations  1.4 us (3%)
    ppermute x10, waiting for transfers between devices, swap(): return lax.ppermute(x, 'vox', [(i, i ^ bit) for i in range(devices)])  17.8 us
    ppermute x10, starting transfers between devices, swap(): return lax.ppermute(x, 'vox', [(i, i ^ bit) for i in range(devices)])  12.6 us
    pallas_call x1, Pallas kernels, shards(): pl.pallas_call(step_kernel, out_shape=tuple((jax.ShapeDtypeStruct(shape,...  9.85 us
    pallas_call x1, Pallas kernels, shards(): pl.pallas_call(gram_kernel, out_shape=(part, part, jax.ShapeDtypeStruct((...  3.73 us
    ppermute x1, starting transfers between devices, all_reduce(): lax.ppermute(gram[:head], 'fold', [(i, i ^ 1) for i in range(folds)])  1.6 us
  transfers between devices with their start and end apart: 11, of which 10 were waited for; matrix products, arithmetic and copies ran while one was open for 0% of the time, Pallas kernels for 0%

profile of v6, /device:TPU:0, one launch (start us, length us, event | category | flops | bytes accessed | tf_op | source)
XLA Modules:
  0.0 47.7 jit_solution(8961002628708387063)
XLA Ops:
  1.3 3.7 %grams.1 = (f32[928,128]{1,0:T(8,128)S(1)}, f32[928,128]{1,0:T(8,128)S(1)}, f32[768,256]{1,0:T(8,128)S(1)}, f32[256,128]{1,0:T(8,128)S(1)}) custom-call(s32[1,256]{1,0:T(1,128)} %bitcast.3, s32[1,512]{1,0:T(1,128)} %bitcast.2, s32[1]{0:T(128)S(6)} %copy.19.held_ref, f32[512,768]{1,0:T(8,128)} %volumes_hbm.1, f32[768,512]{1,0:T(8,128)} %dict_ref.1), custom_call_target="tpu_custom_call" | custom-call | tf_op jit(solution)/shard_map/grams/pallas_call | solution.py:319
  5.0 0.5 %collective-permute-start = (f32[928,128]{1,0:T(8,128)S(1)}, f32[928,128]{1,0:T(8,128)S(1)}, u32[]{:S(2)}, u32[]{:S(2)}) collective-permute-start(f32[928,128]{1,0:T(8,128)S(1)} %get-tuple-element.15), channel_id=1, source_target_pairs={{0,1},{1,0},{2,3},{3,2},{4,5},{5,4},{6,7},{7,6},{8,9},{9,8},{10,11... | collective-permute-start | bytes 1425416 | tf_op jit(solution)/shard_map/ppermute | solution.py:276
  5.5 1.5 %collective-permute-done = f32[928,128]{1,0:T(8,128)S(1)} collective-permute-done((f32[928,128]{1,0:T(8,128)S(1)}, f32[928,128]{1,0:T(8,128)S(1)}, u32[]{:S(2)}, u32[]{:S(2)}) %collective-permute-start) | collective-permute-done | bytes 475168 | tf_op jit(solution)/shard_map/ppermute | solution.py:276
  7.0 0.0 copy-start
  7.1 3.0 %collective-permute-start.1 = (f32[232,128]{1,0:T(8,128)S(1)}, f32[232,128]{1,0:T(8,128)S(1)}, u32[]{:S(2)}, u32[]{:S(2)}) collective-permute-start(f32[232,128]{1,0:T(8,128)S(1)} %get-tuple-element.25), channel_id=1, source_target_pairs={{0,4},{1,5},{2,6},{3,7},{4,0},{5,1},{6,2},{7,3},{8,12},{9,13},{10,... | collective-permute-start | bytes 356360 | tf_op jit(solution)/shard_map/ppermute | solution.py:276
  10.1 1.5 %collective-permute-start.3 = (f32[232,128]{1,0:T(8,128)S(1)}, f32[232,128]{1,0:T(8,128)S(1)}, u32[]{:S(2)}, u32[]{:S(2)}) collective-permute-start(f32[232,128]{1,0:T(8,128)S(1)} %get-tuple-element.26), channel_id=1, source_target_pairs={{0,2},{1,3},{2,0},{3,1},{4,6},{5,7},{6,4},{7,5},{8,10},{9,11},{10,... | collective-permute-start | bytes 356360 | tf_op jit(solution)/shard_map/ppermute | solution.py:276
  11.6 0.1 collective-permute-start.2
  11.7 2.1 %collective-permute-done.1 = f32[232,128]{1,0:T(8,128)S(1)} collective-permute-done((f32[232,128]{1,0:T(8,128)S(1)}, f32[232,128]{1,0:T(8,128)S(1)}, u32[]{:S(2)}, u32[]{:S(2)}) %collective-permute-start.1) | collective-permute-done | bytes 118816 | tf_op jit(solution)/shard_map/ppermute | solution.py:276
  13.7 3.9 %collective-permute-done.3 = f32[232,128]{1,0:T(8,128)S(1)} collective-permute-done((f32[232,128]{1,0:T(8,128)S(1)}, f32[232,128]{1,0:T(8,128)S(1)}, u32[]{:S(2)}, u32[]{:S(2)}) %collective-permute-start.3) | collective-permute-done | bytes 118816 | tf_op jit(solution)/shard_map/ppermute | solution.py:276
  17.7 0.0 collective-permute-done.2
  17.7 3.3 %collective-permute-start.4 = (f32[88,128]{1,0:T(8,128)S(1)}, f32[88,128]{1,0:T(8,128)S(1)}, u32[]{:S(2)}, u32[]{:S(2)}) collective-permute-start(f32[88,128]{1,0:T(8,128)S(1)} %slice.54), channel_id=1, source_target_pairs={{0,12},{1,13},{2,14},{3,15},{4,8},{5,9},{6,10},{7,11},{8,4},{9,5},... | collective-permute-start | bytes 135176 | tf_op jit(solution)/shard_map/ppermute | solution.py:276
  21.0 0.6 %collective-permute-start.6 = (f32[144,128]{1,0:T(8,128)S(1)}, f32[144,128]{1,0:T(8,128)S(1)}, u32[]{:S(2)}, u32[]{:S(2)}) collective-permute-start(f32[144,128]{1,0:T(8,128)S(1)} %slice.55), channel_id=1, source_target_pairs={{0,12},{1,13},{2,14},{3,15},{4,8},{5,9},{6,10},{7,11},{8,4},{9,5},... | collective-permute-start | bytes 221192 | tf_op jit(solution)/shard_map/ppermute | solution.py:276
  21.6 2.0 %collective-permute-done.4 = f32[88,128]{1,0:T(8,128)S(1)} collective-permute-done((f32[88,128]{1,0:T(8,128)S(1)}, f32[88,128]{1,0:T(8,128)S(1)}, u32[]{:S(2)}, u32[]{:S(2)}) %collective-permute-start.4) | collective-permute-done | bytes 45088 | tf_op jit(solution)/shard_map/ppermute | solution.py:276
  23.6 1.6 %collective-permute-start.5 = (f32[72,128]{1,0:T(8,128)S(1)}, f32[72,128]{1,0:T(8,128)S(1)}, u32[]{:S(2)}, u32[]{:S(2)}) collective-permute-start(f32[72,128]{1,0:T(8,128)S(1)} %slice.57), channel_id=1, source_target_pairs={{0,16},{16,0},{1,17},{17,1},{2,18},{18,2},{3,19},{19,3},{4,20},{20... | collective-permute-start | bytes 110600 | tf_op jit(solution)/shard_map/ppermute | solution.py:291
  25.3 1.9 %collective-permute-done.6 = f32[144,128]{1,0:T(8,128)S(1)} collective-permute-done((f32[144,128]{1,0:T(8,128)S(1)}, f32[144,128]{1,0:T(8,128)S(1)}, u32[]{:S(2)}, u32[]{:S(2)}) %collective-permute-start.6) | collective-permute-done | bytes 73760 | tf_op jit(solution)/shard_map/ppermute | solution.py:276
  27.2 0.5 %collective-permute-done.5 = f32[72,128]{1,0:T(8,128)S(1)} collective-permute-done((f32[72,128]{1,0:T(8,128)S(1)}, f32[72,128]{1,0:T(8,128)S(1)}, u32[]{:S(2)}, u32[]{:S(2)}) %collective-permute-start.5) | collective-permute-done | bytes 36896 | tf_op jit(solution)/shard_map/ppermute | solution.py:291
  27.7 0.1 collective-permute-start.9
  27.9 1.7 %collective-permute-start.8 = (f32[296,128]{1,0:T(8,128)S(1)}, f32[296,128]{1,0:T(8,128)S(1)}, u32[]{:S(2)}, u32[]{:S(2)}) collective-permute-start(f32[296,128]{1,0:T(8,128)S(1)} %get-tuple-element.34), channel_id=1, source_target_pairs={{0,2},{1,3},{2,0},{3,1},{4,6},{5,7},{6,4},{7,5},{8,10},{9,11},{10,... | collective-permute-start | bytes 454664 | tf_op jit(solution)/shard_map/ppermute | solution.py:276
  29.5 1.8 %collective-permute-start.7 = (f32[296,128]{1,0:T(8,128)S(1)}, f32[296,128]{1,0:T(8,128)S(1)}, u32[]{:S(2)}, u32[]{:S(2)}) collective-permute-start(f32[296,128]{1,0:T(8,128)S(1)} %get-tuple-element.34), channel_id=1, source_target_pairs={{0,6},{1,7},{2,4},{3,5},{4,2},{5,3},{6,0},{7,1},{8,14},{9,15},{10,... | collective-permute-start | bytes 454664 | tf_op jit(solution)/shard_map/ppermute | solution.py:276
  31.3 1.7 %collective-permute-done.9 = f32[296,128]{1,0:T(8,128)S(1)} collective-permute-done((f32[296,128]{1,0:T(8,128)S(1)}, f32[296,128]{1,0:T(8,128)S(1)}, u32[]{:S(2)}, u32[]{:S(2)}) %collective-permute-start.9) | collective-permute-done | bytes 151584 | tf_op jit(solution)/shard_map/ppermute | solution.py:276
  33.0 0.1 collective-permute-done.8
  33.1 2.6 %collective-permute-done.7 = f32[296,128]{1,0:T(8,128)S(1)} collective-permute-done((f32[296,128]{1,0:T(8,128)S(1)}, f32[296,128]{1,0:T(8,128)S(1)}, u32[]{:S(2)}, u32[]{:S(2)}) %collective-permute-start.7) | collective-permute-done | bytes 151584 | tf_op jit(solution)/shard_map/ppermute | solution.py:276
  35.8 0.1 collective-permute-start.10
  35.8 2.0 %collective-permute-done.10.other_ref = f32[1184,128]{1,0:T(8,128)S(1)} collective-permute-done((f32[1184,128]{1,0:T(8,128)S(1)}, f32[1184,128]{1,0:T(8,128)S(1)}, u32[]{:S(2)}, u32[]{:S(2)}) %collective-permute-start.10) | collective-permute-done | bytes 606240 | tf_op jit(solution)/shard_map/ppermute | solution.py:276
  37.9 0.0 copy-done
  37.9 9.8 %step.1 = (f32[768,512]{1,0:T(8,128)}, f32[256,512]{1,0:T(8,128)}, f32[512,512]{1,0:T(8,128)}) custom-call(f32[1184,128]{1,0:T(8,128)S(1)} %constant_dynamic-update-slice_fusion.5.mine_ref, f32[1184,128]{1,0:T(8,128)S(1)} %collective-permute-done.10.other_ref, f32[768,256]{1,0:T(8,128)S(1)} %get-tuple-element.23.flipped_ref, ...), custom_call_target="tpu_custom_call" | custom-call | tf_op jit(solution)/shard_map/step/pallas_call | solution.py:333
  (16 shorter events, 0.2 us)
Async XLA Ops:
  5.0 2.0 %collective-permute-start = (f32[928,128]{1,0:T(8,128)S(1)}, f32[928,128]{1,0:T(8,128)S(1)}, u32[]{:S(2)}, u32[]{:S(2)}) collective-permute-start(f32[928,128]{1,0:T(8,128)S(1)} %get-tuple-element.15), channel_id=1, source_target_pairs={{0,1},{1,0},{2,3},{3,2},{4,5},{5,4},{6,7},{7,6},{8,9},{9,8},{10,11... | collective-permute-start | bytes 1425416 | tf_op jit(solution)/shard_map/ppermute | solution.py:276
  7.0 30.8 %copy-start = (f32[768,512]{1,0:T(8,128)S(1)}, f32[768,512]{1,0:T(8,128)}, u32[]{:S(2)}) copy-start(f32[768,512]{1,0:T(8,128)} %dict_ref.1) | copy-start | bytes 4718596
  7.1 6.6 %collective-permute-start.1 = (f32[232,128]{1,0:T(8,128)S(1)}, f32[232,128]{1,0:T(8,128)S(1)}, u32[]{:S(2)}, u32[]{:S(2)}) collective-permute-start(f32[232,128]{1,0:T(8,128)S(1)} %get-tuple-element.25), channel_id=1, source_target_pairs={{0,4},{1,5},{2,6},{3,7},{4,0},{5,1},{6,2},{7,3},{8,12},{9,13},{10,... | collective-permute-start | bytes 356360 | tf_op jit(solution)/shard_map/ppermute | solution.py:276
  10.1 7.5 %collective-permute-start.3 = (f32[232,128]{1,0:T(8,128)S(1)}, f32[232,128]{1,0:T(8,128)S(1)}, u32[]{:S(2)}, u32[]{:S(2)}) collective-permute-start(f32[232,128]{1,0:T(8,128)S(1)} %get-tuple-element.26), channel_id=1, source_target_pairs={{0,2},{1,3},{2,0},{3,1},{4,6},{5,7},{6,4},{7,5},{8,10},{9,11},{10,... | collective-permute-start | bytes 356360 | tf_op jit(solution)/shard_map/ppermute | solution.py:276
  11.6 6.1 %collective-permute-start.2 = (f32[232,128]{1,0:T(8,128)S(1)}, f32[232,128]{1,0:T(8,128)S(1)}, u32[]{:S(2)}, u32[]{:S(2)}) collective-permute-start(f32[232,128]{1,0:T(8,128)S(1)} %get-tuple-element.27), channel_id=1, source_target_pairs={{0,6},{1,7},{2,4},{3,5},{4,2},{5,3},{6,0},{7,1},{8,14},{9,15},{10,... | collective-permute-start | bytes 356360 | tf_op jit(solution)/shard_map/ppermute | solution.py:276
  17.7 5.9 %collective-permute-start.4 = (f32[88,128]{1,0:T(8,128)S(1)}, f32[88,128]{1,0:T(8,128)S(1)}, u32[]{:S(2)}, u32[]{:S(2)}) collective-permute-start(f32[88,128]{1,0:T(8,128)S(1)} %slice.54), channel_id=1, source_target_pairs={{0,12},{1,13},{2,14},{3,15},{4,8},{5,9},{6,10},{7,11},{8,4},{9,5},... | collective-permute-start | bytes 135176 | tf_op jit(solution)/shard_map/ppermute | solution.py:276
  21.0 6.2 %collective-permute-start.6 = (f32[144,128]{1,0:T(8,128)S(1)}, f32[144,128]{1,0:T(8,128)S(1)}, u32[]{:S(2)}, u32[]{:S(2)}) collective-permute-start(f32[144,128]{1,0:T(8,128)S(1)} %slice.55), channel_id=1, source_target_pairs={{0,12},{1,13},{2,14},{3,15},{4,8},{5,9},{6,10},{7,11},{8,4},{9,5},... | collective-permute-start | bytes 221192 | tf_op jit(solution)/shard_map/ppermute | solution.py:276
  23.6 4.0 %collective-permute-start.5 = (f32[72,128]{1,0:T(8,128)S(1)}, f32[72,128]{1,0:T(8,128)S(1)}, u32[]{:S(2)}, u32[]{:S(2)}) collective-permute-start(f32[72,128]{1,0:T(8,128)S(1)} %slice.57), channel_id=1, source_target_pairs={{0,16},{16,0},{1,17},{17,1},{2,18},{18,2},{3,19},{19,3},{4,20},{20... | collective-permute-start | bytes 110600 | tf_op jit(solution)/shard_map/ppermute | solution.py:291
  27.7 5.3 %collective-permute-start.9 = (f32[296,128]{1,0:T(8,128)S(1)}, f32[296,128]{1,0:T(8,128)S(1)}, u32[]{:S(2)}, u32[]{:S(2)}) collective-permute-start(f32[296,128]{1,0:T(8,128)S(1)} %get-tuple-element.34), channel_id=1, source_target_pairs={{0,4},{1,5},{2,6},{3,7},{4,0},{5,1},{6,2},{7,3},{8,12},{9,13},{10,... | collective-permute-start | bytes 454664 | tf_op jit(solution)/shard_map/ppermute | solution.py:276
  27.9 5.2 %collective-permute-start.8 = (f32[296,128]{1,0:T(8,128)S(1)}, f32[296,128]{1,0:T(8,128)S(1)}, u32[]{:S(2)}, u32[]{:S(2)}) collective-permute-start(f32[296,128]{1,0:T(8,128)S(1)} %get-tuple-element.34), channel_id=1, source_target_pairs={{0,2},{1,3},{2,0},{3,1},{4,6},{5,7},{6,4},{7,5},{8,10},{9,11},{10,... | collective-permute-start | bytes 454664 | tf_op jit(solution)/shard_map/ppermute | solution.py:276
  29.5 6.2 %collective-permute-start.7 = (f32[296,128]{1,0:T(8,128)S(1)}, f32[296,128]{1,0:T(8,128)S(1)}, u32[]{:S(2)}, u32[]{:S(2)}) collective-permute-start(f32[296,128]{1,0:T(8,128)S(1)} %get-tuple-element.34), channel_id=1, source_target_pairs={{0,6},{1,7},{2,4},{3,5},{4,2},{5,3},{6,0},{7,1},{8,14},{9,15},{10,... | collective-permute-start | bytes 454664 | tf_op jit(solution)/shard_map/ppermute | solution.py:276
  35.8 2.1 %collective-permute-start.10 = (f32[1184,128]{1,0:T(8,128)S(1)}, f32[1184,128]{1,0:T(8,128)S(1)}, u32[]{:S(2)}, u32[]{:S(2)}) collective-permute-start(f32[1184,128]{1,0:T(8,128)S(1)} %constant_dynamic-update-slice_fusion.5.mine_ref), channel_id=1, source_target_pairs={{0,1},{1,0},{2,3},{3,2},{4,5},{5,4},{6,7},{7,6},{8,9},{9,8},{10,11... | collective-permute-start | bytes 1818632 | tf_op jit(solution)/shard_map/ppermute | solution.py:276

commit v7 on v6

--- a/solution.py
+++ b/solution.py
@@ -12,7 +12,7 @@
 TILE = 128
 SPARE = 8
 BITS = 3
-SQUARE = (4, 6, 2)
+SQUARE = ((4, 2), (6, 6), (2, 4))
 F32 = jnp.float32
 BF16 = jnp.bfloat16
 
@@ -43,7 +43,7 @@
 
 
 def top_row_sum(x):
-    return jnp.max(jnp.sum(jnp.abs(x), axis=1, keepdims=True), axis=0, keepdims=True)
+    return jnp.max(jnp.sum(jnp.abs(x), axis=0, keepdims=True), axis=1, keepdims=True)
 
 
 def upper_tiles(first, count):
@@ -65,9 +65,10 @@
 
 
 def slot_of(vox):
+    core = vox & 1
     x = (vox >> 1) & 1
     z = ((vox >> 2) ^ (vox >> 3)) & 1
-    return (vox & 1) * 4 + x * 2 + (x ^ z)
+    return core * 4 + (x + core * (z - x)) * 2 + (x ^ z)
 
 
 def column(row):
@@ -142,11 +143,11 @@
         spare = spare + jnp.where(place == j, row, 0.0)
     slots = 1 << BITS
     rows = TILE // slots
-    me = slot_of(lax.axis_index("vox"))
+    vox = lax.axis_index("vox")
     half = slots // 2
     for o in range(slots):
         out = keep_ref if o < half else send_ref
-        which = me ^ o
+        which = slot_of(vox ^ (o // half)) ^ (o % half)
         base = o % half * (at * rows + SPARE)
         for k in range(at):
             to = base + k * rows + (SPARE if k >= first else 0)
@@ -161,7 +162,7 @@
     slots = 1 << BITS
     rows = TILE // slots
     half = slots // 2
-    place = slot_of(lax.axis_index("vox"))
+    vox = lax.axis_index("vox")
     grams, rest = layout(batch, atoms)
     kinds = []
     for pairs, plain in grams + [rest]:
@@ -170,7 +171,7 @@
     spare = jnp.zeros((SPARE, TILE), F32)
     for o in range(slots):
         source = mine_ref if o < half else other_ref
-        start = (place ^ o) * rows
+        start = (slot_of(vox ^ (o // half)) ^ (o % half)) * rows
         base = o % half * (len(kinds) * rows + SPARE)
         packed = 0
         for k, ((r, c), pair) in enumerate(kinds):
@@ -273,12 +274,14 @@
 
 def all_reduce(keep, send, gram_rows, devices, folds):
     def swap(x, bit):
-        return lax.ppermute(x, "vox", [(i, i ^ bit) for i in range(devices)])
+        bits = bit if isinstance(bit, tuple) else (bit, bit)
+        return lax.ppermute(x, "vox", [(i, i ^ bits[i % 2]) for i in range(devices)])
 
     total = keep + swap(send, 1)
     slot = total.shape[0] // (len(SQUARE) + 1)
     own = total[:slot]
     got = [swap(total[(k + 1) * slot:(k + 2) * slot], bit) for k, bit in enumerate(SQUARE)]
+    got = lax.optimization_barrier((got[2], got[0], got[1]))
     for part in got:
         own = own + part
     head = gram_rows + SPARE

time: 47.9 us -> 47.8 us (level)
  no operation moved by 1% of the time
where the time goes in v7:
time: 47.8 us; the launch traced here: 47.6 us
  waiting for transfers between devices  18.2 us (38%)
  starting transfers between devices  14.2 us (30%)
  Pallas kernels  13.6 us (28%)
  between operations  1.4 us (3%)
    ppermute x10, waiting for transfers between devices, swap(): lax.ppermute(x, 'vox', [(i, i ^ bits[i % 2]) for i in range(devices)])  18 us
    ppermute x10, starting transfers between devices, swap(): lax.ppermute(x, 'vox', [(i, i ^ bits[i % 2]) for i in range(devices)])  12.6 us
    pallas_call x1, Pallas kernels, shards(): pl.pallas_call(step_kernel, out_shape=tuple((jax.ShapeDtypeStruct(shape,...  9.84 us
    pallas_call x1, Pallas kernels, shards(): pl.pallas_call(gram_kernel, out_shape=(part, part, jax.ShapeDtypeStruct((...  3.73 us
    ppermute x1, starting transfers between devices, all_reduce(): lax.ppermute(gram[:head], 'fold', [(i, i ^ 1) for i in range(folds)])  1.61 us
  transfers between devices with their start and end apart: 11, of which 10 were waited for; matrix products, arithmetic and copies ran while one was open for 0% of the time, Pallas kernels for 0%

profile of v7, /device:TPU:0, one launch (start us, length us, event | category | flops | bytes accessed | tf_op | source)
XLA Modules:
  0.0 47.6 jit_solution(4343807562538559123)
XLA Ops:
  1.3 3.7 %grams.1 = (f32[928,128]{1,0:T(8,128)S(1)}, f32[928,128]{1,0:T(8,128)S(1)}, f32[768,256]{1,0:T(8,128)S(1)}, f32[256,128]{1,0:T(8,128)S(1)}) custom-call(s32[1,256]{1,0:T(1,128)} %bitcast.3, s32[1,512]{1,0:T(1,128)} %bitcast.2, s32[1]{0:T(128)S(6)} %copy.19.held_ref, f32[512,768]{1,0:T(8,128)} %volumes_hbm.1, f32[768,512]{1,0:T(8,128)} %dict_ref.1), custom_call_target="tpu_custom_call" | custom-call | tf_op jit(solution)/shard_map/grams/pallas_call | solution.py:322
  5.0 0.5 %collective-permute-start = (f32[928,128]{1,0:T(8,128)S(1)}, f32[928,128]{1,0:T(8,128)S(1)}, u32[]{:S(2)}, u32[]{:S(2)}) collective-permute-start(f32[928,128]{1,0:T(8,128)S(1)} %get-tuple-element.18), channel_id=1, source_target_pairs={{0,1},{1,0},{2,3},{3,2},{4,5},{5,4},{6,7},{7,6},{8,9},{9,8},{10,11... | collective-permute-start | bytes 1425416 | tf_op jit(solution)/shard_map/ppermute | solution.py:278
  5.5 1.5 %collective-permute-done = f32[928,128]{1,0:T(8,128)S(1)} collective-permute-done((f32[928,128]{1,0:T(8,128)S(1)}, f32[928,128]{1,0:T(8,128)S(1)}, u32[]{:S(2)}, u32[]{:S(2)}) %collective-permute-start) | collective-permute-done | bytes 475168 | tf_op jit(solution)/shard_map/ppermute | solution.py:278
  7.0 0.0 copy-start
  7.1 3.9 %collective-permute-start.3 = (f32[232,128]{1,0:T(8,128)S(1)}, f32[232,128]{1,0:T(8,128)S(1)}, u32[]{:S(2)}, u32[]{:S(2)}) collective-permute-start(f32[232,128]{1,0:T(8,128)S(1)} %get-tuple-element.31), channel_id=1, source_target_pairs={{0,6},{1,7},{2,4},{3,5},{4,2},{5,3},{6,0},{7,1},{8,14},{9,15},{10,... | collective-permute-start | bytes 356360 | tf_op jit(solution)/shard_map/ppermute | solution.py:278
  11.0 0.4 collective-permute-start.2
  11.5 0.2 collective-permute-start.1
  11.7 3.0 %collective-permute-done.3 = f32[232,128]{1,0:T(8,128)S(1)} collective-permute-done((f32[232,128]{1,0:T(8,128)S(1)}, f32[232,128]{1,0:T(8,128)S(1)}, u32[]{:S(2)}, u32[]{:S(2)}) %collective-permute-start.3) | collective-permute-done | bytes 118816 | tf_op jit(solution)/shard_map/ppermute | solution.py:278
  14.7 2.6 %collective-permute-done.2 = f32[232,128]{1,0:T(8,128)S(1)} collective-permute-done((f32[232,128]{1,0:T(8,128)S(1)}, f32[232,128]{1,0:T(8,128)S(1)}, u32[]{:S(2)}, u32[]{:S(2)}) %collective-permute-start.2) | collective-permute-done | bytes 118816 | tf_op jit(solution)/shard_map/ppermute | solution.py:278
  17.3 0.0 collective-permute-done.1
  17.3 3.7 %collective-permute-start.4 = (f32[88,128]{1,0:T(8,128)S(1)}, f32[88,128]{1,0:T(8,128)S(1)}, u32[]{:S(2)}, u32[]{:S(2)}) collective-permute-start(f32[88,128]{1,0:T(8,128)S(1)} %slice.54), channel_id=1, source_target_pairs={{0,12},{1,13},{2,14},{3,15},{4,8},{5,9},{6,10},{7,11},{8,4},{9,5},... | collective-permute-start | bytes 135176 | tf_op jit(solution)/shard_map/ppermute | solution.py:278
  21.1 0.2 collective-permute-start.6
  21.2 2.1 %collective-permute-done.4 = f32[88,128]{1,0:T(8,128)S(1)} collective-permute-done((f32[88,128]{1,0:T(8,128)S(1)}, f32[88,128]{1,0:T(8,128)S(1)}, u32[]{:S(2)}, u32[]{:S(2)}) %collective-permute-start.4) | collective-permute-done | bytes 45088 | tf_op jit(solution)/shard_map/ppermute | solution.py:278
  23.4 1.6 %collective-permute-start.5 = (f32[72,128]{1,0:T(8,128)S(1)}, f32[72,128]{1,0:T(8,128)S(1)}, u32[]{:S(2)}, u32[]{:S(2)}) collective-permute-start(f32[72,128]{1,0:T(8,128)S(1)} %slice.57), channel_id=1, source_target_pairs={{0,16},{16,0},{1,17},{17,1},{2,18},{18,2},{3,19},{19,3},{4,20},{20... | collective-permute-start | bytes 110600 | tf_op jit(solution)/shard_map/ppermute | solution.py:294
  25.0 2.2 %collective-permute-done.6 = f32[144,128]{1,0:T(8,128)S(1)} collective-permute-done((f32[144,128]{1,0:T(8,128)S(1)}, f32[144,128]{1,0:T(8,128)S(1)}, u32[]{:S(2)}, u32[]{:S(2)}) %collective-permute-start.6) | collective-permute-done | bytes 73760 | tf_op jit(solution)/shard_map/ppermute | solution.py:278
  27.2 0.2 collective-permute-done.5
  27.5 0.7 %collective-permute-start.9 = (f32[296,128]{1,0:T(8,128)S(1)}, f32[296,128]{1,0:T(8,128)S(1)}, u32[]{:S(2)}, u32[]{:S(2)}) collective-permute-start(f32[296,128]{1,0:T(8,128)S(1)} %get-tuple-element.40), channel_id=1, source_target_pairs={{0,4},{1,3},{2,6},{3,1},{4,0},{5,7},{6,2},{7,5},{8,12},{9,11},{10,... | collective-permute-start | bytes 454664 | tf_op jit(solution)/shard_map/ppermute | solution.py:278
  28.2 0.8 %collective-permute-start.8 = (f32[296,128]{1,0:T(8,128)S(1)}, f32[296,128]{1,0:T(8,128)S(1)}, u32[]{:S(2)}, u32[]{:S(2)}) collective-permute-start(f32[296,128]{1,0:T(8,128)S(1)} %get-tuple-element.40), channel_id=1, source_target_pairs={{0,2},{1,5},{2,0},{3,7},{4,6},{5,1},{6,4},{7,3},{8,10},{9,13},{10,... | collective-permute-start | bytes 454664 | tf_op jit(solution)/shard_map/ppermute | solution.py:278
  29.0 2.0 %collective-permute-start.7 = (f32[296,128]{1,0:T(8,128)S(1)}, f32[296,128]{1,0:T(8,128)S(1)}, u32[]{:S(2)}, u32[]{:S(2)}) collective-permute-start(f32[296,128]{1,0:T(8,128)S(1)} %get-tuple-element.40), channel_id=1, source_target_pairs={{0,6},{1,7},{2,4},{3,5},{4,2},{5,3},{6,0},{7,1},{8,14},{9,15},{10,... | collective-permute-start | bytes 454664 | tf_op jit(solution)/shard_map/ppermute | solution.py:278
  31.0 2.9 %collective-permute-done.9 = f32[296,128]{1,0:T(8,128)S(1)} collective-permute-done((f32[296,128]{1,0:T(8,128)S(1)}, f32[296,128]{1,0:T(8,128)S(1)}, u32[]{:S(2)}, u32[]{:S(2)}) %collective-permute-start.9) | collective-permute-done | bytes 151584 | tf_op jit(solution)/shard_map/ppermute | solution.py:278
  33.9 0.1 collective-permute-done.8
  34.0 1.6 %collective-permute-done.7 = f32[296,128]{1,0:T(8,128)S(1)} collective-permute-done((f32[296,128]{1,0:T(8,128)S(1)}, f32[296,128]{1,0:T(8,128)S(1)}, u32[]{:S(2)}, u32[]{:S(2)}) %collective-permute-start.7) | collective-permute-done | bytes 151584 | tf_op jit(solution)/shard_map/ppermute | solution.py:278
  35.7 0.1 collective-permute-start.10
  35.8 2.0 %collective-permute-done.10.other_ref = f32[1184,128]{1,0:T(8,128)S(1)} collective-permute-done((f32[1184,128]{1,0:T(8,128)S(1)}, f32[1184,128]{1,0:T(8,128)S(1)}, u32[]{:S(2)}, u32[]{:S(2)}) %collective-permute-start.10) | collective-permute-done | bytes 606240 | tf_op jit(solution)/shard_map/ppermute | solution.py:278
  37.8 0.0 copy-done
  37.8 9.8 %step.1 = (f32[768,512]{1,0:T(8,128)}, f32[256,512]{1,0:T(8,128)}, f32[512,512]{1,0:T(8,128)}) custom-call(f32[1184,128]{1,0:T(8,128)S(1)} %constant_dynamic-update-slice_fusion.5.mine_ref, f32[1184,128]{1,0:T(8,128)S(1)} %collective-permute-done.10.other_ref, f32[768,256]{1,0:T(8,128)S(1)} %get-tuple-element.29.flipped_ref, ...), custom_call_target="tpu_custom_call" | custom-call | tf_op jit(solution)/shard_map/step/pallas_call | solution.py:336
  (16 shorter events, 0.2 us)
Async XLA Ops:
  5.0 2.0 %collective-permute-start = (f32[928,128]{1,0:T(8,128)S(1)}, f32[928,128]{1,0:T(8,128)S(1)}, u32[]{:S(2)}, u32[]{:S(2)}) collective-permute-start(f32[928,128]{1,0:T(8,128)S(1)} %get-tuple-element.18), channel_id=1, source_target_pairs={{0,1},{1,0},{2,3},{3,2},{4,5},{5,4},{6,7},{7,6},{8,9},{9,8},{10,11... | collective-permute-start | bytes 1425416 | tf_op jit(solution)/shard_map/ppermute | solution.py:278
  7.0 30.7 %copy-start = (f32[768,512]{1,0:T(8,128)S(1)}, f32[768,512]{1,0:T(8,128)}, u32[]{:S(2)}) copy-start(f32[768,512]{1,0:T(8,128)} %dict_ref.1) | copy-start | bytes 4718596
  7.1 7.6 %collective-permute-start.3 = (f32[232,128]{1,0:T(8,128)S(1)}, f32[232,128]{1,0:T(8,128)S(1)}, u32[]{:S(2)}, u32[]{:S(2)}) collective-permute-start(f32[232,128]{1,0:T(8,128)S(1)} %get-tuple-element.31), channel_id=1, source_target_pairs={{0,6},{1,7},{2,4},{3,5},{4,2},{5,3},{6,0},{7,1},{8,14},{9,15},{10,... | collective-permute-start | bytes 356360 | tf_op jit(solution)/shard_map/ppermute | solution.py:278
  11.0 6.2 %collective-permute-start.2 = (f32[232,128]{1,0:T(8,128)S(1)}, f32[232,128]{1,0:T(8,128)S(1)}, u32[]{:S(2)}, u32[]{:S(2)}) collective-permute-start(f32[232,128]{1,0:T(8,128)S(1)} %get-tuple-element.32), channel_id=1, source_target_pairs={{0,4},{1,3},{2,6},{3,1},{4,0},{5,7},{6,2},{7,5},{8,12},{9,11},{10,... | collective-permute-start | bytes 356360 | tf_op jit(solution)/shard_map/ppermute | solution.py:278
  11.5 5.8 %collective-permute-start.1 = (f32[232,128]{1,0:T(8,128)S(1)}, f32[232,128]{1,0:T(8,128)S(1)}, u32[]{:S(2)}, u32[]{:S(2)}) collective-permute-start(f32[232,128]{1,0:T(8,128)S(1)} %get-tuple-element.33), channel_id=1, source_target_pairs={{0,2},{1,5},{2,0},{3,7},{4,6},{5,1},{6,4},{7,3},{8,10},{9,13},{10,... | collective-permute-start | bytes 356360 | tf_op jit(solution)/shard_map/ppermute | solution.py:278
  17.3 6.0 %collective-permute-start.4 = (f32[88,128]{1,0:T(8,128)S(1)}, f32[88,128]{1,0:T(8,128)S(1)}, u32[]{:S(2)}, u32[]{:S(2)}) collective-permute-start(f32[88,128]{1,0:T(8,128)S(1)} %slice.54), channel_id=1, source_target_pairs={{0,12},{1,13},{2,14},{3,15},{4,8},{5,9},{6,10},{7,11},{8,4},{9,5},... | collective-permute-start | bytes 135176 | tf_op jit(solution)/shard_map/ppermute | solution.py:278
  21.1 6.2 %collective-permute-start.6 = (f32[144,128]{1,0:T(8,128)S(1)}, f32[144,128]{1,0:T(8,128)S(1)}, u32[]{:S(2)}, u32[]{:S(2)}) collective-permute-start(f32[144,128]{1,0:T(8,128)S(1)} %slice.55), channel_id=1, source_target_pairs={{0,12},{1,13},{2,14},{3,15},{4,8},{5,9},{6,10},{7,11},{8,4},{9,5},... | collective-permute-start | bytes 221192 | tf_op jit(solution)/shard_map/ppermute | solution.py:278
  23.4 4.0 %collective-permute-start.5 = (f32[72,128]{1,0:T(8,128)S(1)}, f32[72,128]{1,0:T(8,128)S(1)}, u32[]{:S(2)}, u32[]{:S(2)}) collective-permute-start(f32[72,128]{1,0:T(8,128)S(1)} %slice.57), channel_id=1, source_target_pairs={{0,16},{16,0},{1,17},{17,1},{2,18},{18,2},{3,19},{19,3},{4,20},{20... | collective-permute-start | bytes 110600 | tf_op jit(solution)/shard_map/ppermute | solution.py:294
  27.5 6.4 %collective-permute-start.9 = (f32[296,128]{1,0:T(8,128)S(1)}, f32[296,128]{1,0:T(8,128)S(1)}, u32[]{:S(2)}, u32[]{:S(2)}) collective-permute-start(f32[296,128]{1,0:T(8,128)S(1)} %get-tuple-element.40), channel_id=1, source_target_pairs={{0,4},{1,3},{2,6},{3,1},{4,0},{5,7},{6,2},{7,5},{8,12},{9,11},{10,... | collective-permute-start | bytes 454664 | tf_op jit(solution)/shard_map/ppermute | solution.py:278
  28.2 5.8 %collective-permute-start.8 = (f32[296,128]{1,0:T(8,128)S(1)}, f32[296,128]{1,0:T(8,128)S(1)}, u32[]{:S(2)}, u32[]{:S(2)}) collective-permute-start(f32[296,128]{1,0:T(8,128)S(1)} %get-tuple-element.40), channel_id=1, source_target_pairs={{0,2},{1,5},{2,0},{3,7},{4,6},{5,1},{6,4},{7,3},{8,10},{9,13},{10,... | collective-permute-start | bytes 454664 | tf_op jit(solution)/shard_map/ppermute | solution.py:278
  29.0 6.6 %collective-permute-start.7 = (f32[296,128]{1,0:T(8,128)S(1)}, f32[296,128]{1,0:T(8,128)S(1)}, u32[]{:S(2)}, u32[]{:S(2)}) collective-permute-start(f32[296,128]{1,0:T(8,128)S(1)} %get-tuple-element.40), channel_id=1, source_target_pairs={{0,6},{1,7},{2,4},{3,5},{4,2},{5,3},{6,0},{7,1},{8,14},{9,15},{10,... | collective-permute-start | bytes 454664 | tf_op jit(solution)/shard_map/ppermute | solution.py:278
  35.7 2.1 %collective-permute-start.10 = (f32[1184,128]{1,0:T(8,128)S(1)}, f32[1184,128]{1,0:T(8,128)S(1)}, u32[]{:S(2)}, u32[]{:S(2)}) collective-permute-start(f32[1184,128]{1,0:T(8,128)S(1)} %constant_dynamic-update-slice_fusion.5.mine_ref), channel_id=1, source_target_pairs={{0,1},{1,0},{2,3},{3,2},{4,5},{5,4},{6,7},{7,6},{8,9},{9,8},{10,11... | collective-permute-start | bytes 1818632 | tf_op jit(solution)/shard_map/ppermute | solution.py:278

commit v8 on v7

--- a/solution.py
+++ b/solution.py
@@ -285,7 +285,7 @@
     for part in got:
         own = own + part
     head = gram_rows + SPARE
-    cut = head + 2 * SPARE
+    cut = head + SPARE
     gram, rest = lax.optimization_barrier((own[:cut], own[cut:]))
     for k in range(BITS, devices.bit_length() - 1):
         bit = 3 << (k - 1) if k == BITS else 1 << k
@@ -298,7 +298,7 @@
     second = jnp.where(even, next_gram[:gram_rows], gram[:gram_rows])
     own = jnp.concatenate([first, second, gram[gram_rows:head] + next_gram[gram_rows:], gram[head:], rest])
     ahead, across, along = (swap(own, bit) for bit in SQUARE)
-    across, along, ahead = lax.optimization_barrier((across, along, ahead))
+    along, ahead, across = lax.optimization_barrier((along, ahead, across))
     mine = jnp.concatenate([own, ahead, across, along])
     return mine, swap(mine, 1)
 

time: 47.8 us -> 47.7 us (level)
  no operation moved by 1% of the time
where the time goes in v8:
time: 47.7 us; the launch traced here: 47.5 us
  waiting for transfers between devices  18.1 us (38%)
  starting transfers between devices  14.2 us (30%)
  Pallas kernels  13.6 us (29%)
  between operations  1.4 us (3%)
    ppermute x10, waiting for transfers between devices, swap(): lax.ppermute(x, 'vox', [(i, i ^ bits[i % 2]) for i in range(devices)])  18 us
    ppermute x10, starting transfers between devices, swap(): lax.ppermute(x, 'vox', [(i, i ^ bits[i % 2]) for i in range(devices)])  12.6 us
    pallas_call x1, Pallas kernels, shards(): pl.pallas_call(step_kernel, out_shape=tuple((jax.ShapeDtypeStruct(shape,...  9.83 us
    pallas_call x1, Pallas kernels, shards(): pl.pallas_call(gram_kernel, out_shape=(part, part, jax.ShapeDtypeStruct((...  3.73 us
    ppermute x1, starting transfers between devices, all_reduce(): lax.ppermute(gram[:head], 'fold', [(i, i ^ 1) for i in range(folds)])  1.61 us
  transfers between devices with their start and end apart: 11, of which 10 were waited for; matrix products, arithmetic and copies ran while one was open for 0% of the time, Pallas kernels for 0%

profile of v8, /device:TPU:0, one launch (start us, length us, event | category | flops | bytes accessed | tf_op | source)
XLA Modules:
  0.0 47.5 jit_solution(3544554580334101814)
XLA Ops:
  1.3 3.7 %grams.1 = (f32[928,128]{1,0:T(8,128)S(1)}, f32[928,128]{1,0:T(8,128)S(1)}, f32[768,256]{1,0:T(8,128)S(1)}, f32[256,128]{1,0:T(8,128)S(1)}) custom-call(s32[1,256]{1,0:T(1,128)} %bitcast.3, s32[1,512]{1,0:T(1,128)} %bitcast.2, s32[1]{0:T(128)S(6)} %copy.19.held_ref, f32[512,768]{1,0:T(8,128)} %volumes_hbm.1, f32[768,512]{1,0:T(8,128)} %dict_ref.1), custom_call_target="tpu_custom_call" | custom-call | tf_op jit(solution)/shard_map/grams/pallas_call | solution.py:322
  5.0 0.5 %collective-permute-start = (f32[928,128]{1,0:T(8,128)S(1)}, f32[928,128]{1,0:T(8,128)S(1)}, u32[]{:S(2)}, u32[]{:S(2)}) collective-permute-start(f32[928,128]{1,0:T(8,128)S(1)} %get-tuple-element.18), channel_id=1, source_target_pairs={{0,1},{1,0},{2,3},{3,2},{4,5},{5,4},{6,7},{7,6},{8,9},{9,8},{10,11... | collective-permute-start | bytes 1425416 | tf_op jit(solution)/shard_map/ppermute | solution.py:278
  5.5 1.5 %collective-permute-done = f32[928,128]{1,0:T(8,128)S(1)} collective-permute-done((f32[928,128]{1,0:T(8,128)S(1)}, f32[928,128]{1,0:T(8,128)S(1)}, u32[]{:S(2)}, u32[]{:S(2)}) %collective-permute-start) | collective-permute-done | bytes 475168 | tf_op jit(solution)/shard_map/ppermute | solution.py:278
  7.0 0.0 copy-start
  7.1 3.9 %collective-permute-start.3 = (f32[232,128]{1,0:T(8,128)S(1)}, f32[232,128]{1,0:T(8,128)S(1)}, u32[]{:S(2)}, u32[]{:S(2)}) collective-permute-start(f32[232,128]{1,0:T(8,128)S(1)} %get-tuple-element.31), channel_id=1, source_target_pairs={{0,6},{1,7},{2,4},{3,5},{4,2},{5,3},{6,0},{7,1},{8,14},{9,15},{10,... | collective-permute-start | bytes 356360 | tf_op jit(solution)/shard_map/ppermute | solution.py:278
  11.0 0.4 collective-permute-start.2
  11.5 0.2 collective-permute-start.1
  11.7 3.0 %collective-permute-done.3 = f32[232,128]{1,0:T(8,128)S(1)} collective-permute-done((f32[232,128]{1,0:T(8,128)S(1)}, f32[232,128]{1,0:T(8,128)S(1)}, u32[]{:S(2)}, u32[]{:S(2)}) %collective-permute-start.3) | collective-permute-done | bytes 118816 | tf_op jit(solution)/shard_map/ppermute | solution.py:278
  14.7 2.6 %collective-permute-done.2 = f32[232,128]{1,0:T(8,128)S(1)} collective-permute-done((f32[232,128]{1,0:T(8,128)S(1)}, f32[232,128]{1,0:T(8,128)S(1)}, u32[]{:S(2)}, u32[]{:S(2)}) %collective-permute-start.2) | collective-permute-done | bytes 118816 | tf_op jit(solution)/shard_map/ppermute | solution.py:278
  17.3 0.0 collective-permute-done.1
  17.3 3.7 %collective-permute-start.4 = (f32[80,128]{1,0:T(8,128)S(1)}, f32[80,128]{1,0:T(8,128)S(1)}, u32[]{:S(2)}, u32[]{:S(2)}) collective-permute-start(f32[80,128]{1,0:T(8,128)S(1)} %slice.54), channel_id=1, source_target_pairs={{0,12},{1,13},{2,14},{3,15},{4,8},{5,9},{6,10},{7,11},{8,4},{9,5},... | collective-permute-start | bytes 122888 | tf_op jit(solution)/shard_map/ppermute | solution.py:278
  21.1 0.2 collective-permute-start.6
  21.2 2.1 %collective-permute-done.4 = f32[80,128]{1,0:T(8,128)S(1)} collective-permute-done((f32[80,128]{1,0:T(8,128)S(1)}, f32[80,128]{1,0:T(8,128)S(1)}, u32[]{:S(2)}, u32[]{:S(2)}) %collective-permute-start.4) | collective-permute-done | bytes 40992 | tf_op jit(solution)/shard_map/ppermute | solution.py:278
  23.3 1.6 %collective-permute-start.5 = (f32[72,128]{1,0:T(8,128)S(1)}, f32[72,128]{1,0:T(8,128)S(1)}, u32[]{:S(2)}, u32[]{:S(2)}) collective-permute-start(f32[72,128]{1,0:T(8,128)S(1)} %slice.57), channel_id=1, source_target_pairs={{0,16},{16,0},{1,17},{17,1},{2,18},{18,2},{3,19},{19,3},{4,20},{20... | collective-permute-start | bytes 110600 | tf_op jit(solution)/shard_map/ppermute | solution.py:294
  24.9 2.3 %collective-permute-done.6 = f32[152,128]{1,0:T(8,128)S(1)} collective-permute-done((f32[152,128]{1,0:T(8,128)S(1)}, f32[152,128]{1,0:T(8,128)S(1)}, u32[]{:S(2)}, u32[]{:S(2)}) %collective-permute-start.6) | collective-permute-done | bytes 77856 | tf_op jit(solution)/shard_map/ppermute | solution.py:278
  27.3 0.1 collective-permute-done.5
  27.4 0.7 %collective-permute-start.9 = (f32[296,128]{1,0:T(8,128)S(1)}, f32[296,128]{1,0:T(8,128)S(1)}, u32[]{:S(2)}, u32[]{:S(2)}) collective-permute-start(f32[296,128]{1,0:T(8,128)S(1)} %get-tuple-element.34), channel_id=1, source_target_pairs={{0,6},{1,7},{2,4},{3,5},{4,2},{5,3},{6,0},{7,1},{8,14},{9,15},{10,... | collective-permute-start | bytes 454664 | tf_op jit(solution)/shard_map/ppermute | solution.py:278
  28.2 2.2 %collective-permute-start.8 = (f32[296,128]{1,0:T(8,128)S(1)}, f32[296,128]{1,0:T(8,128)S(1)}, u32[]{:S(2)}, u32[]{:S(2)}) collective-permute-start(f32[296,128]{1,0:T(8,128)S(1)} %get-tuple-element.34), channel_id=1, source_target_pairs={{0,4},{1,3},{2,6},{3,1},{4,0},{5,7},{6,2},{7,5},{8,12},{9,11},{10,... | collective-permute-start | bytes 454664 | tf_op jit(solution)/shard_map/ppermute | solution.py:278
  30.4 0.6 %collective-permute-start.7 = (f32[296,128]{1,0:T(8,128)S(1)}, f32[296,128]{1,0:T(8,128)S(1)}, u32[]{:S(2)}, u32[]{:S(2)}) collective-permute-start(f32[296,128]{1,0:T(8,128)S(1)} %get-tuple-element.34), channel_id=1, source_target_pairs={{0,2},{1,5},{2,0},{3,7},{4,6},{5,1},{6,4},{7,3},{8,10},{9,13},{10,... | collective-permute-start | bytes 454664 | tf_op jit(solution)/shard_map/ppermute | solution.py:278
  31.0 2.8 %collective-permute-done.9 = f32[296,128]{1,0:T(8,128)S(1)} collective-permute-done((f32[296,128]{1,0:T(8,128)S(1)}, f32[296,128]{1,0:T(8,128)S(1)}, u32[]{:S(2)}, u32[]{:S(2)}) %collective-permute-start.9) | collective-permute-done | bytes 151584 | tf_op jit(solution)/shard_map/ppermute | solution.py:278
  33.8 1.5 %collective-permute-done.8 = f32[296,128]{1,0:T(8,128)S(1)} collective-permute-done((f32[296,128]{1,0:T(8,128)S(1)}, f32[296,128]{1,0:T(8,128)S(1)}, u32[]{:S(2)}, u32[]{:S(2)}) %collective-permute-start.8) | collective-permute-done | bytes 151584 | tf_op jit(solution)/shard_map/ppermute | solution.py:278
  35.2 0.3 collective-permute-done.7
  35.6 0.1 collective-permute-start.10
  35.7 2.0 %collective-permute-done.10.other_ref = f32[1184,128]{1,0:T(8,128)S(1)} collective-permute-done((f32[1184,128]{1,0:T(8,128)S(1)}, f32[1184,128]{1,0:T(8,128)S(1)}, u32[]{:S(2)}, u32[]{:S(2)}) %collective-permute-start.10) | collective-permute-done | bytes 606240 | tf_op jit(solution)/shard_map/ppermute | solution.py:278
  37.7 0.0 copy-done
  37.7 9.8 %step.1 = (f32[768,512]{1,0:T(8,128)}, f32[256,512]{1,0:T(8,128)}, f32[512,512]{1,0:T(8,128)}) custom-call(f32[1184,128]{1,0:T(8,128)S(1)} %constant_dynamic-update-slice_fusion.5.mine_ref, f32[1184,128]{1,0:T(8,128)S(1)} %collective-permute-done.10.other_ref, f32[768,256]{1,0:T(8,128)S(1)} %get-tuple-element.29.flipped_ref, ...), custom_call_target="tpu_custom_call" | custom-call | tf_op jit(solution)/shard_map/step/pallas_call | solution.py:336
  (16 shorter events, 0.2 us)
Async XLA Ops:
  5.0 2.0 %collective-permute-start = (f32[928,128]{1,0:T(8,128)S(1)}, f32[928,128]{1,0:T(8,128)S(1)}, u32[]{:S(2)}, u32[]{:S(2)}) collective-permute-start(f32[928,128]{1,0:T(8,128)S(1)} %get-tuple-element.18), channel_id=1, source_target_pairs={{0,1},{1,0},{2,3},{3,2},{4,5},{5,4},{6,7},{7,6},{8,9},{9,8},{10,11... | collective-permute-start | bytes 1425416 | tf_op jit(solution)/shard_map/ppermute | solution.py:278
  7.0 30.6 %copy-start = (f32[768,512]{1,0:T(8,128)S(1)}, f32[768,512]{1,0:T(8,128)}, u32[]{:S(2)}) copy-start(f32[768,512]{1,0:T(8,128)} %dict_ref.1) | copy-start | bytes 4718596
  7.1 7.6 %collective-permute-start.3 = (f32[232,128]{1,0:T(8,128)S(1)}, f32[232,128]{1,0:T(8,128)S(1)}, u32[]{:S(2)}, u32[]{:S(2)}) collective-permute-start(f32[232,128]{1,0:T(8,128)S(1)} %get-tuple-element.31), channel_id=1, source_target_pairs={{0,6},{1,7},{2,4},{3,5},{4,2},{5,3},{6,0},{7,1},{8,14},{9,15},{10,... | collective-permute-start | bytes 356360 | tf_op jit(solution)/shard_map/ppermute | solution.py:278
  11.0 6.2 %collective-permute-start.2 = (f32[232,128]{1,0:T(8,128)S(1)}, f32[232,128]{1,0:T(8,128)S(1)}, u32[]{:S(2)}, u32[]{:S(2)}) collective-permute-start(f32[232,128]{1,0:T(8,128)S(1)} %get-tuple-element.32), channel_id=1, source_target_pairs={{0,4},{1,3},{2,6},{3,1},{4,0},{5,7},{6,2},{7,5},{8,12},{9,11},{10,... | collective-permute-start | bytes 356360 | tf_op jit(solution)/shard_map/ppermute | solution.py:278
  11.5 5.8 %collective-permute-start.1 = (f32[232,128]{1,0:T(8,128)S(1)}, f32[232,128]{1,0:T(8,128)S(1)}, u32[]{:S(2)}, u32[]{:S(2)}) collective-permute-start(f32[232,128]{1,0:T(8,128)S(1)} %get-tuple-element.33), channel_id=1, source_target_pairs={{0,2},{1,5},{2,0},{3,7},{4,6},{5,1},{6,4},{7,3},{8,10},{9,13},{10,... | collective-permute-start | bytes 356360 | tf_op jit(solution)/shard_map/ppermute | solution.py:278
  17.3 6.0 %collective-permute-start.4 = (f32[80,128]{1,0:T(8,128)S(1)}, f32[80,128]{1,0:T(8,128)S(1)}, u32[]{:S(2)}, u32[]{:S(2)}) collective-permute-start(f32[80,128]{1,0:T(8,128)S(1)} %slice.54), channel_id=1, source_target_pairs={{0,12},{1,13},{2,14},{3,15},{4,8},{5,9},{6,10},{7,11},{8,4},{9,5},... | collective-permute-start | bytes 122888 | tf_op jit(solution)/shard_map/ppermute | solution.py:278
  21.1 6.2 %collective-permute-start.6 = (f32[152,128]{1,0:T(8,128)S(1)}, f32[152,128]{1,0:T(8,128)S(1)}, u32[]{:S(2)}, u32[]{:S(2)}) collective-permute-start(f32[152,128]{1,0:T(8,128)S(1)} %slice.55), channel_id=1, source_target_pairs={{0,12},{1,13},{2,14},{3,15},{4,8},{5,9},{6,10},{7,11},{8,4},{9,5},... | collective-permute-start | bytes 233480 | tf_op jit(solution)/shard_map/ppermute | solution.py:278
  23.3 4.0 %collective-permute-start.5 = (f32[72,128]{1,0:T(8,128)S(1)}, f32[72,128]{1,0:T(8,128)S(1)}, u32[]{:S(2)}, u32[]{:S(2)}) collective-permute-start(f32[72,128]{1,0:T(8,128)S(1)} %slice.57), channel_id=1, source_target_pairs={{0,16},{16,0},{1,17},{17,1},{2,18},{18,2},{3,19},{19,3},{4,20},{20... | collective-permute-start | bytes 110600 | tf_op jit(solution)/shard_map/ppermute | solution.py:294
  27.4 6.4 %collective-permute-start.9 = (f32[296,128]{1,0:T(8,128)S(1)}, f32[296,128]{1,0:T(8,128)S(1)}, u32[]{:S(2)}, u32[]{:S(2)}) collective-permute-start(f32[296,128]{1,0:T(8,128)S(1)} %get-tuple-element.34), channel_id=1, source_target_pairs={{0,6},{1,7},{2,4},{3,5},{4,2},{5,3},{6,0},{7,1},{8,14},{9,15},{10,... | collective-permute-start | bytes 454664 | tf_op jit(solution)/shard_map/ppermute | solution.py:278
  28.2 7.1 %collective-permute-start.8 = (f32[296,128]{1,0:T(8,128)S(1)}, f32[296,128]{1,0:T(8,128)S(1)}, u32[]{:S(2)}, u32[]{:S(2)}) collective-permute-start(f32[296,128]{1,0:T(8,128)S(1)} %get-tuple-element.34), channel_id=1, source_target_pairs={{0,4},{1,3},{2,6},{3,1},{4,0},{5,7},{6,2},{7,5},{8,12},{9,11},{10,... | collective-permute-start | bytes 454664 | tf_op jit(solution)/shard_map/ppermute | solution.py:278
  30.4 5.2 %collective-permute-start.7 = (f32[296,128]{1,0:T(8,128)S(1)}, f32[296,128]{1,0:T(8,128)S(1)}, u32[]{:S(2)}, u32[]{:S(2)}) collective-permute-start(f32[296,128]{1,0:T(8,128)S(1)} %get-tuple-element.34), channel_id=1, source_target_pairs={{0,2},{1,5},{2,0},{3,7},{4,6},{5,1},{6,4},{7,3},{8,10},{9,13},{10,... | collective-permute-start | bytes 454664 | tf_op jit(solution)/shard_map/ppermute | solution.py:278
  35.6 2.1 %collective-permute-start.10 = (f32[1184,128]{1,0:T(8,128)S(1)}, f32[1184,128]{1,0:T(8,128)S(1)}, u32[]{:S(2)}, u32[]{:S(2)}) collective-permute-start(f32[1184,128]{1,0:T(8,128)S(1)} %constant_dynamic-update-slice_fusion.5.mine_ref), channel_id=1, source_target_pairs={{0,1},{1,0},{2,3},{3,2},{4,5},{5,4},{6,7},{7,6},{8,9},{9,8},{10,11... | collective-permute-start | bytes 1818632 | tf_op jit(solution)/shard_map/ppermute | solution.py:278
